TPU v7x, 32 devices: a whole 2x2x4 slice. The times are simulated.
32 devices in a mesh: dp: 4 (over z), seq: 8 (over y, x, core).
Axes of the slice: x: 2, y: 2, z: 4, core: 2. Of those that a mesh axis runs over, the one named last changes fastest.
Arguments:
- tokens: bfloat16 [8, 1024, 1024], P('dp', 'seq'), may hold values from -6 to 6
- variate_ids: int32 [8, 1024], P('dp', 'seq'), may hold values from 0 to 3
- time_ids: int32 [8, 1024], P('dp', 'seq'), may hold values from 0 to 1023
- w_qkv: bfloat16 [2, 1024, 3072], P(None, ('dp', 'seq')), may hold values from -0.1875 to 0.1875
- w_out: bfloat16 [2, 1024, 1024], P(None, ('dp', 'seq')), may hold values from -3.5 to 3.5
- w_in: bfloat16 [2, 1024, 8192], P(None, ('dp', 'seq')), may hold values from -0.1875 to 0.1875
- w_down: bfloat16 [2, 4096, 1024], P(None, ('dp', 'seq')), may hold values from -0.09375 to 0.09375
- norm_gains: float32 [2, 2, 1024], replicated, may hold values from 0.5 to 1.5
- qk_gains: float32 [2, 2, 64], replicated, may hold values from 0.5 to 1.5
- head_bias: float32 [2, 2, 16], replicated, may hold values from -2 to 2
- cotangent: bfloat16 [8, 1024, 1024], P('dp', 'seq'), may hold values from -6 to 6
Outputs:
- layer_out: bfloat16 [8, 1024, 1024], P('dp', 'seq')
- input_grad: float32 [8, 1024, 1024], P('dp', 'seq')
- grad_qkv: float32 [2, 1024, 3072], P(None, ('dp', 'seq'))
- grad_out: float32 [2, 1024, 1024], P(None, ('dp', 'seq'))
- grad_in: float32 [2, 1024, 8192], P(None, ('dp', 'seq'))
- grad_down: float32 [2, 4096, 1024], P(None, ('dp', 'seq'))
- grad_norms: float32 [2, 2, 1024], replicated
- grad_qk: float32 [2, 2, 64], replicated
- grad_bias: float32 [2, 2, 16], replicated
- clipped_qkv: bfloat16 [2, 1024, 3072], P(None, ('dp', 'seq'))
- logit_max: float32 [2, 16], replicated
All inputs are finite; a program needn't handle non-finite values.
Results may differ from a plain program's by a relative error of at most 0.022.
Values may be sent and summed in bfloat16 or wider, within the bound.
No kernel may reach another device: no remote copies, remote signals or barrier semaphores. Data moves between devices by JAX's collectives and lax.ppermute only.
A program may use at most 320 MiB of HBM per device.

v0:
```python
import math

import jax
import jax.numpy as jnp
from jax import lax
from jax.sharding import PartitionSpec as P

EPSILON = 1e-05
CLIP_LIMIT = 2.0
FLOOR_VALUE = -1e30


def rms_scale(values, gain):
    return values * lax.rsqrt(jnp.mean(values * values, axis=-1, keepdims=True) + EPSILON) * gain


def rotate(values, places):
    half_width = values.shape[-1] // 2
    frequency = jnp.exp(
        jnp.arange(half_width, dtype=jnp.float32) * (-2.0 * math.log(10000.0) / values.shape[-1])
    )
    angles = places.astype(jnp.float32)[..., None] * frequency
    cosine = jnp.cos(angles)
    sine = jnp.sin(angles)
    front_part = values[..., :half_width]
    back_part = values[..., half_width:]
    return jnp.concatenate(
        [front_part * cosine - back_part * sine, back_part * cosine + front_part * sine], axis=-1
    )


def head_prep(unscaled_portion, gain_part, places):
    return rotate(rms_scale(unscaled_portion, gain_part), places)


def swiglu(joined):
    hidden_units = joined.shape[-1] // 2
    return jax.nn.silu(joined[:, :hidden_units]) * joined[:, hidden_units:]


def layer_scores(block_queries, key_rows, block_ids, key_ids, bias_pair, score_scale):
    scores = (
        jnp.einsum("pgl,pfl->pgf", block_queries, key_rows, preferred_element_type=jnp.float32)
        * score_scale
    )
    matches = block_ids[:, :, None] == key_ids[:, None, :]
    bias_terms = jnp.where(matches, bias_pair[0][:, None, None], bias_pair[1][:, None, None])
    return (scores + bias_terms, matches)


def attend_forward(query, key_rows, value_portion, key_ids, bias_pair):
    batch_rows, length, head_size = query.shape
    block_rows = min(512, length)
    score_scale = 1.0 / math.sqrt(head_size)

    def one_block(offset):
        block_queries = lax.dynamic_slice_in_dim(query, offset, block_rows, 1)
        block_ids = lax.dynamic_slice_in_dim(key_ids, offset, block_rows, 1)
        scores, matches = layer_scores(
            block_queries, key_rows, block_ids, key_ids, bias_pair, score_scale
        )
        row_top = jnp.max(scores, axis=-1)
        exponent = jnp.exp(scores - row_top[..., None])
        row_total = jnp.sum(exponent, axis=-1)
        attention_probs = (exponent / row_total[..., None]).astype(jnp.bfloat16)
        attended = jnp.einsum(
            "gpm,gmv->gpv", attention_probs, value_portion, preferred_element_type=jnp.float32
        )
        return (
            attended.astype(jnp.bfloat16),
            row_top + jnp.log(row_total),
            jnp.max(row_top, axis=-1),
        )

    offsets = jnp.arange(length // block_rows, dtype=jnp.int32) * block_rows
    attended, log_total, block_tops = lax.map(one_block, offsets)
    attended = jnp.transpose(attended, (1, 0, 2, 3)).reshape(batch_rows, length, head_size)
    log_total = jnp.transpose(log_total, (1, 0, 2)).reshape(batch_rows, length)
    return (attended, log_total, jnp.max(block_tops, axis=0))


def attend_backward(query, key_rows, value_portion, key_ids, bias_pair, log_total, grad_attended):
    batch_rows, length, head_size = query.shape
    block_rows = min(512, length)
    score_scale = 1.0 / math.sqrt(head_size)

    def one_block(running, offset):
        grad_keys, grad_values, grad_match, grad_other = running
        block_queries = lax.dynamic_slice_in_dim(query, offset, block_rows, 1)
        block_ids = lax.dynamic_slice_in_dim(key_ids, offset, block_rows, 1)
        block_total = lax.dynamic_slice_in_dim(log_total, offset, block_rows, 1)
        block_gradient = lax.dynamic_slice_in_dim(grad_attended, offset, block_rows, 1)
        scores, matches = layer_scores(
            block_queries, key_rows, block_ids, key_ids, bias_pair, score_scale
        )
        attention_probs = jnp.exp(scores - block_total[..., None])
        grad_prob = jnp.einsum(
            "pgl,pfl->pgf", block_gradient, value_portion, preferred_element_type=jnp.float32
        )
        grad_scores = attention_probs * (
            grad_prob - jnp.sum(attention_probs * grad_prob, axis=-1, keepdims=True)
        )
        reduced_precision_scores = grad_scores.astype(jnp.bfloat16)
        grad_match = grad_match + jnp.sum(
            jnp.where(matches, reduced_precision_scores, 0.0).astype(jnp.float32), axis=(1, 2)
        )
        grad_other = grad_other + jnp.sum(
            jnp.where(matches, 0.0, reduced_precision_scores).astype(jnp.float32), axis=(1, 2)
        )
        grad_query = (
            jnp.einsum(
                "gpm,gmv->gpv",
                reduced_precision_scores,
                key_rows,
                preferred_element_type=jnp.float32,
            )
            * score_scale
        )
        grad_keys = (
            grad_keys
            + jnp.einsum(
                "sla,sle->sae",
                reduced_precision_scores,
                block_queries,
                preferred_element_type=jnp.float32,
            )
            * score_scale
        )
        grad_values = grad_values + jnp.einsum(
            "sla,sle->sae",
            attention_probs.astype(jnp.bfloat16),
            block_gradient,
            preferred_element_type=jnp.float32,
        )
        return ((grad_keys, grad_values, grad_match, grad_other), grad_query)

    offsets = jnp.arange(length // block_rows, dtype=jnp.int32) * block_rows
    zero_field = jnp.zeros((batch_rows, length, head_size), jnp.float32)
    zero_heads = jnp.zeros((batch_rows,), jnp.float32)
    running, grad_query = lax.scan(
        one_block, (zero_field, zero_field, zero_heads, zero_heads), offsets
    )
    grad_query = jnp.transpose(grad_query, (1, 0, 2, 3)).reshape(batch_rows, length, head_size)
    return (grad_query, running[0], running[1], running[2], running[3])


def fetch_layer(w_qkv, w_out, w_in, w_down, layer_index):
    return (
        lax.all_gather(w_qkv[layer_index], ("dp", "seq"), axis=0, tiled=True),
        lax.all_gather(w_out[layer_index], ("dp", "seq"), axis=0, tiled=True),
        lax.all_gather(w_in[layer_index], ("dp", "seq"), axis=0, tiled=True),
        lax.all_gather(w_down[layer_index], ("dp", "seq"), axis=0, tiled=True),
    )


def shards(
    tokens,
    variate_ids,
    time_ids,
    w_qkv,
    w_out,
    w_in,
    w_down,
    norm_gains,
    qk_gains,
    head_bias,
    cotangent,
):
    sequences, tok_dev, model_width = tokens.shape
    layers = w_qkv.shape[0]
    head_count = head_bias.shape[2]
    head_size = qk_gains.shape[2]
    seq_devices = lax.axis_size("seq")
    local_heads = head_count // seq_devices
    head_start = lax.axis_index("seq") * local_heads
    token_rows = sequences * tok_dev
    all_ids, all_places = (
        lax.all_gather(variate_ids, "seq", axis=1, tiled=True),
        lax.all_gather(time_ids, "seq", axis=1, tiled=True),
    )
    length = all_ids.shape[1]
    batch_rows = sequences * local_heads
    key_ids = jnp.broadcast_to(all_ids[:, None, :], (sequences, local_heads, length)).reshape(
        batch_rows, length
    )
    head_places = all_places[:, None, :]
    head_shape = (sequences, local_heads, length, head_size)
    hidden_state = tokens.astype(jnp.float32).reshape(token_rows, model_width)
    saved = []
    best_scores = jnp.full((layers, head_count), FLOOR_VALUE, jnp.float32)
    for layer_index in range(layers):
        matrices = fetch_layer(w_qkv, w_out, w_in, w_down, layer_index)
        matrix_qkv, matrix_out, matrix_in, matrix_down = matrices
        layer_in = hidden_state
        normed = rms_scale(layer_in, norm_gains[layer_index, 0]).astype(jnp.bfloat16)
        mixed = jnp.dot(normed, matrix_qkv, preferred_element_type=jnp.float32).astype(jnp.bfloat16)
        arrived = lax.all_to_all(
            mixed.reshape(sequences, tok_dev, 3, model_width),
            "seq",
            split_axis=3,
            concat_axis=1,
            tiled=True,
        )
        raw_heads = arrived.reshape(sequences, length, 3, local_heads, head_size).transpose(
            2, 0, 3, 1, 4
        )
        query_full, query_pull = jax.vjp(
            lambda unscaled_portion, gain_part: head_prep(unscaled_portion, gain_part, head_places),
            raw_heads[0].astype(jnp.float32),
            qk_gains[layer_index, 0],
        )
        key_full, key_pull = jax.vjp(
            lambda unscaled_portion, gain_part: head_prep(unscaled_portion, gain_part, head_places),
            raw_heads[1].astype(jnp.float32),
            qk_gains[layer_index, 1],
        )
        query = query_full.astype(jnp.bfloat16).reshape(batch_rows, length, head_size)
        key_rows = key_full.astype(jnp.bfloat16).reshape(batch_rows, length, head_size)
        value_portion = raw_heads[2].reshape(batch_rows, length, head_size)
        local_pair = lax.dynamic_slice_in_dim(head_bias[layer_index], head_start, local_heads, 1)
        bias_pair = jnp.broadcast_to(local_pair[:, None, :], (2, sequences, local_heads)).reshape(
            2, batch_rows
        )
        attended, log_total, block_tops = attend_forward(
            query, key_rows, value_portion, key_ids, bias_pair
        )
        head_tops = jnp.max(block_tops.reshape(sequences, local_heads), axis=0)
        best_scores = lax.dynamic_update_slice(
            best_scores, head_tops[None, :], (jnp.int32(layer_index), head_start)
        )
        leaving = (
            attended.reshape(head_shape)
            .transpose(0, 2, 1, 3)
            .reshape(sequences, length, local_heads * head_size)
        )
        returned = lax.all_to_all(leaving, "seq", split_axis=1, concat_axis=2, tiled=True).reshape(
            token_rows, model_width
        )
        middle = layer_in + jnp.dot(returned, matrix_out, preferred_element_type=jnp.float32)
        second = rms_scale(middle, norm_gains[layer_index, 1]).astype(jnp.bfloat16)
        joined = jnp.dot(second, matrix_in, preferred_element_type=jnp.float32)
        gated = swiglu(joined).astype(jnp.bfloat16)
        hidden_state = middle + jnp.dot(gated, matrix_down, preferred_element_type=jnp.float32)
        saved.append(
            (
                matrices,
                layer_in,
                normed,
                query,
                key_rows,
                value_portion,
                query_pull,
                key_pull,
                bias_pair,
                log_total,
                returned,
                middle,
                second,
                joined,
                gated,
            )
        )
    best_scores = lax.pmax(best_scores, ("dp", "seq"))
    gradient = cotangent.astype(jnp.float32).reshape(token_rows, model_width)
    qkv_parts = [None] * layers
    out_parts = [None] * layers
    in_parts = [None] * layers
    down_parts = [None] * layers
    norm_parts = [None] * layers
    qk_parts = [None] * layers
    bias_parts = [None] * layers
    for layer_index in reversed(range(layers)):
        (
            matrices,
            layer_in,
            normed,
            query,
            key_rows,
            value_portion,
            query_pull,
            key_pull,
            bias_pair,
            log_total,
            returned,
            middle,
            second,
            joined,
            gated,
        ) = saved[layer_index]
        matrix_qkv, matrix_out, matrix_in, matrix_down = (
            lax.all_gather(w_qkv[layer_index], ("dp", "seq"), axis=0, tiled=True),
            lax.all_gather(w_out[layer_index], ("dp", "seq"), axis=0, tiled=True),
            lax.all_gather(w_in[layer_index], ("dp", "seq"), axis=0, tiled=True),
            lax.all_gather(w_down[layer_index], ("dp", "seq"), axis=0, tiled=True),
        )
        down_input = gradient.astype(jnp.bfloat16)
        grad_gated = jnp.dot(down_input, matrix_down.T, preferred_element_type=jnp.float32)
        grad_down = jnp.dot(gated.T, down_input, preferred_element_type=jnp.float32)
        unused_value, swiglu_pull = jax.vjp(swiglu, joined)
        grad_joined = swiglu_pull(grad_gated)[0].astype(jnp.bfloat16)
        grad_second = jnp.dot(grad_joined, matrix_in.T, preferred_element_type=jnp.float32)
        grad_in = jnp.dot(second.T, grad_joined, preferred_element_type=jnp.float32)
        unused_value, second_pull = jax.vjp(rms_scale, middle, norm_gains[layer_index, 1])
        grad_middle, gain_second = second_pull(grad_second)
        gradient = gradient + grad_middle
        branch_input = gradient.astype(jnp.bfloat16)
        grad_returned = jnp.dot(
            branch_input, matrix_out.T, preferred_element_type=jnp.float32
        ).astype(jnp.bfloat16)
        grad_out = jnp.dot(returned.T, branch_input, preferred_element_type=jnp.float32)
        grad_heads = lax.all_to_all(
            grad_returned.reshape(sequences, tok_dev, model_width),
            "seq",
            split_axis=2,
            concat_axis=1,
            tiled=True,
        )
        grad_heads = grad_heads.reshape(sequences, length, local_heads, head_size).transpose(
            0, 2, 1, 3
        )
        grad_heads = grad_heads.reshape(batch_rows, length, head_size)
        grad_query, grad_keys, grad_values, grad_match, grad_other = attend_backward(
            query, key_rows, value_portion, key_ids, bias_pair, log_total, grad_heads
        )
        grad_qraw, gain_query = query_pull(grad_query.reshape(head_shape))
        grad_kraw, gain_key = key_pull(grad_keys.reshape(head_shape))
        grad_raw = jnp.stack([grad_qraw, grad_kraw, grad_values.reshape(head_shape)]).astype(
            jnp.bfloat16
        )
        grad_raw = grad_raw.transpose(1, 3, 0, 2, 4).reshape(
            sequences, length, 3, local_heads * head_size
        )
        grad_mixed = lax.all_to_all(
            grad_raw, "seq", split_axis=1, concat_axis=3, tiled=True
        ).reshape(token_rows, 3 * model_width)
        grad_normed = jnp.dot(grad_mixed, matrix_qkv.T, preferred_element_type=jnp.float32)
        grad_qkv = jnp.dot(normed.T, grad_mixed, preferred_element_type=jnp.float32)
        unused_value, first_pull = jax.vjp(rms_scale, layer_in, norm_gains[layer_index, 0])
        grad_layer_in, gain_first = first_pull(grad_normed)
        gradient = gradient + grad_layer_in
        shares = (
            lax.psum_scatter(grad_qkv, ("dp", "seq"), scatter_dimension=0, tiled=True),
            lax.psum_scatter(grad_out, ("dp", "seq"), scatter_dimension=0, tiled=True),
            lax.psum_scatter(grad_in, ("dp", "seq"), scatter_dimension=0, tiled=True),
            lax.psum_scatter(grad_down, ("dp", "seq"), scatter_dimension=0, tiled=True),
        )
        qkv_parts[layer_index] = shares[0]
        out_parts[layer_index] = shares[1]
        in_parts[layer_index] = shares[2]
        down_parts[layer_index] = shares[3]
        norm_parts[layer_index] = jnp.stack([gain_first, gain_second])
        qk_parts[layer_index] = jnp.stack([gain_query, gain_key])
        bias_local = (
            jnp.stack([grad_match, grad_other]).reshape(2, sequences, local_heads).sum(axis=1)
        )
        bias_parts[layer_index] = lax.dynamic_update_slice(
            jnp.zeros((2, head_count), jnp.float32), bias_local, (jnp.int32(0), head_start)
        )
    norm_sum, qk_sum, bias_sum = lax.psum(
        (jnp.stack(norm_parts), jnp.stack(qk_parts), jnp.stack(bias_parts)), ("dp", "seq")
    )
    factor = jnp.sqrt(CLIP_LIMIT / jnp.maximum(best_scores, CLIP_LIMIT))
    spread = jnp.repeat(factor, head_size, axis=1)
    column_scale = jnp.concatenate(
        [spread, spread, jnp.ones((layers, model_width), jnp.float32)], axis=1
    )
    clipped = (w_qkv.astype(jnp.float32) * column_scale[:, None, :]).astype(jnp.bfloat16)
    layer_out = hidden_state.reshape(sequences, tok_dev, model_width).astype(jnp.bfloat16)
    input_grad = gradient.reshape(sequences, tok_dev, model_width)
    return (
        layer_out,
        input_grad,
        jnp.stack(qkv_parts),
        jnp.stack(out_parts),
        jnp.stack(in_parts),
        jnp.stack(down_parts),
        norm_sum,
        qk_sum,
        bias_sum,
        clipped,
        best_scores,
    )


def solution(mesh):
    in_specs = (
        P("dp", "seq", None),
        P("dp", "seq"),
        P("dp", "seq"),
        P(None, ("dp", "seq"), None),
        P(None, ("dp", "seq"), None),
        P(None, ("dp", "seq"), None),
        P(None, ("dp", "seq"), None),
        P(),
        P(),
        P(),
        P("dp", "seq", None),
    )
    out_specs = (
        P("dp", "seq", None),
        P("dp", "seq", None),
        P(None, ("dp", "seq"), None),
        P(None, ("dp", "seq"), None),
        P(None, ("dp", "seq"), None),
        P(None, ("dp", "seq"), None),
        P(),
        P(),
        P(),
        P(None, ("dp", "seq"), None),
        P(),
    )
    return jax.shard_map(shards, mesh=mesh, in_specs=in_specs, out_specs=out_specs, check_vma=False)
```

profile of v0, /device:TPU:0, one launch (start us, length us, event | category | flops | bytes accessed | tf_op | source)
XLA Modules:
  0.0 2429.9 jit_solution(11042010508315754562)
XLA Ops:
  16.9 66.8 %all-gather.17.cloned.1.call-done = bf16[1,1024,3072]{2,1,0:T(8,128)(2,1)} async-done(((bf16[1,32,3072]{2,1,0:T(8,128)(2,1)}), bf16[1,1024,3072]{2,1,0:T(8,128)(2,1)}) %all-gather.17.cloned.1.call-update) | async-done | bytes 6291472 | tf_op jit(solution)/shard_map/all_gather | solution.py:149
  101.8 24.9 %all_gather.39 = s32[2,1024]{1,0:T(2,128)S(1)} all-gather(s32[2,128]{1,0:T(2,128)S(1)} %copy-done.114), channel_id=1, replica_groups=mesh['dp'=4,'seq'=8] {'seq'}, dimensions={1}, use_global_device_ids=true | all-gather | bytes 9216 | tf_op jit(solution)/shard_map/all_gather | solution.py:179
  143.5 19.6 while.72
  171.3 9.0 all-to-all-done.1
  184.2 78.8 %all-gather.21.cloned.1.call-done = bf16[1,1024,8192]{2,1,0:T(8,128)(2,1)} async-done(((bf16[1,32,8192]{2,1,0:T(8,128)(2,1)}), bf16[1,1024,8192]{2,1,0:T(8,128)(2,1)}) %all-gather.21.cloned.1.call-update) | async-done | bytes 16777232 | tf_op jit(solution)/shard_map/all_gather | solution.py:151
  277.1 65.0 %all-gather.23.cloned.1.call-done = bf16[1,4096,1024]{2,1,0:T(8,128)(2,1)} async-done(((bf16[1,128,1024]{2,1,0:T(8,128)(2,1)}), bf16[1,4096,1024]{2,1,0:T(8,128)(2,1)}) %all-gather.23.cloned.1.call-update) | async-done | bytes 8388624 | tf_op jit(solution)/shard_map/all_gather | solution.py:152
  348.5 64.9 %all-gather.25.cloned.1.call-done = bf16[1,1024,3072]{2,1,0:T(8,128)(2,1)} async-done(((bf16[1,32,3072]{2,1,0:T(8,128)(2,1)}), bf16[1,1024,3072]{2,1,0:T(8,128)(2,1)}) %all-gather.25.cloned.1.call-update) | async-done | bytes 6291472 | tf_op jit(solution)/shard_map/all_gather | solution.py:149
  431.4 22.6 all-to-all-done.2
  461.4 19.6 while.73
  482.3 16.1 all_to_all.120
  501.5 93.7 %all-gather.29.cloned.1.call-done = bf16[1,1024,8192]{2,1,0:T(8,128)(2,1)} async-done(((bf16[1,32,8192]{2,1,0:T(8,128)(2,1)}), bf16[1,1024,8192]{2,1,0:T(8,128)(2,1)}) %all-gather.29.cloned.1.call-update) | async-done | bytes 16777232 | tf_op jit(solution)/shard_map/all_gather | solution.py:151
  595.3 12.7 fusion.68
  608.0 66.4 %all-gather.31.cloned.1.call-done = bf16[1,4096,1024]{2,1,0:T(8,128)(2,1)} async-done(((bf16[1,128,1024]{2,1,0:T(8,128)(2,1)}), bf16[1,4096,1024]{2,1,0:T(8,128)(2,1)}) %all-gather.31.cloned.1.call-update) | async-done | bytes 8388624 | tf_op jit(solution)/shard_map/all_gather | solution.py:152
  674.4 13.7 fusion.180
  688.1 12.1 multiply_reduce_fusion.2
  724.7 53.9 %while.74 = (s32[]{:T(128)}, f32[4,1024,64]{1,2,0:T(8,128)S(1)}, f32[4,1024,64]{1,2,0:T(8,128)S(1)}, f32[4]{0:T(128)S(1)}, f32[4]{0:T(128)S(1)}, /*index=5*/f32[...) while((s32[]{:T(128)}, f32[4,1024,64]{1,2,0:T(8,128)S(1)}, ...), condition=%wide.region_23.24_spmd.clone, body=%wide.region_19.23_spmd.clone.sunk | while | flops 1381365760 | bytes 179471456 | solution.py:140
  791.3 32.0 %all_to_all.121 = bf16[2,1024,3,128]{3,0,2,1:T(2,128)(2,1)S(1)} all-to-all(bf16[2,1024,3,128]{3,0,2,1:T(2,128)(2,1)S(1)} %copy.131), channel_id=1, replica_groups=mesh['dp'=4,'seq'=8] {'seq'}, dimensions={1} | all-to-all | bytes 3145728 | tf_op jit(solution)/shard_map/all_to_all | solution.py:333
  834.7 13.6 fusion.179
  848.3 12.1 multiply_reduce_fusion.4
  880.3 13.2 all-to-all-done.6
  897.0 53.7 %while.75 = (s32[]{:T(128)}, f32[4,1024,64]{1,2,0:T(8,128)S(1)}, f32[4,1024,64]{1,2,0:T(8,128)S(1)}, f32[4]{0:T(128)S(1)}, f32[4]{0:T(128)S(1)}, /*index=5*/f32[...) while((s32[]{:T(128)}, f32[4,1024,64]{1,2,0:T(8,128)S(1)}, ...), condition=%wide.region_32.33_spmd.clone, body=%wide.region_28.32_spmd.clone.sunk | while | flops 1381365760 | bytes 179471456 | solution.py:140
  968.5 25.8 %all-to-all-done.7 = bf16[2,1024,3,128]{3,0,2,1:T(2,128)(2,1)S(1)} async-done(((bf16[2,1024,3,128]{3,0,2,1:T(2,128)(2,1)}), bf16[2,1024,3,128]{3,0,2,1:T(2,128)(2,1)S(1)}, u32[]{:S(2)}, u32[]{:S(2)}) %all-to-all-start.7) | async-done | bytes 1572896 | tf_op jit(solution)/shard_map/all_to_all | solution.py:333
  1016.3 9.0 fusion.187
  1026.5 19.0 fusion.167
  1046.8 18.1 fusion.168
  1066.2 41.0 %pmax.7 = f32[2,16]{1,0:T(2,128)S(1)} all-reduce(f32[2,16]{1,0:T(2,128)S(1)} %dynamic_update_slice.51), channel_id=1, replica_groups=mesh['dp'=4,'seq'=8] {'dp','seq'}, use_global_device_ids=true, to_apply=%region_61.62 | all-reduce | flops 32 | bytes 256 | tf_op jit(solution)/shard_map/pmax | solution.py:263
  1122.6 42.3 %all-reduce.12 = (f32[2,2,1024]{2,1,0:T(2,128)}, f32[2,2,64]{2,1,0:T(2,128)}, f32[2,2,16]{2,1,0:T(2,128)}) all-reduce(f32[2,2,1024]{2,1,0:T(2,128)S(1)} %pad_maximum_fusion.10, f32[2,2,64]{2,1,0:T(2,128)S(1)} %pad_maximum_fusion.11, f32[2,2,16]{2,1,0:T(2,128)S(1)} %pad_maximum_fusion.12), channel_id=1, replica_groups=mesh['dp'=4,'seq'=8] {'dp','seq'}, use_global_device_ids=true, to_apply=%region_48.49 | all-reduce | flops 4416 | bytes 35328 | tf_op jit(solution)/shard_map/psum | solution.py:359
  1169.2 157.7 %reduce-scatter.9.cloned.1.call-done = f32[32,3072]{1,0:T(8,128)} async-done(((f32[1024,3072]{1,0:T(8,128)}), f32[32,3072]{1,0:T(8,128)}) %reduce-scatter.9.cloned.1.call-update) | async-done | bytes 393232 | tf_op jit(solution)/shard_map/reduce_scatter | solution.py:342
  1328.9 182.3 %reduce-scatter.23.cloned.1.call-done = f32[128,1024]{1,0:T(8,128)} async-done(((f32[4096,1024]{1,0:T(8,128)}), f32[128,1024]{1,0:T(8,128)}) %reduce-scatter.23.cloned.1.call-update) | async-done | bytes 524304 | tf_op jit(solution)/shard_map/reduce_scatter | solution.py:345
  1511.1 186.6 %reduce-scatter.21.cloned.1.call-done = f32[128,1024]{1,0:T(8,128)} async-done(((f32[4096,1024]{1,0:T(8,128)}), f32[128,1024]{1,0:T(8,128)}) %reduce-scatter.21.cloned.1.call-update) | async-done | bytes 524304 | tf_op jit(solution)/shard_map/reduce_scatter | solution.py:345
  1700.0 355.9 %reduce-scatter.19.cloned.1.call-done = f32[32,8192]{1,0:T(8,128)} async-done(((f32[1024,8192]{1,0:T(8,128)}), f32[32,8192]{1,0:T(8,128)}) %reduce-scatter.19.cloned.1.call-update) | async-done | bytes 1048592 | tf_op jit(solution)/shard_map/reduce_scatter | solution.py:344
  2055.9 364.1 %reduce-scatter.17.cloned.1.call-done = f32[32,8192]{1,0:T(8,128)} async-done(((f32[1024,8192]{1,0:T(8,128)}), f32[32,8192]{1,0:T(8,128)}) %reduce-scatter.17.cloned.1.call-update) | async-done | bytes 1048592 | tf_op jit(solution)/shard_map/reduce_scatter | solution.py:344
  (579 shorter events, 378.0 us)
Async XLA Ops:
  7.2 76.5 %all-gather.17.cloned.1.call-start = ((), (), s32[]{:S(2)}) async-start(), calls=%async_computation.24 | async-start | bytes 6488064 | tf_op jit(solution)/shard_map/all_gather | solution.py:149
  9.1 172.3 %all-gather.19.cloned.1.call-start = ((), (), s32[]{:S(2)}) async-start(), calls=%async_computation.25 | async-start | bytes 2162688 | tf_op jit(solution)/shard_map/all_gather | solution.py:150
  10.7 252.2 %all-gather.21.cloned.1.call-start = ((), (), s32[]{:S(2)}) async-start(), calls=%async_computation.26 | async-start | bytes 17301504 | tf_op jit(solution)/shard_map/all_gather | solution.py:151
  13.1 329.0 %all-gather.23.cloned.1.call-start = ((), (), s32[]{:S(2)}) async-start(), calls=%async_computation.27 | async-start | bytes 8650752 | tf_op jit(solution)/shard_map/all_gather | solution.py:152
  14.0 399.5 %all-gather.25.cloned.1.call-start = ((), (), s32[]{:S(2)}) async-start(), calls=%async_computation.28 | async-start | bytes 6488064 | tf_op jit(solution)/shard_map/all_gather | solution.py:149
  14.6 484.2 %all-gather.27.cloned.1.call-start = ((), (), s32[]{:S(2)}) async-start(), calls=%async_computation.29 | async-start | bytes 2162688 | tf_op jit(solution)/shard_map/all_gather | solution.py:150
  15.1 580.1 %all-gather.29.cloned.1.call-start = ((), (), s32[]{:S(2)}) async-start(), calls=%async_computation.30 | async-start | bytes 17301504 | tf_op jit(solution)/shard_map/all_gather | solution.py:151
  16.7 246.3 %copy-start.48 = (f32[1,1,1024]{2,1,0:T(1,128)}, f32[1,1,1024]{2,1,0:T(1,128)S(1)}, u32[]{:S(2)}) copy-start(f32[1,1,1024]{2,1,0:T(1,128)S(1)} %get-tuple-element.882) | copy-start | bytes 12292
  16.7 396.7 %copy-start.64 = (f32[1,1,1024]{2,1,0:T(1,128)}, f32[1,1,1024]{2,1,0:T(1,128)S(1)}, u32[]{:S(2)}) copy-start(f32[1,1,1024]{2,1,0:T(1,128)S(1)} %get-tuple-element.884) | copy-start | bytes 12292
  98.2 38.6 %all-to-all-start = ((bf16[2,128,3,1024]{1,0,2,3:T(2,128)(2,1)}), bf16[2,128,3,1024]{1,0,2,3:T(2,128)(2,1)S(1)}, u32[]{:S(2)}, u32[]{:S(2)}) async-start(bf16[2,128,3,1024]{1,0,2,3:T(2,128)(2,1)} %copy.113), calls=%async_computation | async-start | bytes 3145728 | tf_op jit(solution)/shard_map/all_to_all | solution.py:197
  135.8 324.5 %copy-start.98 = (f32[64]{0:T(128)}, f32[64]{0:T(128)S(1)}, u32[]{:S(2)}) copy-start(f32[64]{0:T(128)S(1)} %get-tuple-element.889) | copy-start | bytes 772
  135.8 324.5 %copy-start.100 = (f32[64]{0:T(128)}, f32[64]{0:T(128)S(1)}, u32[]{:S(2)}) copy-start(f32[64]{0:T(128)S(1)} %get-tuple-element.892) | copy-start | bytes 772
  136.8 324.1 %copy-start.32 = (f32[2,1024,32]{1,2,0:T(8,128)}, f32[2,1024,32]{1,2,0:T(8,128)S(1)}, u32[]{:S(2)}) copy-start(f32[2,1024,32]{1,2,0:T(8,128)S(1)} %get-tuple-element.885) | copy-start | bytes 786436
  136.8 324.1 %copy-start.35 = (f32[2,1024,32]{1,2,0:T(8,128)}, f32[2,1024,32]{1,2,0:T(8,128)S(1)}, u32[]{:S(2)}) copy-start(f32[2,1024,32]{1,2,0:T(8,128)S(1)} %get-tuple-element.886) | copy-start | bytes 786436
  167.1 13.3 all-to-all-start.1
  170.6 503.8 %all-gather.31.cloned.1.call-start = ((), (), s32[]{:S(2)}) async-start(), calls=%async_computation.31 | async-start | bytes 8650752 | tf_op jit(solution)/shard_map/all_gather | solution.py:152
  184.1 157.9 %copy-start.21 = (f32[256,1024]{1,0:T(8,128)}, f32[256,1024]{1,0:T(8,128)S(1)}, u32[]{:S(2)}) copy-start(f32[256,1024]{1,0:T(8,128)S(1)} %get-tuple-element.894) | copy-start | bytes 3145732
  427.7 26.4 %all-to-all-start.2 = ((bf16[2,128,3,1024]{1,0,2,3:T(2,128)(2,1)}), bf16[2,128,3,1024]{1,0,2,3:T(2,128)(2,1)S(1)}, u32[]{:S(2)}, u32[]{:S(2)}) async-start(bf16[2,128,3,1024]{1,0,2,3:T(2,128)(2,1)} %copy.121), calls=%async_computation.2 | async-start | bytes 3145728 | tf_op jit(solution)/shard_map/all_to_all | solution.py:197
  481.9 113.4 %copy-start.51 = (f32[1,1,1024]{2,1,0:T(1,128)S(1)}, f32[1,1,1024]{2,1,0:T(1,128)}, u32[]{:S(2)}) copy-start(f32[1,1,1024]{2,1,0:T(1,128)} %get-tuple-element.881) | copy-start | bytes 12292
  501.5 198.7 %copy-start.15 = (f32[256,1024]{1,0:T(8,128)}, f32[256,1024]{1,0:T(8,128)S(1)}, u32[]{:S(2)}) copy-start(f32[256,1024]{1,0:T(8,128)S(1)} %get-tuple-element.898) | copy-start | bytes 3145732
  501.5 198.7 %copy-start.79 = (f32[256]{0:T(256)}, f32[256]{0:T(256)S(1)}, u32[]{:S(2)}) copy-start(f32[256]{0:T(256)S(1)} %fusion.198) | copy-start | bytes 3076
  706.2 13.9 all-to-all-start.4
  710.4 457.1 %reduce-scatter.15.cloned.1.call-start = ((), (), s32[]{:S(2)}) async-start(), calls=%async_computation.19 | async-start | bytes 4325376 | tf_op jit(solution)/shard_map/reduce_scatter | solution.py:343
  714.5 452.9 %reduce-scatter.13.cloned.1.call-start = ((), (), s32[]{:S(2)}) async-start(), calls=%async_computation.18 | async-start | bytes 4325376 | tf_op jit(solution)/shard_map/reduce_scatter | solution.py:343
  865.1 304.0 %reduce-scatter.11.cloned.1.call-start = ((), (), s32[]{:S(2)}) async-start(), calls=%async_computation.17 | async-start | bytes 12976128 | tf_op jit(solution)/shard_map/reduce_scatter | solution.py:342
  876.6 16.9 all-to-all-start.6
  963.6 30.7 %all-to-all-start.7 = ((bf16[2,1024,3,128]{3,0,2,1:T(2,128)(2,1)}), bf16[2,1024,3,128]{3,0,2,1:T(2,128)(2,1)S(1)}, u32[]{:S(2)}, u32[]{:S(2)}) async-start(bf16[2,1024,3,128]{3,0,2,1:T(2,128)(2,1)} %copy.137), calls=%async_computation.7 | async-start | bytes 3145728 | tf_op jit(solution)/shard_map/all_to_all | solution.py:333
  967.4 359.4 %reduce-scatter.9.cloned.1.call-start = ((), (), s32[]{:S(2)}) async-start(), calls=%async_computation.16 | async-start | bytes 12976128 | tf_op jit(solution)/shard_map/reduce_scatter | solution.py:342
  1004.2 507.0 %reduce-scatter.23.cloned.1.call-start = ((), (), s32[]{:S(2)}) async-start(), calls=%async_computation.23 | async-start | bytes 17301504 | tf_op jit(solution)/shard_map/reduce_scatter | solution.py:345
  1014.1 683.6 %reduce-scatter.21.cloned.1.call-start = ((), (), s32[]{:S(2)}) async-start(), calls=%async_computation.22 | async-start | bytes 17301504 | tf_op jit(solution)/shard_map/reduce_scatter | solution.py:345
  1025.3 1030.6 %reduce-scatter.19.cloned.1.call-start = ((), (), s32[]{:S(2)}) async-start(), calls=%async_computation.21 | async-start | bytes 34603008 | tf_op jit(solution)/shard_map/reduce_scatter | solution.py:344
  1045.6 1374.4 %reduce-scatter.17.cloned.1.call-start = ((), (), s32[]{:S(2)}) async-start(), calls=%async_computation.20 | async-start | bytes 34603008 | tf_op jit(solution)/shard_map/reduce_scatter | solution.py:344
  (124 other events, 1572.5 us)
Sparse Core Ops, SparseCore 0:
  11.5 72.1 all-gather.16
  86.6 59.1 all-gather.18
  149.2 113.7 all-gather.20
  266.3 75.7 all-gather.22
  345.3 68.0 all-gather.24
  416.2 59.0 all-gather.26
  478.7 116.5 all-gather.28
  598.7 75.6 all-gather.30
  714.6 141.1 reduce-scatter.14
  865.2 140.2 reduce-scatter.12
  1011.6 154.1 reduce-scatter.10
  1172.6 154.1 reduce-scatter.8
  1329.1 181.9 reduce-scatter.22
  1513.3 184.3 reduce-scatter.20
  1699.8 355.9 reduce-scatter.18
  2058.0 361.8 reduce-scatter.16
where the time goes:
time: 2450 us; the launch traced here: 2430 us
  waiting for transfers between devices  1760 us (72%)
  matrix products  293 us (12%)
  blocking collectives  165 us (7%)
  local copies, waits for them, and re-layouts  98.2 us (4%)
  other arithmetic  56.9 us (2%)
    reduce_scatter x2, waiting for transfers between devices, shards(): lax.psum_scatter(grad_in, ('dp', 'seq'), scatter_dimension=0, tiled=True)  720 us
    reduce_scatter x2, waiting for transfers between devices, shards(): lax.psum_scatter(grad_down, ('dp', 'seq'), scatter_dimension=0, tiled=True)  369 us
    all_gather x2, waiting for transfers between devices, fetch_layer(): lax.all_gather(w_in[layer_index], ('dp', 'seq'), axis=0, tiled=True)  173 us
    reduce_scatter x2, waiting for transfers between devices, shards(): lax.psum_scatter(grad_qkv, ('dp', 'seq'), scatter_dimension=0, tiled=True)  158 us
    all_gather x2, waiting for transfers between devices, fetch_layer(): lax.all_gather(w_qkv[layer_index], ('dp', 'seq'), axis=0, tiled=True)  132 us
    all_gather x2, waiting for transfers between devices, fetch_layer(): lax.all_gather(w_down[layer_index], ('dp', 'seq'), axis=0, tiled=True)  131 us
  transfers between devices with their start and end apart: 22, of which 16 were waited for; matrix products, arithmetic and copies ran while one was open for 16% of the time, Pallas kernels for 0%

commit v1 on v0

v1 whole, which is shorter than its diff:
```python
import math

import jax
import jax.numpy as jnp
from jax import lax
from jax.sharding import PartitionSpec as P

EPSILON = 1e-05
CLIP_LIMIT = 2.0
FLOOR_VALUE = -1e30
BF = jnp.bfloat16
F32 = jnp.float32


def rms_scale(values, gain):
    return values * lax.rsqrt(jnp.mean(values * values, axis=-1, keepdims=True) + EPSILON) * gain


def swiglu(joined):
    hidden_units = joined.shape[-1] // 2
    return jax.nn.silu(joined[:, :hidden_units]) * joined[:, hidden_units:]


def dot(a, b):
    return jnp.dot(a, b, preferred_element_type=F32)


def dot_nt(a, b):
    return lax.dot_general(a, b, (((1,), (1,)), ((), ())), preferred_element_type=F32)


def dot_tn(a, b):
    return lax.dot_general(a, b, (((0,), (0,)), ((), ())), preferred_element_type=F32)


def pick(array, index, axis=0):
    return lax.dynamic_index_in_dim(array, index, axis, keepdims=False)


class Net:
    def __init__(self, dp_n, seq_n, sequences):
        self.dp_n, self.seq_n = dp_n, seq_n
        self.hi_n = sequences
        self.lo_n = seq_n // sequences
        seq = lax.axis_index("seq")
        self.lo = seq % self.lo_n
        self.hi = seq // self.lo_n
        self.dp = lax.axis_index("dp")
        self.lo_bits = [1 << b for b in range(self.lo_n.bit_length() - 1)]
        self.hi_bits = [1 << b for b in range(self.hi_n.bit_length() - 1)]

    def swap_lo(self, x, bit):
        return lax.ppermute(x, "seq", [(i, i ^ bit) for i in range(self.seq_n)])

    def swap_hi(self, x, bit):
        return self.swap_lo(x, bit * self.lo_n)

    def swap_dp(self, x, bit):
        return lax.ppermute(x, "dp", [(i, i ^ bit) for i in range(self.dp_n)])

    def next_dp(self, x):
        return lax.ppermute(x, "dp", [(i, (i + 1) % self.dp_n) for i in range(self.dp_n)])

    def gather_lo(self, block):
        blocks = {0: block}
        for bit in reversed(self.lo_bits):
            for r in list(blocks):
                blocks[r | bit] = self.swap_lo(blocks[r], bit)
        return [blocks[r] for r in range(self.lo_n)]

    def scatter_lo(self, blocks):
        blocks = dict(enumerate(blocks))
        for bit in self.lo_bits:
            blocks = {
                r: blocks[r].astype(F32) + self.swap_lo(blocks[r | bit].astype(BF), bit).astype(F32)
                for r in sorted(blocks, reverse=True)
                if not r & bit
            }
        return blocks[0]

    def trade(self, blocks, bits, swap):
        blocks = list(blocks)
        for bit in reversed(bits):
            for r in range(len(blocks)):
                if r & bit:
                    blocks[r] = swap(blocks[r], bit)
        return blocks

    def trade_lo(self, blocks):
        return self.trade(blocks, self.lo_bits, self.swap_lo)

    def trade_hi(self, blocks):
        return self.trade(blocks, self.hi_bits, self.swap_hi)

    def all_small(self, x, combine):
        for bit in self.lo_bits:
            x = combine(x, self.swap_lo(x, bit))
        for bit in self.hi_bits:
            x = combine(x, self.swap_hi(x, bit))
        bit = 1
        while bit < self.dp_n:
            x = combine(x, self.swap_dp(x, bit))
            bit *= 2
        return x

    def gather_rows(self, own):
        full = jnp.zeros((self.dp_n, self.hi_n) + own.shape, own.dtype)
        chunk = own
        for step in range(self.dp_n):
            if step:
                chunk = self.next_dp(chunk)
            source = (self.dp - step) % self.dp_n
            blocks = {0: chunk}
            for bit in self.hi_bits:
                for q in list(blocks):
                    blocks[q | bit] = self.swap_hi(blocks[q], bit)
            for q, block in blocks.items():
                start = (source, self.hi ^ q) + (0,) * own.ndim
                full = lax.dynamic_update_slice(full, block[None, None], start)
        return full

    def scatter_rows(self, full):
        blocks = {q: pick(full, self.hi ^ q, 1) for q in range(self.hi_n)}
        for bit in self.hi_bits:
            blocks = {
                q: blocks[q] + self.swap_hi(blocks[q | bit].astype(BF), bit).astype(F32)
                for q in blocks
                if not q & bit
            }
        mine = blocks[0]
        running = pick(mine, (self.dp - 1) % self.dp_n)
        for step in range(1, self.dp_n):
            running = self.next_dp(running.astype(BF)).astype(F32)
            running = running + pick(mine, (self.dp - 1 - step) % self.dp_n)
        return running


def fetch_columns(net, shard, width):
    rows, parts = shard.shape[:2]
    blocks = [pick(shard, net.lo ^ r, 2).reshape(rows, parts * width) for r in range(net.lo_n)]
    blocks = net.trade_lo(blocks)
    own = jnp.zeros((net.lo_n,) + blocks[0].shape, BF)
    for r, block in enumerate(blocks):
        own = lax.dynamic_update_slice(own, block[None], (net.lo ^ r, 0, 0))
    own = own.reshape(net.lo_n * rows, parts * width)
    full = net.gather_rows(own)
    return full.reshape(-1, parts * width)


def scatter_columns(net, grad, rows, parts, width):
    grad = grad.reshape(net.dp_n, net.hi_n, net.lo_n * rows, parts * width)
    own = net.scatter_rows(grad).reshape(net.lo_n, rows, parts * width).astype(BF)
    blocks = net.trade_lo([pick(own, net.lo ^ r) for r in range(net.lo_n)])
    shard = jnp.zeros((rows, parts, net.lo_n, width), F32)
    for r, block in enumerate(blocks):
        block = block.astype(F32).reshape(rows, parts, 1, width)
        shard = lax.dynamic_update_slice(shard, block, (0, 0, net.lo ^ r, 0))
    return shard.reshape(rows, parts * net.lo_n * width)


def fetch_hidden(net, shard):
    return net.gather_rows(shard).reshape(-1, shard.shape[-1])


def scatter_hidden(net, grad, rows):
    return net.scatter_rows(grad.reshape(net.dp_n, net.hi_n, rows, -1))


def fetch_whole(net, shard):
    own = net.gather_rows(shard)
    parts = net.gather_lo(own)
    full = jnp.zeros((net.dp_n, net.hi_n, net.lo_n) + shard.shape, BF)
    for r, part in enumerate(parts):
        full = lax.dynamic_update_slice(full, part[:, :, None], (0, 0, net.lo ^ r, 0, 0))
    return full.reshape(-1, shard.shape[-1])


def scatter_whole(net, grad, rows):
    grad = grad.reshape(net.dp_n, net.hi_n, net.lo_n, rows, -1)
    own = net.scatter_lo([pick(grad, net.lo ^ r, 2) for r in range(net.lo_n)])
    return net.scatter_rows(own)


def rotate(values, cosine, sine):
    half_width = values.shape[-1] // 2
    front_part = values[..., :half_width]
    back_part = values[..., half_width:]
    return jnp.concatenate(
        [front_part * cosine - back_part * sine, back_part * cosine + front_part * sine], axis=-1
    )


def layer_scores(block_queries, key_rows, block_ids, key_ids, bias_pair, score_scale):
    scores = (
        jnp.einsum("pgl,pfl->pgf", block_queries, key_rows, preferred_element_type=F32)
        * score_scale
    )
    matches = (block_ids[:, None] == key_ids[None, :])[None]
    bias_terms = jnp.where(matches, bias_pair[0][:, None, None], bias_pair[1][:, None, None])
    return (scores + bias_terms, matches)


def attend_forward(query, key_rows, value_portion, key_ids, bias_pair):
    heads, length, head_size = query.shape
    block_rows = min(512, length)
    score_scale = 1.0 / math.sqrt(head_size)

    def one_block(offset):
        block_queries = lax.dynamic_slice_in_dim(query, offset, block_rows, 1)
        block_ids = lax.dynamic_slice_in_dim(key_ids, offset, block_rows, 0)
        scores, matches = layer_scores(
            block_queries, key_rows, block_ids, key_ids, bias_pair, score_scale
        )
        row_top = jnp.max(scores, axis=-1)
        exponent = jnp.exp(scores - row_top[..., None])
        row_total = jnp.sum(exponent, axis=-1)
        attention_probs = (exponent / row_total[..., None]).astype(BF)
        attended = jnp.einsum(
            "gpm,gmv->gpv", attention_probs, value_portion, preferred_element_type=F32
        )
        return (
            attended.astype(BF),
            row_top + jnp.log(row_total),
            jnp.max(row_top, axis=-1),
        )

    offsets = jnp.arange(length // block_rows, dtype=jnp.int32) * block_rows
    attended, log_total, block_tops = lax.map(one_block, offsets)
    attended = jnp.transpose(attended, (1, 0, 2, 3)).reshape(heads, length, head_size)
    log_total = jnp.transpose(log_total, (1, 0, 2)).reshape(heads, length)
    return (attended, log_total, jnp.max(block_tops, axis=0))


def attend_backward(query, key_rows, value_portion, key_ids, bias_pair, log_total, grad_attended):
    heads, length, head_size = query.shape
    block_rows = min(512, length)
    score_scale = 1.0 / math.sqrt(head_size)

    def one_block(running, offset):
        grad_keys, grad_values, grad_match, grad_other = running
        block_queries = lax.dynamic_slice_in_dim(query, offset, block_rows, 1)
        block_ids = lax.dynamic_slice_in_dim(key_ids, offset, block_rows, 0)
        block_total = lax.dynamic_slice_in_dim(log_total, offset, block_rows, 1)
        block_gradient = lax.dynamic_slice_in_dim(grad_attended, offset, block_rows, 1)
        scores, matches = layer_scores(
            block_queries, key_rows, block_ids, key_ids, bias_pair, score_scale
        )
        attention_probs = jnp.exp(scores - block_total[..., None])
        grad_prob = jnp.einsum(
            "pgl,pfl->pgf", block_gradient, value_portion, preferred_element_type=F32
        )
        grad_scores = attention_probs * (
            grad_prob - jnp.sum(attention_probs * grad_prob, axis=-1, keepdims=True)
        )
        low_scores = grad_scores.astype(BF)
        grad_match = grad_match + jnp.sum(
            jnp.where(matches, low_scores, 0.0).astype(F32), axis=(1, 2)
        )
        grad_other = grad_other + jnp.sum(
            jnp.where(matches, 0.0, low_scores).astype(F32), axis=(1, 2)
        )
        grad_query = (
            jnp.einsum("gpm,gmv->gpv", low_scores, key_rows, preferred_element_type=F32)
            * score_scale
        )
        grad_keys = (
            grad_keys
            + jnp.einsum("sla,sle->sae", low_scores, block_queries, preferred_element_type=F32)
            * score_scale
        )
        grad_values = grad_values + jnp.einsum(
            "sla,sle->sae",
            attention_probs.astype(BF),
            block_gradient,
            preferred_element_type=F32,
        )
        return ((grad_keys, grad_values, grad_match, grad_other), grad_query)

    offsets = jnp.arange(length // block_rows, dtype=jnp.int32) * block_rows
    zero_field = jnp.zeros((heads, length, head_size), F32)
    zero_heads = jnp.zeros((heads,), F32)
    running, grad_query = lax.scan(
        one_block, (zero_field, zero_field, zero_heads, zero_heads), offsets
    )
    grad_query = jnp.transpose(grad_query, (1, 0, 2, 3)).reshape(heads, length, head_size)
    return (grad_query, running[0], running[1], running[2], running[3])


def halves(blocks):
    cut = max(1, len(blocks) // 2)
    parts = [blocks[:cut], blocks[cut:]]
    return [jnp.concatenate(part, axis=0) for part in parts if part]


def split_rows(parts, count):
    each = count // len(parts)
    blocks = []
    for part in parts:
        blocks += jnp.split(part, each, axis=0)
    return blocks


def shards(
    tokens,
    variate_ids,
    time_ids,
    w_qkv,
    w_out,
    w_in,
    w_down,
    norm_gains,
    qk_gains,
    head_bias,
    cotangent,
):
    sequences, tok_dev, width = tokens.shape
    layers = w_qkv.shape[0]
    heads = head_bias.shape[2]
    head_size = qk_gains.shape[2]
    hidden = w_in.shape[2] // 2
    net = Net(lax.axis_size("dp"), lax.axis_size("seq"), sequences)
    lo_n = net.lo_n
    rows = sequences * tok_dev
    local_heads = heads // lo_n
    local_width = local_heads * head_size
    length = rows * lo_n
    head_start = net.lo * local_heads
    unit = w_down.shape[1]

    def to_groups(x):
        return jnp.concatenate(
            net.trade_hi([pick(x, net.hi ^ q) for q in range(sequences)]), axis=0
        )

    def to_devices(x):
        blocks = net.trade_hi(jnp.split(x, sequences, axis=0))
        out = jnp.zeros((sequences, tok_dev) + x.shape[1:], x.dtype)
        for q, block in enumerate(blocks):
            out = lax.dynamic_update_slice(out, block[None], (net.hi ^ q,) + (0,) * x.ndim)
        return out

    state = to_groups(tokens).astype(F32)
    pair = to_groups(jnp.stack([variate_ids, time_ids], axis=-1))
    pair = jnp.concatenate(net.gather_lo(pair), axis=0)
    key_ids, places = pair[:, 0], pair[:, 1]
    frequency = jnp.exp(
        jnp.arange(head_size // 2, dtype=F32) * (-2.0 * math.log(10000.0) / head_size)
    )
    angles = places.astype(F32)[:, None] * frequency
    cosine, sine = jnp.cos(angles), jnp.sin(angles)

    def head_prep(raw, gain):
        return rotate(rms_scale(raw, gain), cosine, sine)

    weights = []
    for layer in range(layers):
        rows_w = w_qkv.shape[1]
        weights.append(
            (
                fetch_columns(
                    net, w_qkv[layer].reshape(rows_w, 3, lo_n, local_width), local_width
                ),
                fetch_whole(net, w_out[layer]),
                fetch_columns(
                    net,
                    w_in[layer]
                    .reshape(rows_w, 2 * net.dp_n * net.hi_n, lo_n, unit),
                    unit,
                ),
                fetch_hidden(net, w_down[layer]),
            )
        )

    saved = []
    best_scores = jnp.full((layers, heads), FLOOR_VALUE, F32)
    for layer in range(layers):
        m_qkv, m_out, m_in, m_down = weights[layer]
        layer_in = state
        normed = rms_scale(layer_in, norm_gains[layer, 0]).astype(BF)
        normed_halves = halves(net.gather_lo(normed))
        mixed = jnp.concatenate([dot(part, m_qkv).astype(BF) for part in normed_halves], axis=0)
        raw = mixed.reshape(length, 3, local_heads, head_size).transpose(1, 2, 0, 3)
        query, query_pull = jax.vjp(head_prep, raw[0].astype(F32), qk_gains[layer, 0])
        keys, key_pull = jax.vjp(head_prep, raw[1].astype(F32), qk_gains[layer, 1])
        query, keys, values = query.astype(BF), keys.astype(BF), raw[2]
        bias_pair = lax.dynamic_slice_in_dim(head_bias[layer], head_start, local_heads, 1)
        attended, log_total, head_tops = attend_forward(query, keys, values, key_ids, bias_pair)
        best_scores = lax.dynamic_update_slice(
            best_scores, head_tops[None, :], (jnp.int32(layer), head_start)
        )
        attended = attended.transpose(1, 0, 2).reshape(length, local_width)
        arrived = net.trade_lo(jnp.split(attended, lo_n, axis=0))
        returned = jnp.zeros((rows, width), BF)
        for r, block in enumerate(arrived):
            returned = lax.dynamic_update_slice(returned, block, (0, (net.lo ^ r) * local_width))
        middle = layer_in + dot(returned, m_out)
        second = rms_scale(middle, norm_gains[layer, 1]).astype(BF)
        second_halves = halves(net.gather_lo(second))
        joined = [dot(part, m_in) for part in second_halves]
        gated = [swiglu(part).astype(BF) for part in joined]
        partial = [dot(part, m_down).astype(BF) for part in gated]
        state = middle + net.scatter_lo(split_rows(partial, lo_n))
        saved.append(
            (
                layer_in,
                normed_halves,
                query,
                keys,
                values,
                query_pull,
                key_pull,
                bias_pair,
                log_total,
                returned,
                middle,
                second_halves,
                joined,
                gated,
            )
        )
    best_scores = net.all_small(best_scores, jnp.maximum)
    layer_out = to_devices(state.astype(BF))

    gradient = to_groups(cotangent).astype(F32)
    qkv_parts = [None] * layers
    out_parts = [None] * layers
    in_parts = [None] * layers
    down_parts = [None] * layers
    norm_parts = [None] * layers
    qk_parts = [None] * layers
    bias_parts = [None] * layers
    for layer in reversed(range(layers)):
        m_qkv, m_out, m_in, m_down = weights[layer]
        (
            layer_in,
            normed_halves,
            query,
            keys,
            values,
            query_pull,
            key_pull,
            bias_pair,
            log_total,
            returned,
            middle,
            second_halves,
            joined,
            gated,
        ) = saved[layer]
        down_halves = halves(net.gather_lo(gradient.astype(BF)))
        grad_joined = []
        partial = []
        for part, joined_part in zip(down_halves, joined):
            grad_gated = dot_nt(part, m_down)
            unused, pull = jax.vjp(swiglu, joined_part)
            grad_joined.append(pull(grad_gated)[0].astype(BF))
            partial.append(dot_nt(grad_joined[-1], m_in).astype(BF))
        grad_second = net.scatter_lo(split_rows(partial, lo_n))
        grad_down = dot_tn(jnp.concatenate(gated, axis=0), jnp.concatenate(down_halves, axis=0))
        grad_in = dot_tn(
            jnp.concatenate(second_halves, axis=0), jnp.concatenate(grad_joined, axis=0)
        )
        down_parts[layer] = scatter_hidden(net, grad_down, unit)
        in_parts[layer] = scatter_columns(
            net, grad_in, w_in.shape[1], 2 * net.dp_n * net.hi_n, unit
        )
        unused, second_pull = jax.vjp(rms_scale, middle, norm_gains[layer, 1])
        grad_middle, gain_second = second_pull(grad_second)
        gradient = gradient + grad_middle
        branch = gradient.astype(BF)
        grad_returned = dot_nt(branch, m_out).astype(BF)
        grad_out = dot_tn(returned, branch)
        out_parts[layer] = scatter_whole(net, grad_out, w_out.shape[1])
        leaving = [
            lax.dynamic_slice_in_dim(grad_returned, (net.lo ^ r) * local_width, local_width, 1)
            for r in range(lo_n)
        ]
        grad_heads = jnp.concatenate(net.trade_lo(leaving), axis=0)
        grad_heads = grad_heads.reshape(length, local_heads, head_size).transpose(1, 0, 2)
        grad_query, grad_keys, grad_values, grad_match, grad_other = attend_backward(
            query, keys, values, key_ids, bias_pair, log_total, grad_heads
        )
        grad_qraw, gain_query = query_pull(grad_query)
        grad_kraw, gain_key = key_pull(grad_keys)
        grad_mixed = jnp.stack([grad_qraw, grad_kraw, grad_values]).astype(BF)
        grad_mixed = grad_mixed.transpose(2, 0, 1, 3).reshape(length, 3 * local_width)
        partial = [dot_nt(part, m_qkv).astype(BF) for part in jnp.split(grad_mixed, 2, axis=0)]
        grad_normed = net.scatter_lo(split_rows(partial, lo_n))
        grad_qkv = dot_tn(jnp.concatenate(normed_halves, axis=0), grad_mixed)
        qkv_parts[layer] = scatter_columns(net, grad_qkv, w_qkv.shape[1], 3, local_width)
        unused, first_pull = jax.vjp(rms_scale, layer_in, norm_gains[layer, 0])
        grad_layer_in, gain_first = first_pull(grad_normed)
        gradient = gradient + grad_layer_in
        norm_parts[layer] = jnp.stack([gain_first, gain_second])
        qk_parts[layer] = jnp.stack([gain_query, gain_key])
        bias_parts[layer] = lax.dynamic_update_slice(
            jnp.zeros((2, heads), F32),
            jnp.stack([grad_match, grad_other]),
            (jnp.int32(0), head_start),
        )
    input_grad = to_devices(gradient)
    small = jnp.concatenate(
        [jnp.stack(part).reshape(-1) for part in (norm_parts, qk_parts, bias_parts)]
    )
    small = net.all_small(small, jnp.add)
    cut_norm, cut_qk = norm_gains.size, norm_gains.size + qk_gains.size
    norm_sum = small[:cut_norm].reshape(norm_gains.shape)
    qk_sum = small[cut_norm:cut_qk].reshape(qk_gains.shape)
    bias_sum = small[cut_qk:].reshape(head_bias.shape)

    factor = jnp.sqrt(CLIP_LIMIT / jnp.maximum(best_scores, CLIP_LIMIT))
    spread = jnp.repeat(factor, head_size, axis=1)
    column_scale = jnp.concatenate([spread, spread, jnp.ones((layers, width), F32)], axis=1)
    clipped = (w_qkv.astype(F32) * column_scale[:, None, :]).astype(BF)
    return (
        layer_out,
        input_grad,
        jnp.stack(qkv_parts),
        jnp.stack(out_parts),
        jnp.stack(in_parts),
        jnp.stack(down_parts),
        norm_sum,
        qk_sum,
        bias_sum,
        clipped,
        best_scores,
    )


def solution(mesh):
    in_specs = (
        P("dp", "seq", None),
        P("dp", "seq"),
        P("dp", "seq"),
        P(None, ("dp", "seq"), None),
        P(None, ("dp", "seq"), None),
        P(None, ("dp", "seq"), None),
        P(None, ("dp", "seq"), None),
        P(),
        P(),
        P(),
        P("dp", "seq", None),
    )
    out_specs = (
        P("dp", "seq", None),
        P("dp", "seq", None),
        P(None, ("dp", "seq"), None),
        P(None, ("dp", "seq"), None),
        P(None, ("dp", "seq"), None),
        P(None, ("dp", "seq"), None),
        P(),
        P(),
        P(),
        P(None, ("dp", "seq"), None),
        P(),
    )
    return jax.shard_map(shards, mesh=mesh, in_specs=in_specs, out_specs=out_specs, check_vma=False)
```

time: 2450 us -> 1100 us (0.45)
  waiting for transfers between devices: 1760 us -> 392 us
  blocking collectives: 165 us -> 0 us
  local copies, waits for them, and re-layouts: 98.2 us -> 252 us
  starting transfers between devices: 23.5 us -> 141 us
  matrix products: 293 us -> 179 us
  other arithmetic: 56.9 us -> 101 us
    reduce_scatter x8 -> x0, waiting for transfers between devices: 1250 us -> none  [the longest x2 720 us: shards(): lax.psum_scatter(grad_in, ('dp', 'seq'), scatter_dimension=0, tiled=True)]
    all_gather x8 -> x0, waiting for transfers between devices: 436 us -> none  [the longest x2 173 us: fetch_layer(): lax.all_gather(w_in[layer_index], ('dp', 'seq'), axis=0, tiled=True)]
    ppermute x0 -> x202, waiting for transfers between devices: none -> 392 us  [the longest x150 241 us: swap_lo(): return lax.ppermute(x, 'seq', [(i, i ^ bit) for i in range(self.seq_n)])]
    ppermute x0 -> x202, starting transfers between devices: none -> 141 us  [the longest x150 106 us: swap_lo(): return lax.ppermute(x, 'seq', [(i, i ^ bit) for i in range(self.seq_n)])]
    dynamic_update_slice x2 -> x118, local copies, waits for them, and re-layouts: 0.29 us -> 114 us  [the longest x16 64.6 us: scatter_columns(): shard = lax.dynamic_update_slice(shard, block, (0, 0, net.lo ^ r, 0))]
    dot_general x36 -> x48, matrix products: 229 us -> 137 us  [the longest x14 42 us: dot_nt(): lax.dot_general(a, b, (((1,), (1,)), ((), ())), preferred_element_type=F32)]
    all_to_all x6 -> x0, waiting for transfers between devices: 76.2 us -> none  [the longest x1 25.8 us: shards(): lax.all_to_all(grad_raw, 'seq', split_axis=1, concat_axis=3, tiled=True)]
    all_to_all x2 -> x0, blocking collectives: 48.1 us -> none  [the longest x1 32 us: shards(): lax.all_to_all(grad_raw, 'seq', split_axis=1, concat_axis=3, tiled=True)]
  transfers between devices with their start and end apart: 22 -> 202, of which waited for: 16 -> 80; matrix products, arithmetic and copies ran while one was open for 16% -> 44% of each run, Pallas kernels for 0% -> 0%
where the time goes in v1:
time: 1100 us; the launch traced here: 1090 us
  waiting for transfers between devices  392 us (36%)
  local copies, waits for them, and re-layouts  252 us (23%)
  matrix products  179 us (16%)
  starting transfers between devices  141 us (13%)
  other arithmetic  101 us (9%)
  loops' own time  16.6 us (2%)
    ppermute x150, waiting for transfers between devices, swap_lo(): return lax.ppermute(x, 'seq', [(i, i ^ bit) for i in range(self.seq_n)])  241 us
    ppermute x48, waiting for transfers between devices, next_dp(): lax.ppermute(x, 'dp', [(i, (i + 1) % self.dp_n) for i in range(self.dp_n)])  143 us
    ppermute x150, starting transfers between devices, swap_lo(): return lax.ppermute(x, 'seq', [(i, i ^ bit) for i in range(self.seq_n)])  106 us
    dynamic_update_slice x16, local copies, waits for them, and re-layouts, scatter_columns(): shard = lax.dynamic_update_slice(shard, block, (0, 0, net.lo ^ r, 0))  64.6 us
    dot_general x14, matrix products, dot_nt(): lax.dot_general(a, b, (((1,), (1,)), ((), ())), preferred_element_type=F32)  42 us
    dot_general x14, matrix products, dot(): return jnp.dot(a, b, preferred_element_type=F32)  35.8 us
    dynamic_update_slice x64, local copies, waits for them, and re-layouts, gather_rows(): full = lax.dynamic_update_slice(full, block[None, None], start)  33.7 us
    unnamed x427, local copies, waits for them, and re-layouts  30.2 us
  transfers between devices with their start and end apart: 202, of which 80 were waited for; matrix products, arithmetic and copies ran while one was open for 44% of the time, Pallas kernels for 0%

profile of v1, /device:TPU:0, one launch (start us, length us, event | category | flops | bytes accessed | tf_op | source)
XLA Modules:
  0.0 1087.0 jit_solution(930191556250306272)
XLA Ops:
  144.4 6.9 collective-permute-done.29
  167.8 19.4 %collective-permute-done.8 = bf16[128,768]{1,0:T(8,128)(2,1)S(1)} collective-permute-done((bf16[128,768]{1,0:T(8,128)(2,1)S(1)}, bf16[128,768]{1,0:T(8,128)(2,1)S(1)}, u32[]{:S(2)}, u32[]{:S(2)}) %collective-permute-start.8) | collective-permute-done | bytes 196640 | tf_op jit(solution)/shard_map/ppermute | solution.py:53
  187.2 8.2 collective-permute-done.9
  201.2 7.4 collective-permute-done.65
  211.0 6.1 collective-permute-done.48
  220.0 8.0 collective-permute-done.100
  233.7 7.4 collective-permute-done.11
  247.0 9.6 collective-permute-done.67
  259.2 6.6 collective-permute-done.90
  277.1 9.2 collective-permute-done.83
  313.8 17.0 %collective-permute-done.51 = bf16[128,1024]{1,0:T(8,128)(2,1)S(1)} collective-permute-done((bf16[128,1024]{1,0:T(8,128)(2,1)S(1)}, bf16[128,1024]{1,0:T(8,128)(2,1)S(1)}, u32[]{:S(2)}, u32[]{:S(2)}) %collective-permute-start.51) | collective-permute-done | bytes 262176 | tf_op jit(solution)/shard_map/ppermute | solution.py:53
  343.6 20.6 %while.70 = (s32[]{:T(128)}, bf16[2,4,512,64]{2,3,1,0:T(8,128)(2,1)}, f32[2,4,512]{2,1,0:T(4,128)S(1)}, f32[2,4]{1,0:T(2,128)S(1)}, s32[2]{0:T(128)S(1)}, /*inde...) while((s32[]{:T(128)}, ...), condition=%wide.region_7.8_spmd, body=%wide.region_3.7_spmd.sunk | while | flops 558495744 | bytes 32058736 | solution.py:228
  388.7 9.2 collective-permute-done.42
  401.5 8.0 collective-permute-done.53
  409.9 9.3 collective-permute-done.44
  444.9 6.7 collective-permute-done.56
  459.8 8.2 collective-permute-done.69
  477.3 20.5 %while.71 = (s32[]{:T(128)}, bf16[2,4,512,64]{2,3,1,0:T(8,128)(2,1)}, f32[2,4,512]{2,1,0:T(4,128)S(1)}, f32[2,4]{1,0:T(2,128)S(1)}, s32[2]{0:T(128)S(1)}, /*inde...) while((s32[]{:T(128)}, ...), condition=%wide.region_16.17_spmd, body=%wide.region_12.16_spmd.sunk | while | flops 558495744 | bytes 32058736 | solution.py:228
  567.5 6.1 fusion.56
  578.7 13.9 %collective-permute-done.188 = bf16[4,128,1024]{2,1,0:T(8,128)(2,1)S(1)} collective-permute-done((bf16[4,128,1024]{2,1,0:T(8,128)(2,1)S(1)}, bf16[4,128,1024]{2,1,0:T(8,128)(2,1)S(1)}, u32[]{:S(2)}, u32[]{:S(2)}) %collective-permute-start.188) | collective-permute-done | bytes 1048608 | tf_op jit(solution)/shard_map/ppermute | solution.py:53
  596.0 9.0 collective-permute-done.108
  620.6 46.8 %while.72 = (s32[]{:T(128)}, f32[4,1024,64]{1,2,0:T(8,128)S(1)}, f32[4,1024,64]{1,2,0:T(8,128)S(1)}, f32[4]{0:T(128)S(1)}, f32[4]{0:T(128)S(1)}, /*index=5*/f32[...) while((s32[]{:T(128)}, f32[4,1024,64]{1,2,0:T(8,128)S(1)}, ...), condition=%wide.region_23.24_spmd.clone, body=%wide.region_19.23_spmd.clone.sunk | while | flops 1377695744 | bytes 149474880 | solution.py:282
  688.4 6.6 collective-permute-done.191
  708.8 6.7 collective-permute-done.147
  717.1 11.9 %collective-permute-done.148 = bf16[128,768]{1,0:T(8,128)(2,1)S(1)} collective-permute-done((bf16[128,768]{1,0:T(8,128)(2,1)S(1)}, bf16[128,768]{1,0:T(8,128)(2,1)S(1)}, u32[]{:S(2)}, u32[]{:S(2)}) %collective-permute-start.148) | collective-permute-done | bytes 196640 | tf_op jit(solution)/shard_map/ppermute | solution.py:62
  739.3 8.0 collective-permute-done.152
  857.4 46.8 %while.73 = (s32[]{:T(128)}, f32[4,1024,64]{1,2,0:T(8,128)S(1)}, f32[4,1024,64]{1,2,0:T(8,128)S(1)}, f32[4]{0:T(128)S(1)}, f32[4]{0:T(128)S(1)}, /*index=5*/f32[...) while((s32[]{:T(128)}, f32[4,1024,64]{1,2,0:T(8,128)S(1)}, ...), condition=%wide.region_32.33_spmd.clone, body=%wide.region_28.32_spmd.clone.sunk | while | flops 1377695744 | bytes 149474880 | solution.py:282
  927.3 8.2 collective-permute-done.187
  943.1 13.6 %collective-permute-done.138 = bf16[4,128,768]{2,1,0:T(8,128)(2,1)S(1)} collective-permute-done((bf16[4,128,768]{2,1,0:T(8,128)(2,1)S(1)}, bf16[4,128,768]{2,1,0:T(8,128)(2,1)S(1)}, u32[]{:S(2)}, u32[]{:S(2)}) %collective-permute-start.138) | collective-permute-done | bytes 786464 | tf_op jit(solution)/shard_map/ppermute | solution.py:53
  961.5 10.1 collective-permute-done.163
  971.9 7.1 collective-permute-done.139
  1019.1 10.3 collective-permute-done.170
  (1389 shorter events, 805.9 us)
Async XLA Ops:
  2.3 58.1 %collective-permute-start.23 = (bf16[32,1024]{1,0:T(8,128)(2,1)}, bf16[32,1024]{1,0:T(8,128)(2,1)}, u32[]{:S(2)}, u32[]{:S(2)}) collective-permute-start(bf16[32,1024]{1,0:T(8,128)(2,1)} %get-tuple-element.902), channel_id=1, source_target_pairs={{0,4},{1,5},{2,6},{3,7},{4,0},{5,1},{6,2},{7,3},{8,12},{9,13},{10,... | collective-permute-start | bytes 196616 | tf_op jit(solution)/shard_map/ppermute | solution.py:53
  5.2 60.4 %collective-permute-start.24 = (bf16[32,1024]{1,0:T(8,128)(2,1)}, bf16[32,1024]{1,0:T(8,128)(2,1)}, u32[]{:S(2)}, u32[]{:S(2)}) collective-permute-start(bf16[32,1024]{1,0:T(8,128)(2,1)} %get-tuple-element.902), channel_id=1, source_target_pairs={{0,8},{8,16},{16,24},{24,0},{1,9},{9,17},{17,25},{25,1},{2,10},{10... | collective-permute-start | bytes 196616 | tf_op jit(solution)/shard_map/ppermute | solution.py:62
  10.5 128.4 %collective-permute-start.45 = (bf16[128,1024]{1,0:T(8,128)(2,1)}, bf16[128,1024]{1,0:T(8,128)(2,1)}, u32[]{:S(2)}, u32[]{:S(2)}) collective-permute-start(bf16[128,1024]{1,0:T(8,128)(2,1)} %get-tuple-element.872), channel_id=1, source_target_pairs={{0,4},{1,5},{2,6},{3,7},{4,0},{5,1},{6,2},{7,3},{8,12},{9,13},{10,... | collective-permute-start | bytes 786440 | tf_op jit(solution)/shard_map/ppermute | solution.py:53
  45.2 96.9 %collective-permute-start.46 = (bf16[128,1024]{1,0:T(8,128)(2,1)}, bf16[128,1024]{1,0:T(8,128)(2,1)S(1)}, u32[]{:S(2)}, u32[]{:S(2)}) collective-permute-start(bf16[128,1024]{1,0:T(8,128)(2,1)} %get-tuple-element.872), channel_id=1, source_target_pairs={{0,8},{8,16},{16,24},{24,0},{1,9},{9,17},{17,25},{25,1},{2,10},{10... | collective-permute-start | bytes 786440 | tf_op jit(solution)/shard_map/ppermute | solution.py:62
  74.4 46.7 %collective-permute-start.36 = (bf16[32,2048]{1,0:T(8,128)(2,1)}, bf16[32,2048]{1,0:T(8,128)(2,1)S(1)}, u32[]{:S(2)}, u32[]{:S(2)}) collective-permute-start(bf16[32,2048]{1,0:T(8,128)(2,1)} %bitcast.766), channel_id=1, source_target_pairs={{0,2},{1,3},{2,0},{3,1},{4,6},{5,7},{6,4},{7,5},{8,10},{9,11},{10,... | collective-permute-start | bytes 393224 | tf_op jit(solution)/shard_map/ppermute | solution.py:53
  78.4 48.7 %collective-permute-start.88 = (bf16[32,2048]{1,0:T(8,128)(2,1)S(1)}, bf16[32,2048]{1,0:T(8,128)(2,1)S(1)}, u32[]{:S(2)}, u32[]{:S(2)}) collective-permute-start(bf16[32,2048]{1,0:T(8,128)(2,1)S(1)} %bitcast.938), channel_id=1, source_target_pairs={{0,2},{1,3},{2,0},{3,1},{4,6},{5,7},{6,4},{7,5},{8,10},{9,11},{10,... | collective-permute-start | bytes 393224 | tf_op jit(solution)/shard_map/ppermute | solution.py:53
  162.0 108.9 %collective-permute-start.30 = (bf16[4,2,32,1024]{3,2,1,0:T(8,128)(2,1)S(1)}, bf16[4,2,32,1024]{3,2,1,0:T(8,128)(2,1)S(1)}, u32[]{:S(2)}, u32[]{:S(2)}) collective-permute-start(bf16[4,2,32,1024]{3,2,1,0:T(8,128)(2,1)S(1)} %bitcast_dynamic-update-slice_fusion.70), channel_id=1, source_target_pairs={{0,1},{1,0},{2,3},{3,2},{4,5},{5,4},{6,7},{7,6},{8,9},{9,8},{10,11... | collective-permute-start | bytes 1572872 | tf_op jit(solution)/shard_map/ppermute | solution.py:53
  162.8 110.6 %collective-permute-start.31 = (bf16[4,2,32,1024]{3,2,1,0:T(8,128)(2,1)S(1)}, bf16[4,2,32,1024]{3,2,1,0:T(8,128)(2,1)}, u32[]{:S(2)}, u32[]{:S(2)}) collective-permute-start(bf16[4,2,32,1024]{3,2,1,0:T(8,128)(2,1)S(1)} %bitcast_dynamic-update-slice_fusion.70), channel_id=1, source_target_pairs={{0,2},{1,3},{2,0},{3,1},{4,6},{5,7},{6,4},{7,5},{8,10},{9,11},{10,... | collective-permute-start | bytes 1572872 | tf_op jit(solution)/shard_map/ppermute | solution.py:53
  163.3 94.7 %collective-permute-start.38 = (bf16[128,2048]{1,0:T(8,128)(2,1)S(1)}, bf16[128,2048]{1,0:T(8,128)(2,1)S(1)}, u32[]{:S(2)}, u32[]{:S(2)}) collective-permute-start(bf16[128,2048]{1,0:T(8,128)(2,1)S(1)} %bitcast.888), channel_id=1, source_target_pairs={{0,4},{1,5},{2,6},{3,7},{4,0},{5,1},{6,2},{7,3},{8,12},{9,13},{10,... | collective-permute-start | bytes 1572872 | tf_op jit(solution)/shard_map/ppermute | solution.py:53
  164.9 43.7 %collective-permute-start.47 = (bf16[128,1024]{1,0:T(8,128)(2,1)S(1)}, bf16[128,1024]{1,0:T(8,128)(2,1)S(1)}, u32[]{:S(2)}, u32[]{:S(2)}) collective-permute-start(bf16[128,1024]{1,0:T(8,128)(2,1)S(1)} %collective-permute-done.46), channel_id=1, source_target_pairs={{0,4},{1,5},{2,6},{3,7},{4,0},{5,1},{6,2},{7,3},{8,12},{9,13},{10,... | collective-permute-start | bytes 786440 | tf_op jit(solution)/shard_map/ppermute | solution.py:53
  217.7 40.3 %collective-permute-start.39 = (bf16[128,2048]{1,0:T(8,128)(2,1)S(1)}, bf16[128,2048]{1,0:T(8,128)(2,1)}, u32[]{:S(2)}, u32[]{:S(2)}) collective-permute-start(bf16[128,2048]{1,0:T(8,128)(2,1)S(1)} %bitcast.889), channel_id=1, source_target_pairs={{0,8},{8,16},{16,24},{24,0},{1,9},{9,17},{17,25},{25,1},{2,10},{10... | collective-permute-start | bytes 1572872 | tf_op jit(solution)/shard_map/ppermute | solution.py:62
  258.1 52.5 %collective-permute-start.1 = (bf16[256,1024]{1,0:T(8,128)(2,1)S(1)}, bf16[256,1024]{1,0:T(8,128)(2,1)S(1)}, u32[]{:S(2)}, u32[]{:S(2)}) collective-permute-start(bf16[256,1024]{1,0:T(8,128)(2,1)S(1)} %fusion.113), channel_id=1, source_target_pairs={{0,1},{1,0},{2,3},{3,2},{4,5},{5,4},{6,7},{7,6},{8,9},{9,8},{10,11... | collective-permute-start | bytes 1572872 | tf_op jit(solution)/shard_map/ppermute | solution.py:53
  265.8 47.5 %collective-permute-start.13 = (bf16[256,1024]{1,0:T(8,128)(2,1)S(1)}, bf16[256,1024]{1,0:T(8,128)(2,1)S(1)}, u32[]{:S(2)}, u32[]{:S(2)}) collective-permute-start(bf16[256,1024]{1,0:T(8,128)(2,1)S(1)} %fusion.113), channel_id=1, source_target_pairs={{0,2},{1,3},{2,0},{3,1},{4,6},{5,7},{6,4},{7,5},{8,10},{9,11},{10,... | collective-permute-start | bytes 1572872 | tf_op jit(solution)/shard_map/ppermute | solution.py:53
  308.5 61.0 %collective-permute-start.32 = (bf16[4,2,32,1024]{3,2,1,0:T(8,128)(2,1)}, bf16[4,2,32,1024]{3,2,1,0:T(8,128)(2,1)}, u32[]{:S(2)}, u32[]{:S(2)}) collective-permute-start(bf16[4,2,32,1024]{3,2,1,0:T(8,128)(2,1)} %collective-permute-done.31), channel_id=1, source_target_pairs={{0,1},{1,0},{2,3},{3,2},{4,5},{5,4},{6,7},{7,6},{8,9},{9,8},{10,11... | collective-permute-start | bytes 1572872 | tf_op jit(solution)/shard_map/ppermute | solution.py:53
  310.2 54.1 %collective-permute-start.40 = (bf16[128,2048]{1,0:T(8,128)(2,1)}, bf16[128,2048]{1,0:T(8,128)(2,1)}, u32[]{:S(2)}, u32[]{:S(2)}) collective-permute-start(bf16[128,2048]{1,0:T(8,128)(2,1)} %collective-permute-done.39), channel_id=1, source_target_pairs={{0,4},{1,5},{2,6},{3,7},{4,0},{5,1},{6,2},{7,3},{8,12},{9,13},{10,... | collective-permute-start | bytes 1572872 | tf_op jit(solution)/shard_map/ppermute | solution.py:53
  366.9 71.9 %collective-permute-start.114 = (bf16[256,1024]{1,0:T(8,128)(2,1)}, bf16[256,1024]{1,0:T(8,128)(2,1)}, u32[]{:S(2)}, u32[]{:S(2)}) collective-permute-start(bf16[256,1024]{1,0:T(8,128)(2,1)} %copy-done.114), channel_id=1, source_target_pairs={{0,1},{1,0},{2,3},{3,2},{4,5},{5,4},{6,7},{7,6},{8,9},{9,8},{10,11... | collective-permute-start | bytes 1572872 | tf_op jit(solution)/shard_map/ppermute | solution.py:53
  384.3 71.7 %collective-permute-start.94 = (bf16[128,2048]{1,0:T(8,128)(2,1)}, bf16[128,2048]{1,0:T(8,128)(2,1)}, u32[]{:S(2)}, u32[]{:S(2)}) collective-permute-start(bf16[128,2048]{1,0:T(8,128)(2,1)} %collective-permute-done.93), channel_id=1, source_target_pairs={{0,4},{1,5},{2,6},{3,7},{4,0},{5,1},{6,2},{7,3},{8,12},{9,13},{10,... | collective-permute-start | bytes 1572872 | tf_op jit(solution)/shard_map/ppermute | solution.py:53
  537.5 58.5 %collective-permute-start.104 = (bf16[256,1024]{1,0:T(8,128)(2,1)S(1)}, bf16[256,1024]{1,0:T(8,128)(2,1)S(1)}, u32[]{:S(2)}, u32[]{:S(2)}) collective-permute-start(bf16[256,1024]{1,0:T(8,128)(2,1)S(1)} %split.241), channel_id=1, source_target_pairs={{0,1},{1,0},{2,3},{3,2},{4,5},{5,4},{6,7},{7,6},{8,9},{9,8},{10,11... | collective-permute-start | bytes 1572872 | tf_op jit(solution)/shard_map/ppermute | solution.py:53
  543.6 51.0 %collective-permute-start.112 = (bf16[256,1024]{1,0:T(8,128)(2,1)S(1)}, bf16[256,1024]{1,0:T(8,128)(2,1)S(1)}, u32[]{:S(2)}, u32[]{:S(2)}) collective-permute-start(bf16[256,1024]{1,0:T(8,128)(2,1)S(1)} %split.247), channel_id=1, source_target_pairs={{0,1},{1,0},{2,3},{3,2},{4,5},{5,4},{6,7},{7,6},{8,9},{9,8},{10,11... | collective-permute-start | bytes 1572872 | tf_op jit(solution)/shard_map/ppermute | solution.py:53
  575.5 123.4 %collective-permute-start.176 = (bf16[4,128,2048]{2,1,0:T(8,128)(2,1)}, bf16[4,128,2048]{2,1,0:T(8,128)(2,1)}, u32[]{:S(2)}, u32[]{:S(2)}) collective-permute-start(bf16[4,128,2048]{2,1,0:T(8,128)(2,1)} %fusion.69), channel_id=1, source_target_pairs={{0,4},{1,5},{2,6},{3,7},{4,0},{5,1},{6,2},{7,3},{8,12},{9,13},{10,... | collective-permute-start | bytes 6291464 | tf_op jit(solution)/shard_map/ppermute | solution.py:53
  614.2 71.5 %collective-permute-start.109 = (bf16[128,1024]{1,0:T(8,128)(2,1)}, bf16[128,1024]{1,0:T(8,128)(2,1)}, u32[]{:S(2)}, u32[]{:S(2)}) collective-permute-start(bf16[128,1024]{1,0:T(8,128)(2,1)} %split.245), channel_id=1, source_target_pairs={{0,4},{1,5},{2,6},{3,7},{4,0},{5,1},{6,2},{7,3},{8,12},{9,13},{10,... | collective-permute-start | bytes 786440 | tf_op jit(solution)/shard_map/ppermute | solution.py:53
  615.3 67.6 %collective-permute-start.190 = (bf16[128,1024]{1,0:T(8,128)(2,1)S(1)}, bf16[128,1024]{1,0:T(8,128)(2,1)}, u32[]{:S(2)}, u32[]{:S(2)}) collective-permute-start(bf16[128,1024]{1,0:T(8,128)(2,1)S(1)} %fusion.210), channel_id=1, source_target_pairs={{0,8},{8,16},{16,24},{24,0},{1,9},{9,17},{17,25},{25,1},{2,10},{10... | collective-permute-start | bytes 786440 | tf_op jit(solution)/shard_map/ppermute | solution.py:62
  772.5 61.1 %collective-permute-start.125 = (bf16[256,1024]{1,0:T(8,128)(2,1)}, bf16[256,1024]{1,0:T(8,128)(2,1)}, u32[]{:S(2)}, u32[]{:S(2)}) collective-permute-start(bf16[256,1024]{1,0:T(8,128)(2,1)} %split.259), channel_id=1, source_target_pairs={{0,1},{1,0},{2,3},{3,2},{4,5},{5,4},{6,7},{7,6},{8,9},{9,8},{10,11... | collective-permute-start | bytes 1572872 | tf_op jit(solution)/shard_map/ppermute | solution.py:53
  786.9 43.6 %collective-permute-start.184 = (bf16[4,128,1024]{2,1,0:T(8,128)(2,1)}, bf16[4,128,1024]{2,1,0:T(8,128)(2,1)}, u32[]{:S(2)}, u32[]{:S(2)}) collective-permute-start(bf16[4,128,1024]{2,1,0:T(8,128)(2,1)} %fusion.137), channel_id=1, source_target_pairs={{0,4},{1,5},{2,6},{3,7},{4,0},{5,1},{6,2},{7,3},{8,12},{9,13},{10,... | collective-permute-start | bytes 3145736 | tf_op jit(solution)/shard_map/ppermute | solution.py:53
  814.7 123.3 %collective-permute-start.168 = (bf16[4,128,2048]{2,1,0:T(8,128)(2,1)}, bf16[4,128,2048]{2,1,0:T(8,128)(2,1)}, u32[]{:S(2)}, u32[]{:S(2)}) collective-permute-start(bf16[4,128,2048]{2,1,0:T(8,128)(2,1)} %fusion.68), channel_id=1, source_target_pairs={{0,4},{1,5},{2,6},{3,7},{4,0},{5,1},{6,2},{7,3},{8,12},{9,13},{10,... | collective-permute-start | bytes 6291464 | tf_op jit(solution)/shard_map/ppermute | solution.py:53
  849.5 74.3 %collective-permute-start.155 = (bf16[4,2,32,1024]{3,2,0,1:T(8,128)(2,1)}, bf16[4,2,32,1024]{3,2,0,1:T(8,128)(2,1)}, u32[]{:S(2)}, u32[]{:S(2)}) collective-permute-start(bf16[4,2,32,1024]{3,2,0,1:T(8,128)(2,1)} %bitcast.760), channel_id=1, source_target_pairs={{0,1},{1,0},{2,3},{3,2},{4,5},{5,4},{6,7},{7,6},{8,9},{9,8},{10,11... | collective-permute-start | bytes 1572872 | tf_op jit(solution)/shard_map/ppermute | solution.py:53
  850.1 107.2 %collective-permute-start.154 = (bf16[4,2,32,1024]{3,2,0,1:T(8,128)(2,1)}, bf16[4,2,32,1024]{3,2,0,1:T(8,128)(2,1)}, u32[]{:S(2)}, u32[]{:S(2)}) collective-permute-start(bf16[4,2,32,1024]{3,2,0,1:T(8,128)(2,1)} %bitcast.759), channel_id=1, source_target_pairs={{0,1},{1,0},{2,3},{3,2},{4,5},{5,4},{6,7},{7,6},{8,9},{9,8},{10,11... | collective-permute-start | bytes 1572872 | tf_op jit(solution)/shard_map/ppermute | solution.py:53
  850.4 75.1 %collective-permute-start.162 = (bf16[4,2,32,1024]{3,2,0,1:T(8,128)(2,1)}, bf16[4,2,32,1024]{3,2,0,1:T(8,128)(2,1)}, u32[]{:S(2)}, u32[]{:S(2)}) collective-permute-start(bf16[4,2,32,1024]{3,2,0,1:T(8,128)(2,1)} %bitcast.762), channel_id=1, source_target_pairs={{0,1},{1,0},{2,3},{3,2},{4,5},{5,4},{6,7},{7,6},{8,9},{9,8},{10,11... | collective-permute-start | bytes 1572872 | tf_op jit(solution)/shard_map/ppermute | solution.py:53
  851.8 70.8 %collective-permute-start.186 = (bf16[128,1024]{1,0:T(8,128)(2,1)S(1)}, bf16[128,1024]{1,0:T(8,128)(2,1)}, u32[]{:S(2)}, u32[]{:S(2)}) collective-permute-start(bf16[128,1024]{1,0:T(8,128)(2,1)S(1)} %fusion.213), channel_id=1, source_target_pairs={{0,8},{8,16},{16,24},{24,0},{1,9},{9,17},{17,25},{25,1},{2,10},{10... | collective-permute-start | bytes 786440 | tf_op jit(solution)/shard_map/ppermute | solution.py:62
  935.6 44.5 %collective-permute-start.134 = (bf16[256,1024]{1,0:T(8,128)(2,1)S(1)}, bf16[256,1024]{1,0:T(8,128)(2,1)S(1)}, u32[]{:S(2)}, u32[]{:S(2)}) collective-permute-start(bf16[256,1024]{1,0:T(8,128)(2,1)S(1)} %split.266), channel_id=1, source_target_pairs={{0,1},{1,0},{2,3},{3,2},{4,5},{5,4},{6,7},{7,6},{8,9},{9,8},{10,11... | collective-permute-start | bytes 1572872 | tf_op jit(solution)/shard_map/ppermute | solution.py:53
  959.0 54.5 %collective-permute-start.169 = (bf16[128,2048]{1,0:T(8,128)(2,1)}, bf16[128,2048]{1,0:T(8,128)(2,1)S(1)}, u32[]{:S(2)}, u32[]{:S(2)}) collective-permute-start(bf16[128,2048]{1,0:T(8,128)(2,1)} %fusion.197), channel_id=1, source_target_pairs={{0,8},{8,16},{16,24},{24,0},{1,9},{9,17},{17,25},{25,1},{2,10},{10... | collective-permute-start | bytes 1572872 | tf_op jit(solution)/shard_map/ppermute | solution.py:62
  993.3 66.6 %collective-permute-start.137 = (f32[128,1024]{1,0:T(8,128)}, f32[128,1024]{1,0:T(8,128)}, u32[]{:S(2)}, u32[]{:S(2)}) collective-permute-start(f32[128,1024]{1,0:T(8,128)} %split.271), channel_id=1, source_target_pairs={{0,4},{1,5},{2,6},{3,7},{4,0},{5,1},{6,2},{7,3},{8,12},{9,13},{10,... | collective-permute-start | bytes 1572872 | tf_op jit(solution)/shard_map/ppermute | solution.py:53
  (398 other events, 6725.8 us)

commit v2 on v1

v2 whole, which is shorter than its diff:
```python
import functools
import math

import jax
import jax.numpy as jnp
from jax import lax
from jax.experimental import pallas as pl
from jax.experimental.pallas import tpu as pltpu
from jax.sharding import Mesh
from jax.sharding import PartitionSpec as P

EPSILON = 1e-05
CLIP_LIMIT = 2.0
FLOOR_VALUE = -1e30
BF = jnp.bfloat16
F32 = jnp.float32


def rms_scale(values, gain):
    return values * lax.rsqrt(jnp.mean(values * values, axis=-1, keepdims=True) + EPSILON) * gain


def dot(a, b):
    return jnp.dot(a, b, preferred_element_type=F32)


def pick(array, index, axis=0):
    return lax.dynamic_index_in_dim(array, index, axis, keepdims=False)


class Net:
    def __init__(self):
        self.dp_n, self.hi_n, self.lo_n = (lax.axis_size(name) for name in ("dp", "hi", "lo"))
        self.dp, self.hi, self.lo = (lax.axis_index(name) for name in ("dp", "hi", "lo"))
        self.seq_n = self.hi_n * self.lo_n
        self.seq = self.hi * self.lo_n + self.lo
        self.seq_bits = [1 << b for b in range(self.seq_n.bit_length() - 1)]
        self.lo_bits = [b for b in self.seq_bits if b < self.lo_n]
        self.hi_bits = [b // self.lo_n for b in self.seq_bits if b >= self.lo_n]
        self.chains = {"dp": [], "hi": []}

    def queued(self, name, send, x, depth=2):
        chain = self.chains[name]
        if len(chain) >= depth:
            x = after(x, chain[-depth])
        chain.append(send(x))
        return chain[-1]

    def swap(self, x, bit):
        if bit < self.lo_n:
            return lax.ppermute(x, "lo", [(i, i ^ bit) for i in range(self.lo_n)])
        bit //= self.lo_n
        return lax.ppermute(x, "hi", [(i, i ^ bit) for i in range(self.hi_n)])

    def swap_hi(self, x, bit):
        return self.swap(x, bit * self.lo_n)

    def swap_dp(self, x, bit):
        return lax.ppermute(x, "dp", [(i, i ^ bit) for i in range(self.dp_n)])

    def next_dp(self, x):
        return lax.ppermute(x, "dp", [(i, (i + 1) % self.dp_n) for i in range(self.dp_n)])

    def gather(self, block, bits):
        blocks = {0: block}
        if len(bits) == 3:
            core, first, second = bits
            half = block.shape[0] // 2
            blocks[first], blocks[second] = self.swap(block, first), self.swap(block, second)
            corner = (
                self.swap(blocks[first][:half], second),
                self.swap(blocks[second][half:], first),
            )
            blocks[first | second] = jnp.concatenate(corner, axis=0)
            for r in list(blocks):
                blocks[r | core] = self.swap(blocks[r], core)
        else:
            for bit in reversed(bits):
                for r in list(blocks):
                    blocks[r | bit] = self.swap(blocks[r], bit)
        return [blocks[r] for r in range(len(blocks))]

    def add_swapped(self, mine, sent, bit):
        return mine.astype(F32) + self.swap(sent.astype(BF), bit).astype(F32)

    def scatter(self, blocks, bits):
        if len(bits) == 3:
            core, first, second = bits
            half = blocks[0].shape[0] // 2
            order = (first | second, first, second, 0)
            sums = {r: self.add_swapped(blocks[r], blocks[r | core], core) for r in order}
            corner = sums[first | second]
            top = self.add_swapped(sums[second][:half], corner[:half], first)
            bottom = self.add_swapped(sums[first][half:], corner[half:], second)
            to_second = jnp.concatenate([top, sums[second][half:]], axis=0)
            to_first = jnp.concatenate([sums[first][:half], bottom], axis=0)
            total = self.add_swapped(sums[0], to_first, first)
            return self.add_swapped(total, to_second, second)
        blocks = dict(enumerate(blocks))
        for bit in bits:
            blocks = {
                r: self.add_swapped(blocks[r], blocks[r | bit], bit)
                for r in sorted(blocks, reverse=True)
                if not r & bit
            }
        return blocks[0]

    def trade(self, blocks, bits):
        blocks = dict(enumerate(blocks))
        rows = blocks[0].shape[0]
        for bit in reversed(bits):
            moving = [r for r in blocks if r & bit]
            if bit == 1:
                for r in moving:
                    blocks[r] = self.swap(blocks[r], bit)
            else:
                sent = self.swap(jnp.concatenate([blocks[r] for r in moving], axis=0), bit)
                for n, r in enumerate(moving):
                    blocks[r] = sent[n * rows : (n + 1) * rows]
        return [blocks[r] for r in range(len(blocks))]

    def trade_hi(self, blocks):
        blocks = list(blocks)
        for bit in self.hi_bits:
            blocks = [self.swap_hi(b, bit) if q & bit else b for q, b in enumerate(blocks)]
        return blocks

    def all_small(self, x, combine):
        for bit in self.seq_bits:
            x = combine(x, self.swap(x, bit))
        bit = 1
        while bit < self.dp_n:
            x = combine(x, self.swap_dp(x, bit))
            bit *= 2
        return x

    def gather_rows(self, own):
        full = place_first(own, self.dp_n * self.hi_n, self.dp * self.hi_n + self.hi)
        full = full.reshape((self.dp_n, self.hi_n) + own.shape)
        chunk = own
        for step in range(self.dp_n):
            if step:
                chunk = self.queued("dp", self.next_dp, chunk)
            source = (self.dp - step) % self.dp_n
            blocks = {0: chunk}
            for bit in self.hi_bits:
                for q in list(blocks):
                    blocks[q | bit] = self.queued(
                        "hi", lambda x, bit=bit: self.swap_hi(x, bit), blocks[q]
                    )
            for q, block in blocks.items():
                if step or q:
                    start = (source, self.hi ^ q) + (0,) * own.ndim
                    full = lax.dynamic_update_slice(full, block[None, None], start)
        return full

    def scatter_rows(self, mine, other):
        mine = self.add_swapped(mine, other, self.lo_n)
        running = pick(mine, (self.dp - 1) % self.dp_n)
        for step in range(1, self.dp_n):
            running = self.next_dp(running.astype(BF)).astype(F32)
            running = running + pick(mine, (self.dp - 1 - step) % self.dp_n)
        return running


def after(x, *earlier):
    return lax.optimization_barrier((x,) + earlier)[0]


def in_order(blocks, index):
    stacked = jnp.stack(blocks)
    return jnp.stack([pick(stacked, index ^ j) for j in range(len(blocks))])


def place_first(block, count, position):
    def kernel(at, block_ref, out_ref):
        out_ref[0] = block_ref[...]

    zeros = (0,) * block.ndim
    return pl.pallas_call(
        kernel,
        grid_spec=pltpu.PrefetchScalarGridSpec(
            num_scalar_prefetch=1,
            grid=(1,),
            in_specs=[pl.BlockSpec(block.shape, lambda i, at: zeros)],
            out_specs=pl.BlockSpec((1,) + block.shape, lambda i, at: (at[0],) + zeros),
        ),
        out_shape=jax.ShapeDtypeStruct((count,) + block.shape, block.dtype),
        name="place_first",
    )(position.astype(jnp.int32).reshape(1), block)


def split_columns(shard, index, count, width):
    rows = shard.shape[0]
    parts = shard.shape[1] // count // width
    if width % LANES:
        shard = shard.reshape(rows, parts, count, width)
        return [pick(shard, index ^ r, 2).reshape(rows, -1) for r in range(count)]

    def kernel(at, shard_ref, *outs):
        for r, out in enumerate(outs):
            for p in range(parts):
                start = pl.multiple_of((p * count + (at[0] ^ r)) * width, width)
                out[:, p * width : (p + 1) * width] = shard_ref[:, pl.ds(start, width)]

    return pl.pallas_call(
        kernel,
        in_specs=[pl.BlockSpec(memory_space=pltpu.SMEM), pl.BlockSpec(memory_space=pltpu.VMEM)],
        out_specs=[pl.BlockSpec(memory_space=pltpu.VMEM)] * count,
        out_shape=[jax.ShapeDtypeStruct((rows, parts * width), BF)] * count,
        name="split_columns",
    )(index.astype(jnp.int32).reshape(1), shard)


def merge_columns(blocks, index, width):
    rows, count = blocks[0].shape[0], len(blocks)
    parts = blocks[0].shape[1] // width
    if width % LANES:
        shard = in_order(blocks, index).reshape(count, rows, parts, width)
        return shard.transpose(1, 2, 0, 3).reshape(rows, -1).astype(F32)

    def kernel(at, *refs):
        out = refs[-1]
        for r, block in enumerate(refs[:-1]):
            for p in range(parts):
                start = pl.multiple_of((p * count + (at[0] ^ r)) * width, width)
                out[:, pl.ds(start, width)] = block[:, p * width : (p + 1) * width].astype(F32)

    return pl.pallas_call(
        kernel,
        in_specs=[pl.BlockSpec(memory_space=pltpu.SMEM)]
        + [pl.BlockSpec(memory_space=pltpu.VMEM)] * count,
        out_specs=pl.BlockSpec(memory_space=pltpu.VMEM),
        out_shape=jax.ShapeDtypeStruct((rows, parts * count * width), F32),
        name="merge_columns",
    )(index.astype(jnp.int32).reshape(1), *blocks)


def trade_columns(net, shard, bits, width):
    index, count = (net.seq, net.seq_n) if bits == net.seq_bits else (net.lo, net.lo_n)
    blocks = net.trade(split_columns(shard, index, count, width), bits)
    return join_rows(blocks, index)


def restore_columns(net, own, bits, width):
    index, count = (net.seq, net.seq_n) if bits == net.seq_bits else (net.lo, net.lo_n)
    own = own.astype(BF).reshape(count, -1, own.shape[1])
    blocks = net.trade([pick(own, index ^ r) for r in range(count)], bits)
    return merge_columns(blocks, index, width)


def fetch_attention(net, own_qkv, own_out):
    rows, cut = own_qkv.shape
    pieces = jnp.split(own_out, rows // own_out.shape[0], axis=1)
    own = jnp.concatenate([own_qkv, jnp.concatenate(pieces, axis=0)], axis=1)
    full = net.gather_rows(own).reshape(-1, rows, own.shape[1])
    blocks = net.gather(full[:, :, cut:], net.lo_bits)
    return full.reshape(-1, own.shape[1]), join_middle(blocks, net.lo, own_out.shape[0])


def fetch_hidden(net, own_in, own_down):
    columns = own_in.shape[1]
    pieces = jnp.split(own_down, own_down.shape[1] // columns, axis=1)
    own = jnp.concatenate([own_in] + pieces, axis=0)
    return lax.all_gather(own, "dp", axis=0)


def scatter_hidden(net, grads, rows_in):
    own = lax.psum_scatter(grads, "dp", scatter_dimension=0)
    own_in, own_down = own[:rows_in], own[rows_in:]
    pieces = rows_in * net.dp_n // grads.shape[2]
    return own_in, jnp.concatenate(jnp.split(own_down, pieces, axis=0), axis=1).astype(F32)


LANES = 128
NT = (((1,), (1,)), ((), ()))
TN = (((0,), (0,)), ((), ()))
VMEM = pl.BlockSpec(memory_space=pltpu.VMEM)
SMEM = pl.BlockSpec(memory_space=pltpu.SMEM)
LIMIT = 24 * 2**20


def on_chip(kernel, outs, *arrays, at=None, scratch=(), flops=0, name=None):
    outs = [jax.ShapeDtypeStruct(*out) for out in outs]
    moved = sum(math.prod(x.shape) * x.dtype.itemsize for x in list(arrays) + outs)
    first = [] if at is None else [at.astype(jnp.int32).reshape(1)]
    return pl.pallas_call(
        kernel,
        in_specs=[SMEM] * len(first) + [VMEM] * len(arrays),
        out_specs=[VMEM] * len(outs),
        out_shape=outs,
        scratch_shapes=list(scratch),
        compiler_params=pltpu.CompilerParams(vmem_limit_bytes=LIMIT),
        cost_estimate=pl.CostEstimate(flops=flops, bytes_accessed=moved, transcendentals=0),
        name=name,
    )(*first, *arrays)


def project(blocks, matrix, columns):
    rows = blocks[0].shape[0]

    def kernel(*refs):
        *ins, m, out = refs
        for n, x in enumerate(ins):
            out[n * rows : (n + 1) * rows, :] = dot(x[...], m[:, :columns]).astype(BF)

    return on_chip(
        kernel,
        [((rows * len(blocks), columns), BF)],
        *blocks,
        matrix,
        flops=2 * rows * len(blocks) * matrix.size,
        name="project",
    )[0]


def out_project(state, arrived, matrix, gain, at):
    rows, width = state.shape
    heads = arrived[0].shape[1]

    def kernel(index, x, m, g, *refs):
        *ins, middle, second = refs
        total = x[...]
        for r, block in enumerate(ins):
            start = pl.multiple_of((index[0] ^ r) * heads, heads)
            total = total + dot(block[...], m[pl.ds(start, heads), :])
        middle[...] = total
        second[...] = rms_scale(total, g[...]).astype(BF)

    return on_chip(
        kernel,
        [((rows, width), F32), ((rows, width), BF)],
        state,
        matrix,
        gain.reshape(1, width),
        *arrived,
        at=at,
        flops=2 * rows * matrix.size,
        name="out_project",
    )


def hidden_matrices(pack, width):
    rows = width // pack.shape[0]
    columns = pack.shape[2]
    down = (pack.shape[1] - rows) * columns // width
    m_in = jnp.concatenate([pack[n, :rows, :] for n in range(pack.shape[0])], axis=0)
    m_down = []
    for n in range(pack.shape[0]):
        starts = range(rows, pack.shape[1], down)
        m_down.append(jnp.concatenate([pack[n, p : p + down, :] for p in starts], axis=1))
    return m_in, jnp.concatenate(m_down, axis=0)


def feed_forward(blocks, pack):
    rows, width = blocks[0].shape
    count, hidden = len(blocks), pack.shape[2] // 2

    def kernel(*refs):
        ins, (m, joined), outs = refs[:count], refs[count : count + 2], refs[count + 2 :]
        m_in, m_down = hidden_matrices(m, width)
        for n, (x, out) in enumerate(zip(ins, outs)):
            both = dot(x[...], m_in)
            joined[n * rows : (n + 1) * rows, :] = both.astype(BF)
            gate, up = both[:, :hidden], both[:, hidden:]
            gated = gate / (1.0 + jnp.exp(-gate)) * up
            out[...] = dot(gated.astype(BF), m_down).astype(BF)

    joined, *parts = on_chip(
        kernel,
        [((rows * count, 2 * hidden), BF)] + [((rows, width), BF)] * count,
        *blocks,
        pack,
        flops=2 * rows * count * pack.size,
        name="feed_forward",
    )
    return joined, parts


def feed_backward(blocks, joined, pack):
    rows, width = blocks[0].shape
    count, hidden = len(blocks), pack.shape[2] // 2

    def kernel(*refs):
        ins, (j, m, grad_joined, gated) = refs[:count], refs[count : count + 4]
        m_in, m_down = hidden_matrices(m, width)
        for n, (x, out) in enumerate(zip(ins, refs[count + 4 :])):
            part = slice(n * rows, (n + 1) * rows)
            gate = j[part, :hidden].astype(F32)
            up = j[part, hidden:].astype(F32)
            grad = lax.dot_general(x[...], m_down, NT, preferred_element_type=F32)
            sigmoid = 1.0 / (1.0 + jnp.exp(-gate))
            silu = gate * sigmoid
            gated[part, :] = (silu * up).astype(BF)
            grad_gate = grad * up * (sigmoid + silu * (1.0 - sigmoid))
            grad_joined[part, :hidden] = grad_gate.astype(BF)
            grad_joined[part, hidden:] = (grad * silu).astype(BF)
            total = lax.dot_general(grad_joined[part, :], m_in, NT, preferred_element_type=F32)
            out[...] = total.astype(BF)

    grad_joined, gated, *parts = on_chip(
        kernel,
        [((rows * count, 2 * hidden), BF), ((rows * count, hidden), BF)]
        + [((rows, width), BF)] * count,
        *blocks,
        joined,
        pack,
        flops=2 * rows * count * pack.size,
        name="feed_backward",
    )
    return grad_joined, gated, parts


def side_by_side(refs, scratch, sems, start=0):
    copies, column = [], 0
    for group in refs:
        row = 0
        for x in group:
            place = scratch.at[pl.ds(row, x.shape[0]), pl.ds(column, x.shape[1])]
            copies.append(pltpu.make_async_copy(x, place, sems.at[start + len(copies)]))
            row += x.shape[0]
        column += group[0].shape[1]
    return copies


def weight_call(kernel, outs, groups, shapes, at, flops, name):
    flat = [x for group in groups for column in group for x in column]
    outs = [jax.ShapeDtypeStruct(*out) for out in outs]
    moved = sum(math.prod(x.shape) * x.dtype.itemsize for x in flat + outs)

    def body(index, *refs):
        ins, refs = list(refs[: len(flat)]), refs[len(flat) :]
        results, scratch, sems = refs[: len(outs)], refs[len(outs) : -1], refs[-1]
        copies = []
        for group, target in zip(groups, scratch):
            taken = [[ins.pop(0) for x in column] for column in group]
            copies += side_by_side(taken, target, sems, len(copies))
        for copy in copies:
            copy.start()
        for copy in copies:
            copy.wait()
        kernel(index, *scratch, *results)

    return pl.pallas_call(
        body,
        in_specs=[SMEM] + [pl.BlockSpec(memory_space=pl.ANY)] * len(flat),
        out_specs=[VMEM] * len(outs),
        out_shape=outs,
        scratch_shapes=[pltpu.VMEM(shape, BF) for shape in shapes]
        + [pltpu.SemaphoreType.DMA((len(flat),))],
        compiler_params=pltpu.CompilerParams(vmem_limit_bytes=2 * LIMIT),
        cost_estimate=pl.CostEstimate(flops=flops, bytes_accessed=moved, transcendentals=0),
        name=name,
    )(at.astype(jnp.int32).reshape(1), *flat)


def hidden_weights(net, second, grad_joined, gated, grads):
    length = sum(x.shape[0] for x in second)
    width, columns, hidden = second[0].shape[1], grad_joined[0].shape[1], gated[0].shape[1]
    rows, down = width // net.dp_n, hidden // net.dp_n
    pieces = width // columns

    def kernel(index, a, b, c, d, out):
        for n in range(net.dp_n):
            left = a[:, n * rows : (n + 1) * rows]
            out[n, :rows, :] = lax.dot_general(
                left, b[...], TN, preferred_element_type=F32
            ).astype(BF)
            left = c[:, n * down : (n + 1) * down]
            total = lax.dot_general(left, d[...], TN, preferred_element_type=F32).astype(BF)
            for p in range(pieces):
                start = rows + p * down
                out[n, start : start + down, :] = total[:, p * columns : (p + 1) * columns]

    return weight_call(
        kernel,
        [((net.dp_n, rows + pieces * down, columns), BF)],
        [[second], [grad_joined], [gated], [grads]],
        [(length, width), (length, columns), (length, hidden), (length, width)],
        net.dp,
        2 * length * width * (columns + hidden),
        "hidden_weights",
    )[0]


def mixed_weights(net, normed, grads):
    length, width = sum(x.shape[0] for x in normed), normed[0].shape[1]
    columns = sum(g.shape[1] for g in grads)
    chunk = width // net.dp_n // net.hi_n

    def kernel(index, a, b, mine, other):
        for n in range(net.dp_n * net.hi_n):
            left = a[:, n * chunk : (n + 1) * chunk]
            total = lax.dot_general(left, b[...], TN, preferred_element_type=F32)
            here = index[0] == n % net.hi_n

            @pl.when(here)
            def keep(n=n, total=total):
                mine[n // net.hi_n] = total

            @pl.when(jnp.logical_not(here))
            def send(n=n, total=total):
                other[n // net.hi_n] = total.astype(BF)

    shape = (net.dp_n, chunk, columns)
    return weight_call(
        kernel,
        [(shape, F32), (shape, BF)],
        [[normed], [[g] for g in grads]],
        [(length, width), (length, columns)],
        net.hi,
        2 * length * width * columns,
        "mixed_weights",
    )


def out_backward(net, gradient, total, middle, gain, matrix, arrived, rows_out):
    rows, width = gradient.shape
    count, heads = len(arrived), arrived[0].shape[1]
    groups = width // rows_out // count

    def kernel(index, g, t, mid, gn, m, *refs):
        ins, (new, gain_out), refs = refs[:count], refs[count : count + 2], refs[count + 2 :]
        leaving, shares, scratch = refs[:count], refs[count : 2 * count], refs[2 * count]
        x = mid[...]
        inverse = lax.rsqrt(jnp.mean(x * x, axis=-1, keepdims=True) + EPSILON)
        normal = x * inverse
        grad = t[...]
        gain_out[...] = jnp.sum(grad * normal, axis=0, keepdims=True)
        grad = grad * gn[...]
        grad = (grad - normal * jnp.mean(grad * normal, axis=-1, keepdims=True)) * inverse
        grad = g[...] + grad
        new[...] = grad
        branch = grad.astype(BF)
        for r in range(count):
            start = pl.multiple_of((index[0] ^ r) * heads, heads)
            leaving[r][...] = lax.dot_general(
                branch, m[pl.ds(start, heads), :], NT, preferred_element_type=F32
            ).astype(BF)
            block = lax.dot_general(ins[r][...], branch, TN, preferred_element_type=F32)
            scratch[pl.ds(pl.multiple_of(start // rows_out, heads // rows_out), heads // rows_out)] = (
                block.reshape(heads // rows_out, rows_out, width)
            )
        for r in range(count):
            for n in range(groups):
                shares[r][n] = scratch[n * count + (index[0] ^ r)].astype(BF)

    outs = on_chip(
        kernel,
        [((rows, width), F32), ((1, width), F32)]
        + [((rows, heads), BF)] * count
        + [((groups, rows_out, width), BF)] * count,
        gradient,
        total,
        middle,
        gain.reshape(1, width),
        matrix,
        *arrived,
        at=net.lo,
        scratch=[pltpu.VMEM((width // rows_out, rows_out, width), F32)],
        flops=4 * rows * matrix.size,
        name="out_backward",
    )
    return outs[0], outs[1][0], outs[2 : 2 + count], outs[2 + count :]


def mixed_backward(grads, matrix, rows):
    length = grads[0].shape[0]
    count = length // rows
    width = grads[0].shape[1]

    def kernel(q, k, v, m, *outs):
        for n, out in enumerate(outs):
            part = slice(n * rows, (n + 1) * rows)
            x = jnp.concatenate([q[part, :], k[part, :], v[part, :]], axis=1)
            out[...] = lax.dot_general(
                x, m[:, : 3 * width], NT, preferred_element_type=F32
            ).astype(BF)

    return on_chip(
        kernel,
        [((rows, matrix.shape[0]), BF)] * count,
        *grads,
        matrix,
        flops=2 * length * matrix.size,
        name="mixed_backward",
    )


def join_rows(blocks, index):
    rows = blocks[0].shape[0]
    if rows % 16:
        return in_order(blocks, index).reshape(-1, blocks[0].shape[1])

    def kernel(at, *refs):
        for r, block in enumerate(refs[:-1]):
            start = pl.multiple_of((at[0] ^ r) * rows, rows)
            refs[-1][pl.ds(start, rows), :] = block[...]

    shape = (rows * len(blocks), blocks[0].shape[1])
    return on_chip(kernel, [(shape, BF)], *blocks, at=index, name="join_rows")[0]


def join_middle(blocks, index, rows):
    n, stacked, c = blocks[0].shape
    count, pieces = len(blocks), stacked // rows
    if rows % 16:
        full = in_order(blocks, index).reshape(count, n, pieces, rows, c)
        return full.transpose(1, 0, 3, 2, 4).reshape(-1, pieces * c)

    def kernel(at, *refs):
        for r, block in enumerate(refs[:-1]):
            for i in range(n):
                start = pl.multiple_of((i * count + (at[0] ^ r)) * rows, rows)
                for p in range(pieces):
                    refs[-1][pl.ds(start, rows), p * c : (p + 1) * c] = block[
                        i, p * rows : (p + 1) * rows, :
                    ]

    shape = (n * count * rows, pieces * c)
    return on_chip(kernel, [(shape, BF)], *blocks, at=index, name="join_middle")[0]


def lane_ids():
    return lax.broadcasted_iota(jnp.int32, (1, LANES), 1)


def three_parts(x):
    hi = x.astype(BF).astype(F32)
    mid = (x - hi).astype(BF).astype(F32)
    return hi, mid, x - hi - mid


def group_sum(x, width):
    rows = lax.broadcasted_iota(jnp.int32, (LANES, LANES), 0) // width
    columns = lax.broadcasted_iota(jnp.int32, (LANES, LANES), 1) // width
    ones = jnp.where(rows == columns, 1.0, 0.0).astype(BF)
    return sum(dot(part.astype(BF), ones) for part in three_parts(x))


def swap_halves(x, half):
    front = (lane_ids() // half) % 2 == 0
    return jnp.where(front, pltpu.roll(x, LANES - half, 1), pltpu.roll(x, half, 1))


def head_prep(raw, gain, cosine, sine, width):
    raw = raw.astype(F32)
    inverse = lax.rsqrt(group_sum(raw * raw, width) * (1.0 / width) + EPSILON)
    scaled = raw * inverse * gain
    return scaled * cosine + swap_halves(scaled, width // 2) * sine, inverse


def attend_kernel(
    rows, query_in, key_in, value_in, cosine, sine, marks, gains, bias, attended, kept, tops
):
    length = query_in.shape[0]
    width = LANES // 2
    low = lane_ids() < width
    query, unused = head_prep(query_in[...], gains[0:1, :], cosine[...], sine[...], width)
    keys, unused = head_prep(key_in[...], gains[1:2, :], cosine[...], sine[...], width)
    query = query * (1.0 / math.sqrt(width))
    mark = marks[...].astype(F32)
    value = value_in[...].astype(F32)
    heads = []
    for h in range(2):
        shift = (lambda x: pltpu.roll(x, width, 1)) if h else (lambda x: x)
        heads.append(
            (
                jnp.where(low, shift(query), mark * bias[0, h : h + 1, :]).astype(BF),
                jnp.where(low, shift(keys), mark).astype(BF),
                jnp.where(low, shift(value), 1.0).astype(BF),
            )
        )
    best = [None, None]
    for start in range(0, length, rows):
        part = slice(start, start + rows)
        outs = []
        for h, (head_query, head_keys, head_value) in enumerate(heads):
            scores = lax.dot_general(head_query[part], head_keys, NT, preferred_element_type=F32)
            top = jnp.max(scores, axis=0, keepdims=True)
            best[h] = top if best[h] is None else jnp.maximum(best[h], top)
            mixed = dot(jnp.exp(scores).astype(BF), head_value)
            out = jnp.where(low, mixed / pltpu.roll(mixed, width, 1), jnp.log(mixed))
            kept[h, part, :] = out
            outs.append(out)
        attended[part, :] = jnp.where(low, outs[0], pltpu.roll(outs[1], width, 1)).astype(BF)
    for h in range(2):
        tops[h, :, :] = jnp.broadcast_to(jnp.max(best[h], axis=1, keepdims=True), (8, LANES))


def attend_backward_kernel(
    columns,
    query_in,
    key_in,
    value_in,
    grad_in,
    cosine,
    sine,
    marks,
    gains,
    bias,
    kept,
    grad_query,
    grad_key,
    grad_value,
    grad_gains,
    grad_bias,
    keys_turned,
    sum_keys,
    sum_values,
):
    length = query_in.shape[0]
    width = LANES // 2
    lane = lane_ids()
    low = lane < width
    scale = 1.0 / math.sqrt(width)
    query, query_inverse = head_prep(query_in[...], gains[0:1, :], cosine[...], sine[...], width)
    keys, key_inverse = head_prep(key_in[...], gains[1:2, :], cosine[...], sine[...], width)
    query = query * scale
    mark = marks[...].astype(F32)
    value = value_in[...].astype(F32)
    grads = grad_in[...].astype(F32)

    def place(x, first, other):
        for offset, part in enumerate(three_parts(x)):
            other = jnp.where(lane == first + offset, part, other)
        return other

    all_query, all_keys, all_values = [], [], []
    for h in range(2):
        shift = (lambda x: pltpu.roll(x, width, 1)) if h else (lambda x: x)
        out = kept[h]
        query_marks = place(-out, width + 12, mark * bias[0, h : h + 1, :])
        head_query = jnp.where(low, shift(query), query_marks).astype(BF)
        head_keys = jnp.where(low, shift(keys), mark).astype(BF)
        ones = jnp.where(lane < width + 3, 1.0, 0.0)
        head_value = jnp.where(low, shift(value), ones).astype(BF)
        head_grad = jnp.where(low, shift(grads), 0.0)
        inner = pltpu.roll(-group_sum(head_grad * out, width), width, 1)
        head_grad = place(inner, width, head_grad).astype(BF)
        keys_turned[...] = head_keys.astype(F32).T.astype(BF)
        turned = []
        for start in range(0, length, columns):
            part = slice(start, start + columns)
            scores = lax.dot_general(head_keys, head_query[part], NT, preferred_element_type=F32)
            probability = jnp.exp(scores)
            grad_prob = lax.dot_general(
                head_value, head_grad[part], NT, preferred_element_type=F32
            )
            grad_scores = (probability * grad_prob).astype(BF)
            part_values = dot(probability.astype(BF), head_grad[part])
            part_keys = dot(grad_scores, head_query[part])
            if start:
                sum_values[...] += part_values
                sum_keys[...] += part_keys
            else:
                sum_values[...] = part_values
                sum_keys[...] = part_keys
            turned.append(dot(keys_turned[...], grad_scores).T)
        head_sum = jnp.concatenate(turned, axis=0)
        equal = jnp.where((lane >= width) & (lane < width + 4), mark, 0.0)
        match = jnp.sum(jnp.sum(head_sum * equal, axis=0, keepdims=True), axis=1, keepdims=True)
        total = jnp.sum(
            jnp.where(lane == width + 12, jnp.sum(head_sum, axis=0, keepdims=True), 0.0),
            axis=1,
            keepdims=True,
        )
        both = jnp.where(lane == 0, match, total - match)
        grad_bias[h, :, :] = jnp.broadcast_to(both, (8, LANES))
        all_query.append(head_sum * scale)
        all_keys.append(sum_keys[...])
        all_values.append(sum_values[...])

    def join(pair):
        return jnp.where(low, pair[0], pltpu.roll(pair[1], width, 1))

    grad_value[...] = join(all_values).astype(BF)
    for n, (pair, raw, inverse, out) in enumerate(
        (
            (all_query, query_in, query_inverse, grad_query),
            (all_keys, key_in, key_inverse, grad_key),
        )
    ):
        grad = join(pair)
        grad = grad * cosine[...] - swap_halves(grad, width // 2) * sine[...]
        normal = raw[...].astype(F32) * inverse
        grad_gains[0, n : n + 1, :] = jnp.sum(grad * normal, axis=0, keepdims=True)
        grad = grad * gains[n : n + 1, :]
        mean = group_sum(grad * normal, width) * (1.0 / width)
        out[...] = ((grad - normal * mean) * inverse).astype(BF)


def lane_block(length, offset):
    return pl.BlockSpec((length, LANES), lambda i: (0, offset + i))


def whole_block(shape):
    return pl.BlockSpec(shape, lambda i: (0,) * len(shape))


def attend(mixed, tables, gains, bias):
    length, heads = mixed.shape[0], bias.shape[0]
    pairs = heads // 2
    block = lane_block
    return pl.pallas_call(
        functools.partial(attend_kernel, min(256, length)),
        grid=(pairs,),
        in_specs=[
            block(length, 0),
            block(length, pairs),
            block(length, 2 * pairs),
            whole_block((length, LANES)),
            whole_block((length, LANES)),
            whole_block((length, LANES)),
            whole_block((2, LANES)),
            pl.BlockSpec((1, 2, LANES), lambda i: (i, 0, 0)),
        ],
        out_specs=[
            block(length, 0),
            pl.BlockSpec((2, length, LANES), lambda i: (i, 0, 0)),
            pl.BlockSpec((2, 8, LANES), lambda i: (i, 0, 0)),
        ],
        out_shape=[
            jax.ShapeDtypeStruct((length, pairs * LANES), BF),
            jax.ShapeDtypeStruct((heads, length, LANES), F32),
            jax.ShapeDtypeStruct((heads, 8, LANES), F32),
        ],
        compiler_params=pltpu.CompilerParams(vmem_limit_bytes=48 * 2**20),
        cost_estimate=pl.CostEstimate(
            flops=8 * heads * length * length * LANES,
            bytes_accessed=16 * length * pairs * LANES,
            transcendentals=heads * length * length,
        ),
        name="attend",
    )(mixed, mixed, mixed, *tables, gains, bias.reshape(pairs, 2, LANES))


def attend_backward(mixed, grad, tables, gains, bias, kept):
    length, heads = mixed.shape[0], bias.shape[0]
    pairs = heads // 2
    block = lane_block
    flat = jax.ShapeDtypeStruct((length, pairs * LANES), BF)
    return pl.pallas_call(
        functools.partial(attend_backward_kernel, min(256, length)),
        grid=(pairs,),
        in_specs=[
            block(length, 0),
            block(length, pairs),
            block(length, 2 * pairs),
            block(length, 0),
            whole_block((length, LANES)),
            whole_block((length, LANES)),
            whole_block((length, LANES)),
            whole_block((2, LANES)),
            pl.BlockSpec((1, 2, LANES), lambda i: (i, 0, 0)),
            pl.BlockSpec((2, length, LANES), lambda i: (i, 0, 0)),
        ],
        out_specs=[
            block(length, 0),
            block(length, 0),
            block(length, 0),
            pl.BlockSpec((1, 2, LANES), lambda i: (i, 0, 0)),
            pl.BlockSpec((2, 8, LANES), lambda i: (i, 0, 0)),
        ],
        out_shape=[
            flat,
            flat,
            flat,
            jax.ShapeDtypeStruct((pairs, 2, LANES), F32),
            jax.ShapeDtypeStruct((heads, 8, LANES), F32),
        ],
        scratch_shapes=[
            pltpu.VMEM((LANES, length), BF),
            pltpu.VMEM((length, LANES), F32),
            pltpu.VMEM((length, LANES), F32),
        ],
        compiler_params=pltpu.CompilerParams(vmem_limit_bytes=56 * 2**20),
        cost_estimate=pl.CostEstimate(
            flops=20 * heads * length * length * LANES,
            bytes_accessed=24 * length * pairs * LANES,
            transcendentals=heads * length * length,
        ),
        name="attend_backward",
    )(mixed, mixed, mixed, grad, *tables, gains, bias.reshape(pairs, 2, LANES), kept)


def head_tables(ids, places, width):
    frequency = jnp.exp(jnp.arange(width // 2, dtype=F32) * (-2.0 * math.log(10000.0) / width))
    angles = places.astype(F32)[:, None] * frequency
    cosine, sine = jnp.cos(angles), jnp.sin(angles)
    lane = jnp.arange(LANES)[None, :]
    equal = (ids[:, None] == (lane - width) % 4) & (lane >= width) & (lane < width + 12)
    plain = (lane >= width + 12) & (lane < width + 15)
    return (
        jnp.concatenate([cosine] * 4, axis=1),
        jnp.concatenate([-sine, sine, -sine, sine], axis=1),
        (equal | plain).astype(BF),
    )


def bias_marks(pair, width):
    gap = pair[0] - pair[1]
    hi = lax.reduce_precision(gap, 8, 7)
    mid = lax.reduce_precision(gap - hi, 8, 7)
    lane = jnp.arange(LANES)[None, :]
    marks = jnp.zeros((pair.shape[1], LANES), F32)
    for n, part in enumerate((hi, mid, gap - hi - mid)):
        inside = (lane >= width + 4 * n) & (lane < width + 4 * n + 4)
        marks = jnp.where(inside, part[:, None], marks)
    return marks


def stages(blocks):
    count = len(blocks)
    cuts = [0, 2, 6, 8] if count == 8 else [0, count // 2, count]
    return [blocks[a:b] for a, b in zip(cuts, cuts[1:])]


def shards(
    tokens,
    variate_ids,
    time_ids,
    w_qkv,
    w_out,
    w_in,
    w_down,
    norm_gains,
    qk_gains,
    head_bias,
    cotangent,
):
    sequences, tok_dev, width = tokens.shape
    layers = w_qkv.shape[0]
    heads = head_bias.shape[2]
    head_size = qk_gains.shape[2]
    net = Net()
    lo_n, lo_bits, seq_bits = net.lo_n, net.lo_bits, net.seq_bits
    rows = sequences * tok_dev
    local_heads = heads // lo_n
    local_width = local_heads * head_size
    head_start = net.lo * local_heads
    unit = w_down.shape[1]
    rows_out = w_out.shape[1]

    def to_groups(x):
        return jnp.concatenate(
            net.trade_hi([pick(x, net.hi ^ q) for q in range(sequences)]), axis=0
        )

    def to_devices(x):
        return in_order(net.trade_hi(jnp.split(x, sequences, axis=0)), net.hi)

    state = to_groups(tokens).astype(F32)
    own_qkv = trade_columns(net, w_qkv[0], lo_bits, local_width)
    own_in = trade_columns(net, after(w_in[0], own_qkv), seq_bits, unit)
    weights = []
    for layer in range(layers):
        m_qkv, m_out = fetch_attention(net, own_qkv, w_out[layer])
        weights.append((m_qkv, m_out, fetch_hidden(net, own_in, w_down[layer])))
        if layer + 1 < layers:
            own_qkv = trade_columns(net, after(w_qkv[layer + 1], own_in), lo_bits, local_width)
            own_in = trade_columns(net, after(w_in[layer + 1], own_qkv), seq_bits, unit)

    pair = to_groups(jnp.stack([variate_ids, time_ids], axis=-1))
    pair = jnp.concatenate(net.gather(pair, lo_bits), axis=0)
    tables = head_tables(pair[:, 0], pair[:, 1], head_size)

    saved = []
    best_scores = jnp.full((layers, heads), FLOOR_VALUE, F32)
    for layer in range(layers):
        m_qkv, m_out, pack = weights[layer]
        layer_in = state
        normed = rms_scale(layer_in, norm_gains[layer, 0]).astype(BF)
        normed = net.gather(normed, lo_bits)
        mixed = project(normed, m_qkv, 3 * local_width)
        bias_pair = lax.dynamic_slice_in_dim(head_bias[layer], head_start, local_heads, 1)
        gains = jnp.concatenate([qk_gains[layer]] * 2, axis=1)
        bias = bias_marks(bias_pair, head_size)
        attended, kept, head_tops = attend(mixed, tables, gains, bias)
        head_tops = head_tops[:, 0, 0] + bias_pair[1]
        best_scores = lax.dynamic_update_slice(
            best_scores, head_tops[None, :], (jnp.int32(layer), head_start)
        )
        arrived = net.trade(jnp.split(attended, lo_n, axis=0), lo_bits)
        middle, second = out_project(layer_in, arrived, m_out, norm_gains[layer, 1], net.lo)
        second = net.gather(second, seq_bits)
        joined, partial = [], []
        for part in stages(second):
            joined_part, out = feed_forward(part, pack)
            joined.append(joined_part)
            partial += out
        state = middle + net.scatter(partial, seq_bits)
        saved.append((layer_in, normed, mixed, gains, bias, kept, arrived, middle, second, joined))
    layer_out = to_devices(state.astype(BF))

    gradient = to_groups(cotangent).astype(F32)
    qkv_parts = [None] * layers
    out_parts = [None] * layers
    in_parts = [None] * layers
    down_parts = [None] * layers
    norm_parts = [None] * layers
    qk_parts = [None] * layers
    bias_parts = [None] * layers
    for layer in reversed(range(layers)):
        m_qkv, m_out, pack = weights[layer]
        layer_in, normed, mixed, gains, bias, kept, arrived, middle, second, joined = saved[layer]
        down_in = net.gather(gradient.astype(BF), seq_bits)
        grad_joined, gated, partial = [], [], []
        for part, joined_part in zip(stages(down_in), joined):
            grad_part, gated_part, out = feed_backward(part, joined_part, pack)
            grad_joined.append(grad_part)
            gated.append(gated_part)
            partial += out
        grad_second = net.scatter(partial, seq_bits)
        grad_hidden = hidden_weights(net, second, grad_joined, gated, down_in)
        own_in, down_parts[layer] = scatter_hidden(net, grad_hidden, width // net.dp_n)
        in_parts[layer] = restore_columns(net, own_in, seq_bits, unit)
        gradient, gain_second, leaving, shares = out_backward(
            net, gradient, grad_second, middle, norm_gains[layer, 1], m_out, arrived, rows_out
        )
        grad_out = net.scatter(shares, lo_bits)
        grad_out = grad_out.reshape((net.dp_n, net.hi_n) + grad_out.shape[1:])
        out_parts[layer] = net.scatter_rows(pick(grad_out, net.hi, 1), pick(grad_out, 1 - net.hi, 1))
        grad_heads = jnp.concatenate(net.trade(leaving, lo_bits), axis=0)
        grad_query, grad_keys, grad_values, grad_gains, grad_pair = attend_backward(
            mixed, grad_heads, tables, gains, bias, kept
        )
        grads = [grad_query, grad_keys, grad_values]
        grad_normed = net.scatter(mixed_backward(grads, m_qkv, rows), lo_bits)
        own_qkv = net.scatter_rows(*mixed_weights(net, normed, grads))
        qkv_parts[layer] = restore_columns(net, own_qkv, lo_bits, local_width)
        unused, first_pull = jax.vjp(rms_scale, layer_in, norm_gains[layer, 0])
        grad_layer_in, gain_first = first_pull(grad_normed)
        gradient = gradient + grad_layer_in
        norm_parts[layer] = jnp.stack([gain_first, gain_second])
        qk_parts[layer] = grad_gains.reshape(-1, 2, 2, head_size).sum(axis=(0, 2))
        bias_parts[layer] = lax.dynamic_update_slice(
            jnp.zeros((2, heads), F32), grad_pair[:, 0, :2].T, (jnp.int32(0), head_start)
        )
    input_grad = to_devices(gradient.astype(BF)).astype(F32)
    tops = best_scores.size
    small = jnp.concatenate(
        [best_scores.reshape(-1)]
        + [jnp.stack(part).reshape(-1) for part in (norm_parts, qk_parts, bias_parts)]
    )
    is_top = jnp.arange(small.size) < tops
    small = net.all_small(small, lambda a, b: jnp.where(is_top, jnp.maximum(a, b), a + b))
    best_scores = small[:tops].reshape(best_scores.shape)
    small = small[tops:]
    cut_norm, cut_qk = norm_gains.size, norm_gains.size + qk_gains.size
    norm_sum = small[:cut_norm].reshape(norm_gains.shape)
    qk_sum = small[cut_norm:cut_qk].reshape(qk_gains.shape)
    bias_sum = small[cut_qk:].reshape(head_bias.shape)

    factor = jnp.sqrt(CLIP_LIMIT / jnp.maximum(best_scores, CLIP_LIMIT))
    spread = jnp.repeat(factor, head_size, axis=1)
    column_scale = jnp.concatenate([spread, spread, jnp.ones((layers, width), F32)], axis=1)
    clipped = (w_qkv.astype(F32) * column_scale[:, None, :]).astype(BF)
    return (
        layer_out,
        input_grad,
        jnp.stack(qkv_parts),
        jnp.stack(out_parts),
        jnp.stack(in_parts),
        jnp.stack(down_parts),
        norm_sum,
        qk_sum,
        bias_sum,
        clipped,
        best_scores,
    )


def solution(mesh):
    def program(*arrays):
        dp_n = mesh.shape["dp"]
        sequences = arrays[0].shape[0] // dp_n
        split = Mesh(mesh.devices.reshape(dp_n, sequences, -1), ("dp", "hi", "lo"))
        seq = ("hi", "lo")
        tokens_spec = P("dp", seq, None)
        rows_spec = P(None, ("dp",) + seq, None)
        ids_spec = P("dp", seq)
        in_specs = (tokens_spec, ids_spec, ids_spec) + (rows_spec,) * 4 + (P(),) * 3
        in_specs += (tokens_spec,)
        out_specs = (tokens_spec,) * 2 + (rows_spec,) * 4 + (P(),) * 3 + (rows_spec, P())
        run = jax.shard_map(
            shards, mesh=split, in_specs=in_specs, out_specs=out_specs, check_vma=False
        )
        return run(*arrays)

    return program
```

time: 1100 us -> 770 us (0.70)
  Pallas kernels: 0 us -> 180 us
  matrix products: 179 us -> 0 us
  local copies, waits for them, and re-layouts: 252 us -> 98.2 us
  waiting for transfers between devices: 392 us -> 260 us
  other arithmetic: 101 us -> 70.5 us
  loops' own time: 16.6 us -> 0 us
  between operations: 5.65 us -> 17.7 us
    pallas_call x0 -> x44, Pallas kernels: none -> 180 us  [the longest x26 70.3 us: on_chip(): pl.pallas_call(kernel, in_specs=[SMEM] * len(first) + [VMEM] * len(arrays...]
    dot_general x64 -> x0, matrix products: 179 us -> none  [the longest x14 42 us: dot_nt(): lax.dot_general(a, b, (((1,), (1,)), ((), ())), preferred_element_type=F32)]
    ppermute x150 -> x159, waiting for transfers between devices: 241 us -> 159 us  [the longest x121 89.1 us: swap(): return lax.ppermute(x, 'lo', [(i, i ^ bit) for i in range(self.lo_n)])]
    dynamic_update_slice x58 -> x2, local copies, waits for them, and re-layouts: 80.7 us -> 0.29 us  [shards(): lax.dynamic_update_slice(jnp.zeros((2, heads), F32), grad_pair[:, 0, :2]....]
    ppermute x48 -> x18, waiting for transfers between devices: 143 us -> 98.6 us  [next_dp(): lax.ppermute(x, 'dp', [(i, (i + 1) % self.dp_n) for i in range(self.dp_n)])]
    dynamic_update_slice x64 -> x14, local copies, waits for them, and re-layouts: 33.7 us -> 7.71 us  [gather_rows(): full = lax.dynamic_update_slice(full, block[None, None], start)]
    dynamic_slice x29 -> x0, local copies, waits for them, and re-layouts: 19.5 us -> none  [the longest x7 13.7 us: pick(): return lax.dynamic_index_in_dim(array, index, axis, keepdims=False)]
    another operation x40 -> x0, local copies, waits for them, and re-layouts: 18.9 us -> none
  transfers between devices with their start and end apart: 202 -> 183, of which waited for: 80 -> 61; matrix products, arithmetic and copies ran while one was open for 44% -> 16% of each run, Pallas kernels for 0% -> 23%
where the time goes in v2:
time: 770 us; the launch traced here: 760 us
  waiting for transfers between devices  260 us (34%)
  Pallas kernels  180 us (23%)
  starting transfers between devices  133 us (17%)
  local copies, waits for them, and re-layouts  98.2 us (13%)
  other arithmetic  70.5 us (9%)
  between operations  17.7 us (2%)
    ppermute x18, waiting for transfers between devices, next_dp(): lax.ppermute(x, 'dp', [(i, (i + 1) % self.dp_n) for i in range(self.dp_n)])  98.6 us
    ppermute x121, waiting for transfers between devices, swap(): return lax.ppermute(x, 'lo', [(i, i ^ bit) for i in range(self.lo_n)])  89.1 us
    pallas_call x26, Pallas kernels, on_chip(): pl.pallas_call(kernel, in_specs=[SMEM] * len(first) + [VMEM] * len(arrays...  70.3 us
    ppermute x38, waiting for transfers between devices, swap(): return lax.ppermute(x, 'hi', [(i, i ^ bit) for i in range(self.hi_n)])  69.5 us
    ppermute x121, starting transfers between devices, swap(): return lax.ppermute(x, 'lo', [(i, i ^ bit) for i in range(self.lo_n)])  56.1 us
    unnamed x449, local copies, waits for them, and re-layouts  48.7 us
    ppermute x38, starting transfers between devices, swap(): return lax.ppermute(x, 'hi', [(i, i ^ bit) for i in range(self.hi_n)])  48.3 us
    pallas_call x2, Pallas kernels, attend_backward(): pl.pallas_call(functools.partial(attend_backward_kernel, min(256, length)...  38.1 us
  transfers between devices with their start and end apart: 183, of which 61 were waited for; matrix products, arithmetic and copies ran while one was open for 16% of the time, Pallas kernels for 23%

profile of v2, /device:TPU:0, one launch (start us, length us, event | category | flops | bytes accessed | tf_op | source)
XLA Modules:
  0.0 759.6 jit_solution(10251745745047112338)
XLA Ops:
  55.9 5.2 collective-permute-done.5
  64.6 14.2 %collective-permute-done.7 = bf16[128,1024]{1,0:T(8,128)(2,1)} collective-permute-done((bf16[128,1024]{1,0:T(8,128)(2,1)}, bf16[128,1024]{1,0:T(8,128)(2,1)}, u32[]{:S(2)}, u32[]{:S(2)}) %collective-permute-start.7) | collective-permute-done | bytes 262176 | tf_op jit(solution)/shard_map/ppermute | solution.py:62
  83.7 13.2 %collective-permute-done.9 = bf16[128,1024]{1,0:T(8,128)(2,1)} collective-permute-done((bf16[128,1024]{1,0:T(8,128)(2,1)}, bf16[128,1024]{1,0:T(8,128)(2,1)}, u32[]{:S(2)}, u32[]{:S(2)}) %collective-permute-start.9) | collective-permute-done | bytes 262176 | tf_op jit(solution)/shard_map/ppermute | solution.py:62
  107.7 8.1 %attend.2 = (bf16[1024,256]{1,0:T(8,128)(2,1)S(1)}, f32[4,1024,128]{2,1,0:T(8,128)S(1)}, f32[4,8,128]{2,1,0:T(8,128)S(1)}) custom-call(bf16[1024,768]{1,0:T(8,128)(2,1)S(1)} %project.2.query_in.key_in.value_in, bf16[1024,768]{1,0:T(8,128)(2,1)S(1)} %project.2.query_in.key_in.value_in, bf16[1024,768]{1,0:T(8,128)(2,1)S(1)} %project.2.query_in.key_in.value_in, ...), custom_call_target="tpu_custom_call" | custom-call | flops 4294967296 | bytes 4194304 | tf_op jit(solution)/shard_map/attend/pallas_call | solution.py:805
  134.7 13.6 %collective-permute-done.67 = bf16[128,1024]{1,0:T(8,128)(2,1)S(1)} collective-permute-done((bf16[128,1024]{1,0:T(8,128)(2,1)S(1)}, bf16[128,1024]{1,0:T(8,128)(2,1)S(1)}, u32[]{:S(2)}, u32[]{:S(2)}) %collective-permute-start.67) | collective-permute-done | bytes 262176 | tf_op jit(solution)/shard_map/ppermute | solution.py:53
  157.1 7.1 collective-permute-done.38
  172.3 5.8 feed_forward.7
  200.3 5.9 collective-permute-done.44
  219.6 10.4 %collective-permute-done.50 = bf16[128,1024]{1,0:T(8,128)(2,1)} collective-permute-done((bf16[128,1024]{1,0:T(8,128)(2,1)S(1)}, bf16[128,1024]{1,0:T(8,128)(2,1)}, u32[]{:S(2)}, u32[]{:S(2)}) %collective-permute-start.50) | collective-permute-done | bytes 262176 | tf_op jit(solution)/shard_map/ppermute | solution.py:62
  233.5 5.0 collective-permute-start.52
  243.7 9.7 %collective-permute-done.52 = bf16[128,1024]{1,0:T(8,128)(2,1)S(1)} collective-permute-done((bf16[128,1024]{1,0:T(8,128)(2,1)}, bf16[128,1024]{1,0:T(8,128)(2,1)S(1)}, u32[]{:S(2)}, u32[]{:S(2)}) %collective-permute-start.52) | collective-permute-done | bytes 262176 | tf_op jit(solution)/shard_map/ppermute | solution.py:62
  254.8 6.4 collective-permute-start.54
  261.3 11.6 %collective-permute-done.54 = bf16[128,1024]{1,0:T(8,128)(2,1)S(1)} collective-permute-done((bf16[128,1024]{1,0:T(8,128)(2,1)S(1)}, bf16[128,1024]{1,0:T(8,128)(2,1)S(1)}, u32[]{:S(2)}, u32[]{:S(2)}) %collective-permute-start.54) | collective-permute-done | bytes 262176 | tf_op jit(solution)/shard_map/ppermute | solution.py:62
  283.7 7.7 %attend.3 = (bf16[1024,256]{1,0:T(8,128)(2,1)S(1)}, f32[4,1024,128]{2,1,0:T(8,128)S(1)}, f32[4,8,128]{2,1,0:T(8,128)S(1)}) custom-call(bf16[1024,768]{1,0:T(8,128)(2,1)S(1)} %project.3.query_in.key_in.value_in, bf16[1024,768]{1,0:T(8,128)(2,1)S(1)} %project.3.query_in.key_in.value_in, bf16[1024,768]{1,0:T(8,128)(2,1)S(1)} %project.3.query_in.key_in.value_in, ...), custom_call_target="tpu_custom_call" | custom-call | flops 4294967296 | bytes 4194304 | tf_op jit(solution)/shard_map/attend/pallas_call | solution.py:805
  317.1 8.1 %collective-permute-done.73.refs_0_.refs_2_ = bf16[256,1024]{1,0:T(8,128)(2,1)} collective-permute-done((bf16[256,1024]{1,0:T(8,128)(2,1)}, bf16[256,1024]{1,0:T(8,128)(2,1)}, u32[]{:S(2)}, u32[]{:S(2)}) %collective-permute-start.73) | collective-permute-done | bytes 524320 | tf_op jit(solution)/shard_map/ppermute | solution.py:51
  345.6 5.3 feed_forward.10
  351.5 5.6 feed_backward.7
  370.0 5.7 collective-permute-done.85
  391.1 14.5 %collective-permute-done.104 = bf16[256,1024]{1,0:T(8,128)(2,1)} collective-permute-done((bf16[256,1024]{1,0:T(8,128)(2,1)}, bf16[256,1024]{1,0:T(8,128)(2,1)}, u32[]{:S(2)}, u32[]{:S(2)}) %collective-permute-start.104) | collective-permute-done | bytes 524320 | tf_op jit(solution)/shard_map/ppermute | solution.py:53
  423.4 19.1 %attend_backward.2 = (bf16[1024,256]{1,0:T(8,128)(2,1)}, bf16[1024,256]{1,0:T(8,128)(2,1)}, bf16[1024,256]{1,0:T(8,128)(2,1)}, f32[2,2,128]{2,1,0:T(2,128)}, f32[4,8,128]{2,1,0:T(8,128)}) custom-call(bf16[1024,768]{1,0:T(8,128)(2,1)} %copy-done.122, bf16[1024,768]{1,0:T(8,128)(2,1)} %copy-done.122, bf16[1024,768]{1,0:T(8,128)(2,1)} %copy-done.122, ...), custom_call_target="tpu_custom_call" | custom-call | flops 10737418240 | bytes 6291456 | tf_op jit(solution)/shard_map/attend_backward/pallas_call | solution.py:843
  450.1 13.3 %hidden_weights.3 = bf16[4,384,1024]{2,1,0:T(8,128)(2,1)} custom-call(s32[1]{0:T(128)} %bitcast.90.index, bf16[256,1024]{1,0:T(8,128)(2,1)} %get-tuple-element.191.refs_0_, bf16[256,1024]{1,0:T(8,128)(2,1)} %collective-permute-done.65.refs_1_, bf16[256,1024]{1,0:T(8,128)(2,1)} %collective-permute-done.73.refs_0_.refs_2_, ...), custom_call_target="tpu_custom_call" | custom-call | flops 6442450944 | bytes 17825792 | tf_op jit(solution)/shard_map/hidden_weights/pallas_call | solution.py:444
  472.4 5.1 mixed_weights.3
  485.2 8.0 %collective-permute-done.110 = bf16[256,1024]{1,0:T(8,128)(2,1)} collective-permute-done((bf16[256,1024]{1,0:T(8,128)(2,1)}, bf16[256,1024]{1,0:T(8,128)(2,1)}, u32[]{:S(2)}, u32[]{:S(2)}) %collective-permute-start.110) | collective-permute-done | bytes 524320 | tf_op jit(solution)/shard_map/ppermute | solution.py:51
  523.2 7.2 collective-permute-done.160
  550.1 5.0 collective-permute-done.125
  560.6 7.6 %collective-permute-done.126 = bf16[256,1024]{1,0:T(8,128)(2,1)S(1)} collective-permute-done((bf16[256,1024]{1,0:T(8,128)(2,1)S(1)}, bf16[256,1024]{1,0:T(8,128)(2,1)S(1)}, u32[]{:S(2)}, u32[]{:S(2)}) %collective-permute-start.126) | collective-permute-done | bytes 524320 | tf_op jit(solution)/shard_map/ppermute | solution.py:53
  587.3 13.0 %hidden_weights.2 = bf16[4,384,1024]{2,1,0:T(8,128)(2,1)} custom-call(s32[1]{0:T(128)} %bitcast.90.index, bf16[256,1024]{1,0:T(8,128)(2,1)} %get-tuple-element.159.refs_0_, bf16[256,1024]{1,0:T(8,128)(2,1)} %collective-permute-done.24.refs_1_, bf16[256,1024]{1,0:T(8,128)(2,1)S(1)} %copy-done.53, bf16[256,1024]{1,0:T(8,128)(2,1)S(1)} %copy-done.84, ...), custom_call_target="tpu_custom_call" | custom-call | flops 6442450944 | bytes 17825792 | tf_op jit(solution)/shard_map/hidden_weights/pallas_call | solution.py:444
  602.7 19.1 %attend_backward.3 = (bf16[1024,256]{1,0:T(8,128)(2,1)}, bf16[1024,256]{1,0:T(8,128)(2,1)}, bf16[1024,256]{1,0:T(8,128)(2,1)}, f32[2,2,128]{2,1,0:T(2,128)}, f32[4,8,128]{2,1,0:T(8,128)}) custom-call(bf16[1024,768]{1,0:T(8,128)(2,1)} %copy-done.121, bf16[1024,768]{1,0:T(8,128)(2,1)} %copy-done.121, bf16[1024,768]{1,0:T(8,128)(2,1)} %copy-done.121, ...), custom_call_target="tpu_custom_call" | custom-call | flops 10737418240 | bytes 6291456 | tf_op jit(solution)/shard_map/attend_backward/pallas_call | solution.py:843
  628.9 6.5 mixed_weights.2
  646.9 7.8 %collective-permute-done.150 = bf16[8,32,1024]{2,1,0:T(8,128)(2,1)} collective-permute-done((bf16[8,32,1024]{2,1,0:T(8,128)(2,1)}, bf16[8,32,1024]{2,1,0:T(8,128)(2,1)}, u32[]{:S(2)}, u32[]{:S(2)}) %collective-permute-start.150) | collective-permute-done | bytes 524320 | tf_op jit(solution)/shard_map/ppermute | solution.py:51
  675.3 7.4 collective-permute-done.135
  683.4 5.3 collective-permute-done.153
  (1092 shorter events, 454.6 us)
Async XLA Ops:
  7.3 161.1 %all-gather.5.cloned.1.call-start = ((), (), s32[]{:S(2)}) async-start(), calls=%async_computation.4 | async-start | bytes 3932160 | tf_op jit(solution)/shard_map/all_gather | solution.py:265
  9.2 37.5 %collective-permute-start = (bf16[128,1024]{1,0:T(8,128)(2,1)}, bf16[128,1024]{1,0:T(8,128)(2,1)S(1)}, u32[]{:S(2)}, u32[]{:S(2)}) collective-permute-start(bf16[128,1024]{1,0:T(8,128)(2,1)} %get-tuple-element.342), channel_id=1, source_target_pairs={{0,4},{4,0},{1,5},{5,1},{2,6},{6,2},{3,7},{7,3},{8,12},{12,8},{9,1... | collective-permute-start | bytes 786440 | tf_op jit(solution)/shard_map/ppermute | solution.py:53
  53.2 276.6 %all-gather.7.cloned.1.call-start = ((), (), s32[]{:S(2)}) async-start(), calls=%async_computation.5 | async-start | bytes 3932160 | tf_op jit(solution)/shard_map/all_gather | solution.py:265
  55.3 48.3 %collective-permute-start.14 = (bf16[256,1024]{1,0:T(8,128)(2,1)}, bf16[256,1024]{1,0:T(8,128)(2,1)}, u32[]{:S(2)}, u32[]{:S(2)}) collective-permute-start(bf16[256,1024]{1,0:T(8,128)(2,1)} %multiply_convert_fusion.1.refs_0_), channel_id=1, source_target_pairs={{0,1},{1,0},{2,3},{3,2},{4,5},{5,4},{6,7},{7,6},{8,9},{9,8},{10,11... | collective-permute-start | bytes 1572872 | tf_op jit(solution)/shard_map/ppermute | solution.py:51
  55.3 28.3 %collective-permute-start.15 = (bf16[256,1024]{1,0:T(8,128)(2,1)}, bf16[256,1024]{1,0:T(8,128)(2,1)}, u32[]{:S(2)}, u32[]{:S(2)}) collective-permute-start(bf16[256,1024]{1,0:T(8,128)(2,1)} %multiply_convert_fusion.1.refs_0_), channel_id=1, source_target_pairs={{0,2},{1,3},{2,0},{3,1},{4,6},{5,7},{6,4},{7,5},{8,10},{9,11},{10,... | collective-permute-start | bytes 1572872 | tf_op jit(solution)/shard_map/ppermute | solution.py:51
  156.4 23.8 %collective-permute-start.66 = (bf16[32,1024]{1,0:T(8,128)(2,1)}, bf16[32,1024]{1,0:T(8,128)(2,1)S(1)}, u32[]{:S(2)}, u32[]{:S(2)}) collective-permute-start(bf16[32,1024]{1,0:T(8,128)(2,1)} %get-tuple-element.194), channel_id=1, source_target_pairs={{0,1},{1,0},{2,3},{3,2},{4,5},{5,4},{6,7},{7,6},{8,9},{9,8},{10,11... | collective-permute-start | bytes 196616 | tf_op jit(solution)/shard_map/ppermute | solution.py:51
  181.6 33.5 %collective-permute-start.88 = (bf16[128,1024]{1,0:T(8,128)(2,1)}, bf16[128,1024]{1,0:T(8,128)(2,1)}, u32[]{:S(2)}, u32[]{:S(2)}) collective-permute-start(bf16[128,1024]{1,0:T(8,128)(2,1)} %get-tuple-element.326), channel_id=1, source_target_pairs={{0,4},{4,0},{1,5},{5,1},{2,6},{6,2},{3,7},{7,3},{8,12},{12,8},{9,1... | collective-permute-start | bytes 786440 | tf_op jit(solution)/shard_map/ppermute | solution.py:53
  188.2 454.9 %reduce-scatter.5.cloned.1.call-start = ((), (), s32[]{:S(2)}) async-start(), calls=%async_computation.3 | async-start | bytes 3932160 | tf_op jit(solution)/shard_map/reduce_scatter | solution.py:269
  194.7 38.8 %collective-permute-start.31 = (bf16[256,1024]{1,0:T(8,128)(2,1)}, bf16[256,1024]{1,0:T(8,128)(2,1)}, u32[]{:S(2)}, u32[]{:S(2)}) collective-permute-start(bf16[256,1024]{1,0:T(8,128)(2,1)} %get-tuple-element.170), channel_id=1, source_target_pairs={{0,1},{1,0},{2,3},{3,2},{4,5},{5,4},{6,7},{7,6},{8,9},{9,8},{10,11... | collective-permute-start | bytes 1572872 | tf_op jit(solution)/shard_map/ppermute | solution.py:51
  207.1 31.5 %collective-permute-start.45 = (bf16[256,1024]{1,0:T(8,128)(2,1)}, bf16[256,1024]{1,0:T(8,128)(2,1)S(1)}, u32[]{:S(2)}, u32[]{:S(2)}) collective-permute-start(bf16[256,1024]{1,0:T(8,128)(2,1)} %pad_maximum_fusion.8), channel_id=1, source_target_pairs={{0,4},{4,0},{1,5},{5,1},{2,6},{6,2},{3,7},{7,3},{8,12},{12,8},{9,1... | collective-permute-start | bytes 1572872 | tf_op jit(solution)/shard_map/ppermute | solution.py:53
  209.6 29.7 %collective-permute-start.42 = (bf16[256,1024]{1,0:T(8,128)(2,1)}, bf16[256,1024]{1,0:T(8,128)(2,1)}, u32[]{:S(2)}, u32[]{:S(2)}) collective-permute-start(bf16[256,1024]{1,0:T(8,128)(2,1)} %pad_maximum_fusion.7), channel_id=1, source_target_pairs={{0,2},{1,3},{2,0},{3,1},{4,6},{5,7},{6,4},{7,5},{8,10},{9,11},{10,... | collective-permute-start | bytes 1572872 | tf_op jit(solution)/shard_map/ppermute | solution.py:51
  230.0 63.7 %collective-permute-start.91 = (bf16[256,1024]{1,0:T(8,128)(2,1)}, bf16[256,1024]{1,0:T(8,128)(2,1)S(1)}, u32[]{:S(2)}, u32[]{:S(2)}) collective-permute-start(bf16[256,1024]{1,0:T(8,128)(2,1)} %get-tuple-element.323.refs_0_.refs_14_), channel_id=1, source_target_pairs={{0,2},{1,3},{2,0},{3,1},{4,6},{5,7},{6,4},{7,5},{8,10},{9,11},{10,... | collective-permute-start | bytes 1572872 | tf_op jit(solution)/shard_map/ppermute | solution.py:51
  231.4 64.1 %collective-permute-start.93 = (bf16[256,1024]{1,0:T(8,128)(2,1)}, bf16[256,1024]{1,0:T(8,128)(2,1)S(1)}, u32[]{:S(2)}, u32[]{:S(2)}) collective-permute-start(bf16[256,1024]{1,0:T(8,128)(2,1)} %get-tuple-element.323.refs_0_.refs_14_), channel_id=1, source_target_pairs={{0,4},{4,0},{1,5},{5,1},{2,6},{6,2},{3,7},{7,3},{8,12},{12,8},{9,1... | collective-permute-start | bytes 1572872 | tf_op jit(solution)/shard_map/ppermute | solution.py:53
  242.0 32.3 %collective-permute-start.60 = (bf16[256,1024]{1,0:T(8,128)(2,1)S(1)}, bf16[256,1024]{1,0:T(8,128)(2,1)S(1)}, u32[]{:S(2)}, u32[]{:S(2)}) collective-permute-start(bf16[256,1024]{1,0:T(8,128)(2,1)S(1)} %multiply_convert_fusion.refs_0_), channel_id=1, source_target_pairs={{0,2},{1,3},{2,0},{3,1},{4,6},{5,7},{6,4},{7,5},{8,10},{9,11},{10,... | collective-permute-start | bytes 1572872 | tf_op jit(solution)/shard_map/ppermute | solution.py:51
  304.7 31.9 %collective-permute-start.89 = (bf16[256,1024]{1,0:T(8,128)(2,1)}, bf16[256,1024]{1,0:T(8,128)(2,1)}, u32[]{:S(2)}, u32[]{:S(2)}) collective-permute-start(bf16[256,1024]{1,0:T(8,128)(2,1)} %get-tuple-element.323.refs_0_.refs_14_), channel_id=1, source_target_pairs={{0,1},{1,0},{2,3},{3,2},{4,5},{5,4},{6,7},{7,6},{8,9},{9,8},{10,11... | collective-permute-start | bytes 1572872 | tf_op jit(solution)/shard_map/ppermute | solution.py:51
  304.8 46.1 %collective-permute-start.92 = (bf16[256,1024]{1,0:T(8,128)(2,1)}, bf16[256,1024]{1,0:T(8,128)(2,1)}, u32[]{:S(2)}, u32[]{:S(2)}) collective-permute-start(bf16[256,1024]{1,0:T(8,128)(2,1)} %copy-done.54), channel_id=1, source_target_pairs={{0,1},{1,0},{2,3},{3,2},{4,5},{5,4},{6,7},{7,6},{8,9},{9,8},{10,11... | collective-permute-start | bytes 1572872 | tf_op jit(solution)/shard_map/ppermute | solution.py:51
  344.9 69.9 %collective-permute-start.72 = (bf16[256,1024]{1,0:T(8,128)(2,1)}, bf16[256,1024]{1,0:T(8,128)(2,1)}, u32[]{:S(2)}, u32[]{:S(2)}) collective-permute-start(bf16[256,1024]{1,0:T(8,128)(2,1)} %get-tuple-element.202), channel_id=1, source_target_pairs={{0,1},{1,0},{2,3},{3,2},{4,5},{5,4},{6,7},{7,6},{8,9},{9,8},{10,11... | collective-permute-start | bytes 1572872 | tf_op jit(solution)/shard_map/ppermute | solution.py:51
  350.9 35.9 %collective-permute-start.90 = (bf16[256,1024]{1,0:T(8,128)(2,1)S(1)}, bf16[256,1024]{1,0:T(8,128)(2,1)S(1)}, u32[]{:S(2)}, u32[]{:S(2)}) collective-permute-start(bf16[256,1024]{1,0:T(8,128)(2,1)S(1)} %get-tuple-element.211), channel_id=1, source_target_pairs={{0,1},{1,0},{2,3},{3,2},{4,5},{5,4},{6,7},{7,6},{8,9},{9,8},{10,11... | collective-permute-start | bytes 1572872 | tf_op jit(solution)/shard_map/ppermute | solution.py:51
  380.7 34.2 %collective-permute-start.86 = (bf16[256,1024]{1,0:T(8,128)(2,1)}, bf16[256,1024]{1,0:T(8,128)(2,1)}, u32[]{:S(2)}, u32[]{:S(2)}) collective-permute-start(bf16[256,1024]{1,0:T(8,128)(2,1)} %pad_maximum_fusion.10), channel_id=1, source_target_pairs={{0,4},{4,0},{1,5},{5,1},{2,6},{6,2},{3,7},{7,3},{8,12},{12,8},{9,1... | collective-permute-start | bytes 1572872 | tf_op jit(solution)/shard_map/ppermute | solution.py:53
  387.6 27.3 %collective-permute-start.83 = (bf16[256,1024]{1,0:T(8,128)(2,1)}, bf16[256,1024]{1,0:T(8,128)(2,1)}, u32[]{:S(2)}, u32[]{:S(2)}) collective-permute-start(bf16[256,1024]{1,0:T(8,128)(2,1)} %pad_maximum_fusion.9), channel_id=1, source_target_pairs={{0,2},{1,3},{2,0},{3,1},{4,6},{5,7},{6,4},{7,5},{8,10},{9,11},{10,... | collective-permute-start | bytes 1572872 | tf_op jit(solution)/shard_map/ppermute | solution.py:51
  421.2 42.6 %collective-permute-start.87 = (bf16[128,1024]{1,0:T(8,128)(2,1)}, bf16[128,1024]{1,0:T(8,128)(2,1)}, u32[]{:S(2)}, u32[]{:S(2)}) collective-permute-start(bf16[128,1024]{1,0:T(8,128)(2,1)} %get-tuple-element.329), channel_id=1, source_target_pairs={{0,4},{4,0},{1,5},{5,1},{2,6},{6,2},{3,7},{7,3},{8,12},{12,8},{9,1... | collective-permute-start | bytes 786440 | tf_op jit(solution)/shard_map/ppermute | solution.py:53
  422.3 42.7 %collective-permute-start.156 = (bf16[8,32,1024]{2,1,0:T(8,128)(2,1)}, bf16[8,32,1024]{2,1,0:T(8,128)(2,1)}, u32[]{:S(2)}, u32[]{:S(2)}) collective-permute-start(bf16[8,32,1024]{2,1,0:T(8,128)(2,1)} %get-tuple-element.268), channel_id=1, source_target_pairs={{0,1},{1,0},{2,3},{3,2},{4,5},{5,4},{6,7},{7,6},{8,9},{9,8},{10,11... | collective-permute-start | bytes 1572872 | tf_op jit(solution)/shard_map/ppermute | solution.py:51
  463.4 263.3 %reduce-scatter.3.cloned.1.call-start = ((), (), s32[]{:S(2)}) async-start(), calls=%async_computation.2 | async-start | bytes 3932160 | tf_op jit(solution)/shard_map/reduce_scatter | solution.py:269
  514.8 26.6 %collective-permute-start.143 = (bf16[128,768]{1,0:T(8,128)(2,1)S(1)}, bf16[128,768]{1,0:T(8,128)(2,1)S(1)}, u32[]{:S(2)}, u32[]{:S(2)}) collective-permute-start(bf16[128,768]{1,0:T(8,128)(2,1)S(1)} %fusion.13), channel_id=1, source_target_pairs={{0,8},{8,16},{16,24},{24,0},{1,9},{9,17},{17,25},{25,1},{2,10},{10... | collective-permute-start | bytes 589832 | tf_op jit(solution)/shard_map/ppermute | solution.py:62
  530.5 48.7 %collective-permute-start.161 = (bf16[32,1024]{1,0:T(8,128)(2,1)S(1)}, bf16[32,1024]{1,0:T(8,128)(2,1)S(1)}, u32[]{:S(2)}, u32[]{:S(2)}) collective-permute-start(bf16[32,1024]{1,0:T(8,128)(2,1)S(1)} %fusion.27), channel_id=1, source_target_pairs={{0,8},{8,16},{16,24},{24,0},{1,9},{9,17},{17,25},{25,1},{2,10},{10... | collective-permute-start | bytes 196616 | tf_op jit(solution)/shard_map/ppermute | solution.py:62
  600.3 37.7 %collective-permute-start.149 = (bf16[8,32,1024]{2,1,0:T(8,128)(2,1)}, bf16[8,32,1024]{2,1,0:T(8,128)(2,1)}, u32[]{:S(2)}, u32[]{:S(2)}) collective-permute-start(bf16[8,32,1024]{2,1,0:T(8,128)(2,1)} %get-tuple-element.264), channel_id=1, source_target_pairs={{0,1},{1,0},{2,3},{3,2},{4,5},{5,4},{6,7},{7,6},{8,9},{9,8},{10,11... | collective-permute-start | bytes 1572872 | tf_op jit(solution)/shard_map/ppermute | solution.py:51
  600.8 45.4 %collective-permute-start.148 = (bf16[8,32,1024]{2,1,0:T(8,128)(2,1)}, bf16[8,32,1024]{2,1,0:T(8,128)(2,1)}, u32[]{:S(2)}, u32[]{:S(2)}) collective-permute-start(bf16[8,32,1024]{2,1,0:T(8,128)(2,1)} %get-tuple-element.262), channel_id=1, source_target_pairs={{0,1},{1,0},{2,3},{3,2},{4,5},{5,4},{6,7},{7,6},{8,9},{9,8},{10,11... | collective-permute-start | bytes 1572872 | tf_op jit(solution)/shard_map/ppermute | solution.py:51
  628.8 61.3 %collective-permute-start.130 = (bf16[256,1024]{1,0:T(8,128)(2,1)}, bf16[256,1024]{1,0:T(8,128)(2,1)}, u32[]{:S(2)}, u32[]{:S(2)}) collective-permute-start(bf16[256,1024]{1,0:T(8,128)(2,1)} %get-tuple-element.254), channel_id=1, source_target_pairs={{0,1},{1,0},{2,3},{3,2},{4,5},{5,4},{6,7},{7,6},{8,9},{9,8},{10,11... | collective-permute-start | bytes 1572872 | tf_op jit(solution)/shard_map/ppermute | solution.py:51
  635.4 27.9 %collective-permute-start.134 = (bf16[4,128,768]{2,1,0:T(8,128)(2,1)}, bf16[4,128,768]{2,1,0:T(8,128)(2,1)}, u32[]{:S(2)}, u32[]{:S(2)}) collective-permute-start(bf16[4,128,768]{2,1,0:T(8,128)(2,1)} %get-tuple-element.258), channel_id=1, source_target_pairs={{0,4},{4,0},{1,5},{5,1},{2,6},{6,2},{3,7},{7,3},{8,12},{12,8},{9,1... | collective-permute-start | bytes 2359304 | tf_op jit(solution)/shard_map/ppermute | solution.py:53
  644.9 63.8 %collective-permute-start.168 = (bf16[32,1024]{1,0:T(8,128)(2,1)}, bf16[32,1024]{1,0:T(8,128)(2,1)}, u32[]{:S(2)}, u32[]{:S(2)}) collective-permute-start(bf16[32,1024]{1,0:T(8,128)(2,1)} %get-tuple-element.313), channel_id=1, source_target_pairs={{0,1},{1,0},{2,3},{3,2},{4,5},{5,4},{6,7},{7,6},{8,9},{9,8},{10,11... | collective-permute-start | bytes 196616 | tf_op jit(solution)/shard_map/ppermute | solution.py:51
  654.7 36.0 %collective-permute-start.132 = (bf16[256,1024]{1,0:T(8,128)(2,1)S(1)}, bf16[256,1024]{1,0:T(8,128)(2,1)S(1)}, u32[]{:S(2)}, u32[]{:S(2)}) collective-permute-start(bf16[256,1024]{1,0:T(8,128)(2,1)S(1)} %add_convert_fusion.2), channel_id=1, source_target_pairs={{0,2},{1,3},{2,0},{3,1},{4,6},{5,7},{6,4},{7,5},{8,10},{9,11},{10,... | collective-permute-start | bytes 1572872 | tf_op jit(solution)/shard_map/ppermute | solution.py:51
  663.3 26.1 %collective-permute-start.170 = (bf16[128,1024]{1,0:T(8,128)(2,1)S(1)}, bf16[128,1024]{1,0:T(8,128)(2,1)S(1)}, u32[]{:S(2)}, u32[]{:S(2)}) collective-permute-start(bf16[128,1024]{1,0:T(8,128)(2,1)S(1)} %pad_maximum_fusion.29), channel_id=1, source_target_pairs={{0,2},{1,3},{2,0},{3,1},{4,6},{5,7},{6,4},{7,5},{8,10},{9,11},{10,... | collective-permute-start | bytes 786440 | tf_op jit(solution)/shard_map/ppermute | solution.py:51
  (373 other events, 4113.6 us)
Sparse Core Ops, SparseCore 0:
  53.3 74.1 all-gather.4
  188.3 83.0 all-gather.6
  463.6 69.8 reduce-scatter.4
  600.4 60.2 reduce-scatter.2

commit v3 on v2

--- a/solution.py
+++ b/solution.py
@@ -37,14 +37,6 @@
         self.seq_bits = [1 << b for b in range(self.seq_n.bit_length() - 1)]
         self.lo_bits = [b for b in self.seq_bits if b < self.lo_n]
         self.hi_bits = [b // self.lo_n for b in self.seq_bits if b >= self.lo_n]
-        self.chains = {"dp": [], "hi": []}
-
-    def queued(self, name, send, x, depth=2):
-        chain = self.chains[name]
-        if len(chain) >= depth:
-            x = after(x, chain[-depth])
-        chain.append(send(x))
-        return chain[-1]
 
     def swap(self, x, bit):
         if bit < self.lo_n:
@@ -52,78 +44,50 @@
         bit //= self.lo_n
         return lax.ppermute(x, "hi", [(i, i ^ bit) for i in range(self.hi_n)])
 
-    def swap_hi(self, x, bit):
-        return self.swap(x, bit * self.lo_n)
+    def swap_hi(self, x):
+        return self.swap(x, self.lo_n)
 
     def swap_dp(self, x, bit):
         return lax.ppermute(x, "dp", [(i, i ^ bit) for i in range(self.dp_n)])
 
-    def next_dp(self, x):
-        return lax.ppermute(x, "dp", [(i, (i + 1) % self.dp_n) for i in range(self.dp_n)])
-
-    def gather(self, block, bits):
+    def shift_dp(self, blocks):
+        n = self.dp_n
+        return [
+            lax.ppermute(x, "dp", [(i, (i + k + 1) % n) for i in range(n)])
+            for k, x in enumerate(blocks)
+        ]
+
+    def gather(self, block, bits, held=None):
         blocks = {0: block}
-        if len(bits) == 3:
-            core, first, second = bits
-            half = block.shape[0] // 2
-            blocks[first], blocks[second] = self.swap(block, first), self.swap(block, second)
-            corner = (
-                self.swap(blocks[first][:half], second),
-                self.swap(blocks[second][half:], first),
-            )
-            blocks[first | second] = jnp.concatenate(corner, axis=0)
+        if held is not None:
+            blocks[bits[-1]] = held
+        for bit in reversed(bits):
             for r in list(blocks):
-                blocks[r | core] = self.swap(blocks[r], core)
-        else:
-            for bit in reversed(bits):
-                for r in list(blocks):
-                    blocks[r | bit] = self.swap(blocks[r], bit)
+                if r & bit:
+                    continue
+                if r | bit in blocks:
+                    continue
+                blocks[r | bit] = self.swap(blocks[r], bit)
         return [blocks[r] for r in range(len(blocks))]
 
     def add_swapped(self, mine, sent, bit):
         return mine.astype(F32) + self.swap(sent.astype(BF), bit).astype(F32)
 
     def scatter(self, blocks, bits):
-        if len(bits) == 3:
-            core, first, second = bits
-            half = blocks[0].shape[0] // 2
-            order = (first | second, first, second, 0)
-            sums = {r: self.add_swapped(blocks[r], blocks[r | core], core) for r in order}
-            corner = sums[first | second]
-            top = self.add_swapped(sums[second][:half], corner[:half], first)
-            bottom = self.add_swapped(sums[first][half:], corner[half:], second)
-            to_second = jnp.concatenate([top, sums[second][half:]], axis=0)
-            to_first = jnp.concatenate([sums[first][:half], bottom], axis=0)
-            total = self.add_swapped(sums[0], to_first, first)
-            return self.add_swapped(total, to_second, second)
         blocks = dict(enumerate(blocks))
         for bit in bits:
-            blocks = {
-                r: self.add_swapped(blocks[r], blocks[r | bit], bit)
-                for r in sorted(blocks, reverse=True)
-                if not r & bit
-            }
+            blocks = self.halve(blocks, bit)
         return blocks[0]
 
+    def halve(self, blocks, bit):
+        return {
+            r: self.add_swapped(blocks[r], blocks[r | bit], bit)
+            for r in sorted(blocks, reverse=True)
+            if not r & bit
+        }
+
     def trade(self, blocks, bits):
-        blocks = dict(enumerate(blocks))
-        rows = blocks[0].shape[0]
-        for bit in reversed(bits):
-            moving = [r for r in blocks if r & bit]
-            if bit == 1:
-                for r in moving:
-                    blocks[r] = self.swap(blocks[r], bit)
-            else:
-                sent = self.swap(jnp.concatenate([blocks[r] for r in moving], axis=0), bit)
-                for n, r in enumerate(moving):
-                    blocks[r] = sent[n * rows : (n + 1) * rows]
-        return [blocks[r] for r in range(len(blocks))]
-
-    def trade_hi(self, blocks):
-        blocks = list(blocks)
-        for bit in self.hi_bits:
-            blocks = [self.swap_hi(b, bit) if q & bit else b for q, b in enumerate(blocks)]
-        return blocks
+        return Trade(self, blocks, bits).finish()
 
     def all_small(self, x, combine):
         for bit in self.seq_bits:
@@ -134,33 +98,152 @@
             bit *= 2
         return x
 
-    def gather_rows(self, own):
-        full = place_first(own, self.dp_n * self.hi_n, self.dp * self.hi_n + self.hi)
-        full = full.reshape((self.dp_n, self.hi_n) + own.shape)
-        chunk = own
-        for step in range(self.dp_n):
-            if step:
-                chunk = self.queued("dp", self.next_dp, chunk)
-            source = (self.dp - step) % self.dp_n
-            blocks = {0: chunk}
-            for bit in self.hi_bits:
-                for q in list(blocks):
-                    blocks[q | bit] = self.queued(
-                        "hi", lambda x, bit=bit: self.swap_hi(x, bit), blocks[q]
-                    )
-            for q, block in blocks.items():
-                if step or q:
-                    start = (source, self.hi ^ q) + (0,) * own.ndim
-                    full = lax.dynamic_update_slice(full, block[None, None], start)
-        return full
-
-    def scatter_rows(self, mine, other):
-        mine = self.add_swapped(mine, other, self.lo_n)
-        running = pick(mine, (self.dp - 1) % self.dp_n)
-        for step in range(1, self.dp_n):
-            running = self.next_dp(running.astype(BF)).astype(F32)
-            running = running + pick(mine, (self.dp - 1 - step) % self.dp_n)
-        return running
+
+class Trade:
+    def __init__(self, net, blocks, bits):
+        self.net, self.blocks, self.left, self.moving = net, list(blocks), list(bits), []
+
+    def step(self, *earlier):
+        bit = self.left.pop()
+        moving = [r for r in range(len(self.blocks)) if r & bit]
+        if bit == 1:
+            self.moving = [self.net.swap(after(self.blocks[r], *earlier), bit) for r in moving]
+            for r, x in zip(moving, self.moving):
+                self.blocks[r] = x
+            return
+        rows = self.blocks[0].shape[0]
+        sent = after(jnp.concatenate([self.blocks[r] for r in moving], axis=0), *earlier)
+        self.moving = [self.net.swap(sent, bit)]
+        for n, r in enumerate(moving):
+            self.blocks[r] = self.moving[0][n * rows : (n + 1) * rows]
+
+    def finish(self):
+        while self.left:
+            self.step()
+        return self.blocks
+
+
+class SumAll:
+    def __init__(self, net, blocks):
+        self.net, self.blocks, self.moving, self.step_n = net, blocks, [], 0
+
+    def step(self, *earlier):
+        net, bits = self.net, self.net.seq_bits
+        self.step_n += 1
+        if len(bits) != 3:
+            if self.step_n == 1:
+                self.blocks = [net.scatter(self.blocks, bits)]
+            self.moving = []
+            return
+        core, first, second = bits
+        half = self.blocks[0].shape[0] // 2
+        if self.step_n == 1:
+            order = (first | second, first, second, 0)
+            self.moving = [net.swap(after(self.blocks[r | core], *earlier), core) for r in order]
+            self.pairs = {r: [self.blocks[r], x] for r, x in zip(order, self.moving)}
+        elif self.step_n == 2:
+            top, bottom = add_low([self.pairs[first | second]], cut=half)
+            self.moving = [
+                net.swap(after(top, *earlier), first),
+                net.swap(after(bottom, *earlier), second),
+            ]
+        else:
+            top, bottom = self.moving
+            to_first, to_second = add_low(
+                [self.pairs[first], self.pairs[second]], [(half, bottom), (0, top)]
+            )
+            self.moving = [
+                net.swap(after(to_first, *earlier), first),
+                net.swap(after(to_second, *earlier), second),
+            ]
+
+    def parts(self):
+        while self.step_n < 3:
+            self.step()
+        return self.pairs[0] + self.moving if self.moving else self.blocks
+
+
+class SumLo:
+    def __init__(self, net, blocks):
+        self.net, self.blocks = net, blocks
+
+    def step(self, *earlier):
+        net = self.net
+        if len(net.lo_bits) != 2:
+            self.left = [net.scatter(self.blocks, net.lo_bits)]
+            self.moving = []
+            return
+        self.moving = [net.swap(after(self.blocks[r | 1], *earlier), 1) for r in (2, 0)]
+        self.left = [self.blocks[0], self.moving[1]]
+
+    def parts(self, *earlier):
+        if self.moving:
+            (far,) = add_low([[self.blocks[2], self.moving[0]]])
+            self.moving = [self.net.swap(after(far, *earlier), 2)]
+        return self.left + self.moving
+
+
+class GatherBoth:
+    def __init__(self, net, own, *earlier):
+        self.net, self.own = net, own
+        own = after(own, *earlier)
+        self.own_came = net.swap_hi(own)
+        self.by_dp = net.shift_dp([own] * (net.dp_n - 1))
+        self.moving = [self.own_came] + self.by_dp
+
+    def step(self, *earlier):
+        self.rest_came = self.net.swap_hi(after(jnp.concatenate(self.by_dp, axis=0), *earlier))
+        self.moving = [self.rest_came]
+
+    def finish(self):
+        net = self.net
+        rows, columns = self.own.shape
+        n = net.dp_n
+
+        def kernel(at, own, own_came, rest_came, *refs):
+            *by_dp, out = refs
+            dp, hi = at[0] // 2, at[0] % 2
+            out[at[0]] = own[...]
+            out[dp * 2 + 1 - hi] = own_came[...]
+            for k in range(1, n):
+                source = lax.rem(dp + n - k, n)
+                out[source * 2 + hi] = by_dp[k - 1][...]
+                out[source * 2 + 1 - hi] = rest_came[(k - 1) * rows : k * rows, :]
+
+        return on_chip(
+            kernel,
+            [((2 * n, rows, columns), BF)],
+            self.own,
+            self.own_came,
+            self.rest_came,
+            *self.by_dp,
+            at=net.dp * 2 + net.hi,
+            name="join_gathered",
+        )[0]
+
+
+class SumBoth:
+    def __init__(self, net, mine, came):
+        n = net.dp_n
+
+        def kernel(at, x, y, own, *outs):
+            own[...] = x[at[0]] + y[at[0]].astype(F32)
+            for k, out in enumerate(outs):
+                to = lax.rem(at[0] + k + 1, n)
+                out[...] = (x[to] + y[to].astype(F32)).astype(BF)
+
+        shape = mine.shape[1:]
+        self.own, *self.blocks = on_chip(
+            kernel, [(shape, F32)] + [(shape, BF)] * (n - 1), mine, came, at=net.dp, name="sum_hi"
+        )
+        self.net = net
+
+    def step(self, *earlier):
+        self.blocks[0] = after(self.blocks[0], *earlier)
+        self.moving = self.net.shift_dp(self.blocks)
+
+    def total(self):
+        return self.own + sum(x.astype(F32) for x in self.moving)
 
 
 def after(x, *earlier):
@@ -172,104 +255,64 @@
     return jnp.stack([pick(stacked, index ^ j) for j in range(len(blocks))])
 
 
-def place_first(block, count, position):
-    def kernel(at, block_ref, out_ref):
-        out_ref[0] = block_ref[...]
-
-    zeros = (0,) * block.ndim
-    return pl.pallas_call(
-        kernel,
-        grid_spec=pltpu.PrefetchScalarGridSpec(
-            num_scalar_prefetch=1,
-            grid=(1,),
-            in_specs=[pl.BlockSpec(block.shape, lambda i, at: zeros)],
-            out_specs=pl.BlockSpec((1,) + block.shape, lambda i, at: (at[0],) + zeros),
-        ),
-        out_shape=jax.ShapeDtypeStruct((count,) + block.shape, block.dtype),
-        name="place_first",
-    )(position.astype(jnp.int32).reshape(1), block)
-
-
-def split_columns(shard, index, count, width):
+def split_columns(shard, count, width):
     rows = shard.shape[0]
     parts = shard.shape[1] // count // width
     if width % LANES:
-        shard = shard.reshape(rows, parts, count, width)
-        return [pick(shard, index ^ r, 2).reshape(rows, -1) for r in range(count)]
-
-    def kernel(at, shard_ref, *outs):
-        for r, out in enumerate(outs):
+        shard = shard.reshape(rows, parts, count, width).transpose(2, 0, 1, 3)
+        return shard.reshape(count, rows, parts * width)
+
+    def kernel(shard_ref, out):
+        for r in range(count):
             for p in range(parts):
-                start = pl.multiple_of((p * count + (at[0] ^ r)) * width, width)
-                out[:, p * width : (p + 1) * width] = shard_ref[:, pl.ds(start, width)]
-
-    return pl.pallas_call(
-        kernel,
-        in_specs=[pl.BlockSpec(memory_space=pltpu.SMEM), pl.BlockSpec(memory_space=pltpu.VMEM)],
-        out_specs=[pl.BlockSpec(memory_space=pltpu.VMEM)] * count,
-        out_shape=[jax.ShapeDtypeStruct((rows, parts * width), BF)] * count,
-        name="split_columns",
-    )(index.astype(jnp.int32).reshape(1), shard)
-
-
-def merge_columns(blocks, index, width):
-    rows, count = blocks[0].shape[0], len(blocks)
-    parts = blocks[0].shape[1] // width
+                start = (p * count + r) * width
+                out[r, :, p * width : (p + 1) * width] = shard_ref[:, start : start + width]
+
+    return on_chip(kernel, [((count, rows, parts * width), BF)], shard, name="split_columns")[0]
+
+
+def merge_columns(blocks, layers, width):
+    count, rows = blocks.shape[0], blocks.shape[1] // layers
+    parts = blocks.shape[2] // width
+    columns = parts * count * width
     if width % LANES:
-        shard = in_order(blocks, index).reshape(count, rows, parts, width)
-        return shard.transpose(1, 2, 0, 3).reshape(rows, -1).astype(F32)
-
-    def kernel(at, *refs):
-        out = refs[-1]
-        for r, block in enumerate(refs[:-1]):
-            for p in range(parts):
-                start = pl.multiple_of((p * count + (at[0] ^ r)) * width, width)
-                out[:, pl.ds(start, width)] = block[:, p * width : (p + 1) * width].astype(F32)
-
-    return pl.pallas_call(
-        kernel,
-        in_specs=[pl.BlockSpec(memory_space=pltpu.SMEM)]
-        + [pl.BlockSpec(memory_space=pltpu.VMEM)] * count,
-        out_specs=pl.BlockSpec(memory_space=pltpu.VMEM),
-        out_shape=jax.ShapeDtypeStruct((rows, parts * count * width), F32),
-        name="merge_columns",
-    )(index.astype(jnp.int32).reshape(1), *blocks)
-
-
-def trade_columns(net, shard, bits, width):
-    index, count = (net.seq, net.seq_n) if bits == net.seq_bits else (net.lo, net.lo_n)
-    blocks = net.trade(split_columns(shard, index, count, width), bits)
-    return join_rows(blocks, index)
-
-
-def restore_columns(net, own, bits, width):
-    index, count = (net.seq, net.seq_n) if bits == net.seq_bits else (net.lo, net.lo_n)
-    own = own.astype(BF).reshape(count, -1, own.shape[1])
-    blocks = net.trade([pick(own, index ^ r) for r in range(count)], bits)
-    return merge_columns(blocks, index, width)
-
-
-def fetch_attention(net, own_qkv, own_out):
-    rows, cut = own_qkv.shape
-    pieces = jnp.split(own_out, rows // own_out.shape[0], axis=1)
-    own = jnp.concatenate([own_qkv, jnp.concatenate(pieces, axis=0)], axis=1)
-    full = net.gather_rows(own).reshape(-1, rows, own.shape[1])
-    blocks = net.gather(full[:, :, cut:], net.lo_bits)
-    return full.reshape(-1, own.shape[1]), join_middle(blocks, net.lo, own_out.shape[0])
-
-
-def fetch_hidden(net, own_in, own_down):
-    columns = own_in.shape[1]
-    pieces = jnp.split(own_down, own_down.shape[1] // columns, axis=1)
-    own = jnp.concatenate([own_in] + pieces, axis=0)
-    return lax.all_gather(own, "dp", axis=0)
-
-
-def scatter_hidden(net, grads, rows_in):
-    own = lax.psum_scatter(grads, "dp", scatter_dimension=0)
-    own_in, own_down = own[:rows_in], own[rows_in:]
-    pieces = rows_in * net.dp_n // grads.shape[2]
-    return own_in, jnp.concatenate(jnp.split(own_down, pieces, axis=0), axis=1).astype(F32)
+        shards = blocks.reshape(count, layers, rows, parts, width).transpose(1, 2, 3, 0, 4)
+        return shards.reshape(layers, rows, columns).astype(F32)
+
+    def kernel(ref, out):
+        for r in range(count):
+            for layer in range(layers):
+                for p in range(parts):
+                    start = (p * count + r) * width
+                    part = ref[r, layer * rows : (layer + 1) * rows, p * width : (p + 1) * width]
+                    out[layer, :, start : start + width] = part.astype(F32)
+
+    return on_chip(kernel, [((layers, rows, columns), F32)], blocks, name="merge_columns")[0]
+
+
+def own_columns(blocks, layers):
+    count, rows, columns = blocks.shape
+    blocks = blocks.reshape(count, layers, rows // layers, columns)
+    return [blocks[:, n].reshape(-1, columns) for n in range(layers)]
+
+
+def return_rows(layers, axes, count):
+    own = jnp.stack([x.astype(BF).reshape(count, -1, x.shape[1]) for x in layers], axis=1)
+    own = own.reshape(count, -1, own.shape[-1])
+    return lax.all_to_all(own, axes, 0, 0, tiled=True)
+
+
+def join_pieces(own, other, axis):
+    if axis == 1:
+        pieces = jnp.split(other, own.shape[0] // other.shape[0], axis=1)
+        return jnp.concatenate([own, jnp.concatenate(pieces, axis=0)], axis=1)
+    return jnp.concatenate([own] + jnp.split(other, other.shape[1] // own.shape[1], axis=1))
+
+
+def split_hidden(own, rows_in, width):
+    pieces = width // own.shape[1]
+    down = jnp.concatenate(jnp.split(own[rows_in:], pieces, axis=0), axis=1)
+    return own[:rows_in], down.astype(F32)
 
 
 LANES = 128
@@ -277,7 +320,7 @@
 TN = (((0,), (0,)), ((), ()))
 VMEM = pl.BlockSpec(memory_space=pltpu.VMEM)
 SMEM = pl.BlockSpec(memory_space=pltpu.SMEM)
-LIMIT = 24 * 2**20
+LIMIT = 16 * 2**20
 
 
 def on_chip(kernel, outs, *arrays, at=None, scratch=(), flops=0, name=None):
@@ -296,6 +339,80 @@
     )(*first, *arrays)
 
 
+def add_low(groups, extras=None, cut=None):
+    shape = groups[0][0].shape
+    extras = extras or [None] * len(groups)
+    flat, counts = [], []
+    for group, extra in zip(groups, extras):
+        members = group + ([extra[1]] if extra else [])
+        counts.append(len(members))
+        flat += members
+
+    def kernel(*refs):
+        ins, outs = list(refs[: len(flat)]), list(refs[len(flat) :])
+        for count, extra in zip(counts, extras):
+            members = [ins.pop(0) for _ in range(count)]
+            last = members.pop() if extra else None
+            total = sum(x[...].astype(F32) for x in members)
+            if extra:
+                rows = last.shape[0]
+                part = total[extra[0] : extra[0] + rows] + last[...].astype(F32)
+                pieces = [total[: extra[0]], part, total[extra[0] + rows :]]
+                total = jnp.concatenate([p for p in pieces if p.shape[0]], axis=0)
+            total = total.astype(BF)
+            if cut is None:
+                outs.pop(0)[...] = total
+            else:
+                outs.pop(0)[...] = total[:cut]
+                outs.pop(0)[...] = total[cut:]
+
+    if cut is None:
+        shapes = [(shape, BF)] * len(groups)
+    else:
+        shapes = [((cut,) + shape[1:], BF), ((shape[0] - cut,) + shape[1:], BF)]
+    return on_chip(kernel, shapes, *flat, name="add_low")
+
+
+def finish_layer(middle, parts, gain):
+    rows, width = middle.shape
+
+    def kernel(x, g, *refs):
+        *ins, state, normed = refs
+        total = x[...] + sum(part[...].astype(F32) for part in ins)
+        state[...] = total
+        normed[...] = rms_scale(total, g[...]).astype(BF)
+
+    outs = [((rows, width), F32), ((rows, width), BF)]
+    return on_chip(kernel, outs, middle, gain.reshape(1, width), *parts, name="finish_layer")
+
+
+def norm_backward(gradient, parts, values, gain):
+    rows, width = gradient.shape
+
+    def kernel(g, x, gn, *refs):
+        *ins, new, low, gain_out = refs
+        total = sum(part[...].astype(F32) for part in ins)
+        grad, gain_part = norm_adjoint(x[...], gn[...], total)
+        grad = g[...] + grad
+        new[...] = grad
+        low[...] = grad.astype(BF)
+        gain_out[...] = gain_part
+
+    outs = [((rows, width), F32), ((rows, width), BF), ((1, width), F32)]
+    arrays = [gradient, values, gain.reshape(1, width)]
+    new, low, gain_part = on_chip(kernel, outs, *arrays, *parts, name="norm_backward")
+    return new, low, gain_part[0]
+
+
+def norm_adjoint(values, gain, grad):
+    inverse = lax.rsqrt(jnp.mean(values * values, axis=-1, keepdims=True) + EPSILON)
+    normal = values * inverse
+    gain_part = jnp.sum(grad * normal, axis=0, keepdims=True)
+    grad = grad * gain
+    grad = (grad - normal * jnp.mean(grad * normal, axis=-1, keepdims=True)) * inverse
+    return grad, gain_part
+
+
 def project(blocks, matrix, columns):
     rows = blocks[0].shape[0]
 
@@ -357,7 +474,7 @@
     count, hidden = len(blocks), pack.shape[2] // 2
 
     def kernel(*refs):
-        ins, (m, joined), outs = refs[:count], refs[count : count + 2], refs[count + 2 :]
+        m, ins, joined, outs = refs[0], refs[1 : count + 1], refs[count + 1], refs[count + 2 :]
         m_in, m_down = hidden_matrices(m, width)
         for n, (x, out) in enumerate(zip(ins, outs)):
             both = dot(x[...], m_in)
@@ -369,8 +486,8 @@
     joined, *parts = on_chip(
         kernel,
         [((rows * count, 2 * hidden), BF)] + [((rows, width), BF)] * count,
+        pack,
         *blocks,
-        pack,
         flops=2 * rows * count * pack.size,
         name="feed_forward",
     )
@@ -382,7 +499,7 @@
     count, hidden = len(blocks), pack.shape[2] // 2
 
     def kernel(*refs):
-        ins, (j, m, grad_joined, gated) = refs[:count], refs[count : count + 4]
+        m, ins, (j, grad_joined, gated) = refs[0], refs[1 : count + 1], refs[count + 1 : count + 4]
         m_in, m_down = hidden_matrices(m, width)
         for n, (x, out) in enumerate(zip(ins, refs[count + 4 :])):
             part = slice(n * rows, (n + 1) * rows)
@@ -402,9 +519,9 @@
         kernel,
         [((rows * count, 2 * hidden), BF), ((rows * count, hidden), BF)]
         + [((rows, width), BF)] * count,
+        pack,
         *blocks,
         joined,
-        pack,
         flops=2 * rows * count * pack.size,
         name="feed_backward",
     )
@@ -431,15 +548,15 @@
     def body(index, *refs):
         ins, refs = list(refs[: len(flat)]), refs[len(flat) :]
         results, scratch, sems = refs[: len(outs)], refs[len(outs) : -1], refs[-1]
-        copies = []
+        arrived, count = [], 0
         for group, target in zip(groups, scratch):
             taken = [[ins.pop(0) for x in column] for column in group]
-            copies += side_by_side(taken, target, sems, len(copies))
-        for copy in copies:
-            copy.start()
-        for copy in copies:
-            copy.wait()
-        kernel(index, *scratch, *results)
+            copies = side_by_side(taken, target, sems, count)
+            count += len(copies)
+            for copy in copies:
+                copy.start()
+            arrived.append(Arriving(copies, target))
+        kernel(index, *arrived, *results)
 
     return pl.pallas_call(
         body,
@@ -454,6 +571,17 @@
     )(at.astype(jnp.int32).reshape(1), *flat)
 
 
+class Arriving:
+    def __init__(self, copies, ref):
+        self.copies, self.ref = copies, ref
+
+    def __getitem__(self, index):
+        for copy in self.copies:
+            copy.wait()
+        self.copies = []
+        return self.ref[index]
+
+
 def hidden_weights(net, second, grad_joined, gated, grads):
     length = sum(x.shape[0] for x in second)
     width, columns, hidden = second[0].shape[1], grad_joined[0].shape[1], gated[0].shape[1]
@@ -463,18 +591,19 @@
     def kernel(index, a, b, c, d, out):
         for n in range(net.dp_n):
             left = a[:, n * rows : (n + 1) * rows]
-            out[n, :rows, :] = lax.dot_general(
+            first = n * (rows + pieces * down)
+            out[first : first + rows, :] = lax.dot_general(
                 left, b[...], TN, preferred_element_type=F32
             ).astype(BF)
             left = c[:, n * down : (n + 1) * down]
             total = lax.dot_general(left, d[...], TN, preferred_element_type=F32).astype(BF)
             for p in range(pieces):
-                start = rows + p * down
-                out[n, start : start + down, :] = total[:, p * columns : (p + 1) * columns]
+                start = first + rows + p * down
+                out[start : start + down, :] = total[:, p * columns : (p + 1) * columns]
 
     return weight_call(
         kernel,
-        [((net.dp_n, rows + pieces * down, columns), BF)],
+        [((net.dp_n * (rows + pieces * down), columns), BF)],
         [[second], [grad_joined], [gated], [grads]],
         [(length, width), (length, columns), (length, hidden), (length, width)],
         net.dp,
@@ -483,52 +612,59 @@
     )[0]
 
 
-def mixed_weights(net, normed, grads):
+def mixed_weights(net, normed, grads, shares, rows, kept):
     length, width = sum(x.shape[0] for x in normed), normed[0].shape[1]
     columns = sum(g.shape[1] for g in grads)
     chunk = width // net.dp_n // net.hi_n
-
-    def kernel(index, a, b, mine, other):
+    pieces = chunk // rows
+    c = shares[0].shape[1] // pieces
+
+    def kernel(index, a, b, *refs):
+        *parts, mine, other = refs
         for n in range(net.dp_n * net.hi_n):
             left = a[:, n * chunk : (n + 1) * chunk]
             total = lax.dot_general(left, b[...], TN, preferred_element_type=F32)
+            out = sum(part[n * rows : (n + 1) * rows, :].astype(F32) for part in parts)
             here = index[0] == n % net.hi_n
 
-            @pl.when(here)
-            def keep(n=n, total=total):
-                mine[n // net.hi_n] = total
-
-            @pl.when(jnp.logical_not(here))
-            def send(n=n, total=total):
-                other[n // net.hi_n] = total.astype(BF)
-
-    shape = (net.dp_n, chunk, columns)
+            def store(target, kind, n=n, total=total, out=out):
+                target[n // net.hi_n, :, :columns] = total.astype(kind)
+                for p in range(pieces):
+                    cut = out[:, p * c : (p + 1) * c].astype(kind)
+                    target[n // net.hi_n, p * rows : (p + 1) * rows, columns:] = cut
+
+            pl.when(here)(lambda: store(mine, kept))
+            pl.when(jnp.logical_not(here))(lambda: store(other, BF))
+
+    shape = (net.dp_n, chunk, columns + c)
+    flat = [x.astype(BF) for x in shares]
     return weight_call(
         kernel,
-        [(shape, F32), (shape, BF)],
-        [[normed], [[g] for g in grads]],
-        [(length, width), (length, columns)],
+        [(shape, kept), (shape, BF)],
+        [[normed], [[g] for g in grads]] + [[[x]] for x in flat],
+        [(length, width), (length, columns)] + [x.shape for x in flat],
         net.hi,
         2 * length * width * columns,
         "mixed_weights",
     )
 
 
-def out_backward(net, gradient, total, middle, gain, matrix, arrived, rows_out):
+def split_pieces(own, columns, rows):
+    pieces = own.shape[0] // rows
+    return own[:, :columns], jnp.concatenate(jnp.split(own[:, columns:], pieces, axis=0), axis=1)
+
+
+def out_backward(net, gradient, parts, middle, gain, matrix, arrived, rows_out):
     rows, width = gradient.shape
     count, heads = len(arrived), arrived[0].shape[1]
     groups = width // rows_out // count
 
-    def kernel(index, g, t, mid, gn, m, *refs):
+    def kernel(index, g, mid, gn, *refs):
+        sums, m, refs = refs[: len(parts)], refs[len(parts)], refs[len(parts) + 1 :]
         ins, (new, gain_out), refs = refs[:count], refs[count : count + 2], refs[count + 2 :]
         leaving, shares, scratch = refs[:count], refs[count : 2 * count], refs[2 * count]
-        x = mid[...]
-        inverse = lax.rsqrt(jnp.mean(x * x, axis=-1, keepdims=True) + EPSILON)
-        normal = x * inverse
-        grad = t[...]
-        gain_out[...] = jnp.sum(grad * normal, axis=0, keepdims=True)
-        grad = grad * gn[...]
-        grad = (grad - normal * jnp.mean(grad * normal, axis=-1, keepdims=True)) * inverse
+        total = sum(part[...].astype(F32) for part in sums)
+        grad, gain_out[...] = norm_adjoint(mid[...], gn[...], total)
         grad = g[...] + grad
         new[...] = grad
         branch = grad.astype(BF)
@@ -551,9 +687,9 @@
         + [((rows, heads), BF)] * count
         + [((groups, rows_out, width), BF)] * count,
         gradient,
-        total,
         middle,
         gain.reshape(1, width),
+        *parts,
         matrix,
         *arrived,
         at=net.lo,
@@ -585,20 +721,6 @@
         flops=2 * length * matrix.size,
         name="mixed_backward",
     )
-
-
-def join_rows(blocks, index):
-    rows = blocks[0].shape[0]
-    if rows % 16:
-        return in_order(blocks, index).reshape(-1, blocks[0].shape[1])
-
-    def kernel(at, *refs):
-        for r, block in enumerate(refs[:-1]):
-            start = pl.multiple_of((at[0] ^ r) * rows, rows)
-            refs[-1][pl.ds(start, rows), :] = block[...]
-
-    shape = (rows * len(blocks), blocks[0].shape[1])
-    return on_chip(kernel, [(shape, BF)], *blocks, at=index, name="join_rows")[0]
 
 
 def join_middle(blocks, index, rows):
@@ -825,7 +947,7 @@
             jax.ShapeDtypeStruct((heads, length, LANES), F32),
             jax.ShapeDtypeStruct((heads, 8, LANES), F32),
         ],
-        compiler_params=pltpu.CompilerParams(vmem_limit_bytes=48 * 2**20),
+        compiler_params=pltpu.CompilerParams(vmem_limit_bytes=LIMIT * max(1, length // 1024)),
         cost_estimate=pl.CostEstimate(
             flops=8 * heads * length * length * LANES,
             bytes_accessed=16 * length * pairs * LANES,
@@ -874,7 +996,7 @@
             pltpu.VMEM((length, LANES), F32),
             pltpu.VMEM((length, LANES), F32),
         ],
-        compiler_params=pltpu.CompilerParams(vmem_limit_bytes=56 * 2**20),
+        compiler_params=pltpu.CompilerParams(vmem_limit_bytes=LIMIT * max(1, length // 1024)),
         cost_estimate=pl.CostEstimate(
             flops=20 * heads * length * length * LANES,
             bytes_accessed=24 * length * pairs * LANES,
@@ -910,10 +1032,27 @@
     return marks
 
 
-def stages(blocks):
-    count = len(blocks)
-    cuts = [0, 2, 6, 8] if count == 8 else [0, count // 2, count]
-    return [blocks[a:b] for a, b in zip(cuts, cuts[1:])]
+def wave(net, own, compute, held=None):
+    bits = net.seq_bits
+    if len(bits) != 3:
+        blocks = net.gather(own, bits)
+        cuts = (blocks[: len(blocks) // 2], blocks[len(blocks) // 2 :])
+        return blocks, [compute(n, cut) for n, cut in enumerate(cuts)]
+    core, first, second = bits
+    half = own.shape[0] // 2
+    if held is None:
+        held = [net.swap(own, bit) for bit in (first, second)]
+    by_core = net.swap(own, core)
+    outs = [compute(0, [own, by_core])]
+    by_first, by_second = (after(x, outs[0][0]) for x in held)
+    corner = [net.swap(by_first[:half], second), net.swap(by_second[half:], first)]
+    blocks = [own, by_core, by_first, net.swap(by_first, core)]
+    blocks += [by_second, net.swap(by_second, core)]
+    outs.append(compute(1, blocks[2:6]))
+    corner = jnp.concatenate([after(x, outs[1][0]) for x in corner], axis=0)
+    blocks += [corner, net.swap(corner, core)]
+    outs.append(compute(2, blocks[6:]))
+    return blocks, outs
 
 
 def shards(
@@ -943,36 +1082,54 @@
     rows_out = w_out.shape[1]
 
     def to_groups(x):
-        return jnp.concatenate(
-            net.trade_hi([pick(x, net.hi ^ q) for q in range(sequences)]), axis=0
-        )
-
-    def to_devices(x):
-        return in_order(net.trade_hi(jnp.split(x, sequences, axis=0)), net.hi)
-
-    state = to_groups(tokens).astype(F32)
-    own_qkv = trade_columns(net, w_qkv[0], lo_bits, local_width)
-    own_in = trade_columns(net, after(w_in[0], own_qkv), seq_bits, unit)
-    weights = []
-    for layer in range(layers):
-        m_qkv, m_out = fetch_attention(net, own_qkv, w_out[layer])
-        weights.append((m_qkv, m_out, fetch_hidden(net, own_in, w_down[layer])))
-        if layer + 1 < layers:
-            own_qkv = trade_columns(net, after(w_qkv[layer + 1], own_in), lo_bits, local_width)
-            own_in = trade_columns(net, after(w_in[layer + 1], own_qkv), seq_bits, unit)
+        return jnp.concatenate([pick(x, net.hi), net.swap_hi(pick(x, 1 - net.hi))], axis=0)
+
+    def keep_own(x, came):
+        return in_order([x[:tok_dev], came], net.hi)
+
+    qkv_blocks = split_columns(w_qkv.reshape(-1, 3 * width), lo_n, local_width)
+    qkv_came = lax.all_to_all(qkv_blocks, "lo", 0, 0, tiled=True)
+    token_parts = after(tokens, qkv_blocks)
+    tokens_came = net.swap_hi(pick(token_parts, 1 - net.hi))
+    state = jnp.concatenate([pick(token_parts, net.hi), tokens_came], axis=0).astype(F32)
+    flat_in = after(w_in.reshape(-1, w_in.shape[2]), qkv_blocks)
+    in_blocks = split_columns(flat_in, net.seq_n, unit)
+    in_came = lax.all_to_all(in_blocks, ("hi", "lo"), 0, 0, tiled=True)
+    own_qkv = own_columns(qkv_came, layers)
+    ring = GatherBoth(net, join_pieces(own_qkv[0], w_out[0], 1))
+    normed = rms_scale(state, norm_gains[0, 0]).astype(BF)
+    normed_held = net.swap(normed, lo_bits[-1])
+    ring.step(tokens_came, ring.own_came)
+    first_full = ring.finish()
+    own_in = own_columns(in_came, layers)
+    own_packs = [join_pieces(own_in[n], w_down[n], 0) for n in range(layers)]
+    packs = [lax.all_gather(after(own_packs[0], *ring.by_dp), "dp", axis=0)]
 
     pair = to_groups(jnp.stack([variate_ids, time_ids], axis=-1))
     pair = jnp.concatenate(net.gather(pair, lo_bits), axis=0)
     tables = head_tables(pair[:, 0], pair[:, 1], head_size)
 
-    saved = []
+    def matrices(full):
+        full = full.reshape((-1, own_qkv[0].shape[0]) + full.shape[2:])
+        blocks = net.gather(full[:, :, 3 * local_width :], lo_bits)
+        return full.reshape(-1, full.shape[2]), join_middle(blocks, net.lo, rows_out)
+
+    saved, weights = [], []
     best_scores = jnp.full((layers, heads), FLOOR_VALUE, F32)
     for layer in range(layers):
+        final = layer + 1 == layers
+        weights.append(matrices(full_next if layer else first_full) + (packs[layer],))
         m_qkv, m_out, pack = weights[layer]
+        ring = None
         layer_in = state
-        normed = rms_scale(layer_in, norm_gains[layer, 0]).astype(BF)
-        normed = net.gather(normed, lo_bits)
-        mixed = project(normed, m_qkv, 3 * local_width)
+        blocks = net.gather(normed, lo_bits, None if layer else normed_held)
+        mixed = project(blocks, m_qkv, 3 * local_width)
+        if not final:
+            own_next = join_pieces(own_qkv[layer + 1], w_out[layer + 1], 1)
+            came_next = net.swap_hi(after(own_next, mixed))
+        if final:
+            seed_grad = to_groups(after(cotangent, blocks[-1]))
+            seed_held = [net.swap(after(seed_grad, mixed), seq_bits[-1])]
         bias_pair = lax.dynamic_slice_in_dim(head_bias[layer], head_start, local_heads, 1)
         gains = jnp.concatenate([qk_gains[layer]] * 2, axis=1)
         bias = bias_marks(bias_pair, head_size)
@@ -981,19 +1138,33 @@
         best_scores = lax.dynamic_update_slice(
             best_scores, head_tops[None, :], (jnp.int32(layer), head_start)
         )
-        arrived = net.trade(jnp.split(attended, lo_n, axis=0), lo_bits)
+        leaving = attended
+        leaving = after(attended, *(seed_held if final else [came_next]))
+        arrived = net.trade(jnp.split(leaving, lo_n, axis=0), lo_bits)
+        if not final:
+            own_next = in_order([own_next, came_next], net.hi).reshape(-1, own_next.shape[1])
+            full_next = lax.all_gather(after(own_next, packs[-1]), "dp", axis=0, tiled=True)
+            packs.append(lax.all_gather(after(own_packs[layer + 1], full_next), "dp", axis=0))
+            full_next = full_next.reshape((net.dp_n * 2, -1) + full_next.shape[1:])
         middle, second = out_project(layer_in, arrived, m_out, norm_gains[layer, 1], net.lo)
-        second = net.gather(second, seq_bits)
-        joined, partial = [], []
-        for part in stages(second):
-            joined_part, out = feed_forward(part, pack)
-            joined.append(joined_part)
-            partial += out
-        state = middle + net.scatter(partial, seq_bits)
-        saved.append((layer_in, normed, mixed, gains, bias, kept, arrived, middle, second, joined))
-    layer_out = to_devices(state.astype(BF))
-
-    gradient = to_groups(cotangent).astype(F32)
+
+        def forward(n, blocks, pack=pack):
+            joined, parts = feed_forward(blocks, pack)
+            return [joined] + parts
+
+        second, outs = wave(net, second, forward)
+        joined = [out[0] for out in outs]
+        partial = [part for out in outs for part in out[1:]]
+        if final:
+            final_sum = SumAll(net, partial)
+        else:
+            parts = SumAll(net, partial).parts()
+            state, normed = finish_layer(middle, parts, norm_gains[layer + 1, 0])
+        saved.append((layer_in, blocks, mixed, gains, bias, kept, arrived, middle, second, joined))
+
+    if len(seq_bits) == 3:
+        seed_held = [net.swap(after(seed_grad, outs[0][0]), seq_bits[1])] + seed_held
+    gradient = seed_grad.astype(F32)
     qkv_parts = [None] * layers
     out_parts = [None] * layers
     in_parts = [None] * layers
@@ -1001,48 +1172,98 @@
     norm_parts = [None] * layers
     qk_parts = [None] * layers
     bias_parts = [None] * layers
+    hidden_sums = [None] * layers
+    attention_sums = [None] * layers
+    sums, low = None, seed_grad
     for layer in reversed(range(layers)):
+        final = layer + 1 == layers
         m_qkv, m_out, pack = weights[layer]
         layer_in, normed, mixed, gains, bias, kept, arrived, middle, second, joined = saved[layer]
-        down_in = net.gather(gradient.astype(BF), seq_bits)
-        grad_joined, gated, partial = [], [], []
-        for part, joined_part in zip(stages(down_in), joined):
-            grad_part, gated_part, out = feed_backward(part, joined_part, pack)
-            grad_joined.append(grad_part)
-            gated.append(gated_part)
-            partial += out
-        grad_second = net.scatter(partial, seq_bits)
-        grad_hidden = hidden_weights(net, second, grad_joined, gated, down_in)
-        own_in, down_parts[layer] = scatter_hidden(net, grad_hidden, width // net.dp_n)
-        in_parts[layer] = restore_columns(net, own_in, seq_bits, unit)
+
+        def backward(n, blocks, joined=joined, pack=pack, final=final, sums=sums):
+            if n == 2 and not final:
+                blocks = [after(blocks[0], hidden_sums[layer + 1])] + blocks[1:]
+            grad_part, gated_part, parts = feed_backward(blocks, joined[n], pack)
+            return [grad_part, gated_part] + parts
+
+        held = seed_held if final and len(seq_bits) == 3 else None
+        down_in, outs = wave(net, low, backward, held)
+        grad_joined, gated = [out[0] for out in outs], [out[1] for out in outs]
+        second_sum = SumAll(net, [part for out in outs for part in out[2:]])
+        second_sum.step()
+        moved = second_sum.moving
+        second_sum.step()
+        joined_first = after(grad_joined[0], *second_sum.moving)
+        grad_hidden = hidden_weights(net, second, [joined_first] + grad_joined[1:], gated, down_in)
+        hidden_sums[layer] = lax.psum_scatter(
+            grad_hidden, "dp", scatter_dimension=0, tiled=True
+        )
+        if final:
+            final_sum.step(*moved)
+        parts = second_sum.parts()
+        parts[0] = after(parts[0], grad_hidden, *(final_sum.moving if final else []))
         gradient, gain_second, leaving, shares = out_backward(
-            net, gradient, grad_second, middle, norm_gains[layer, 1], m_out, arrived, rows_out
+            net, gradient, parts, middle, norm_gains[layer, 1], m_out, arrived, rows_out
         )
-        grad_out = net.scatter(shares, lo_bits)
-        grad_out = grad_out.reshape((net.dp_n, net.hi_n) + grad_out.shape[1:])
-        out_parts[layer] = net.scatter_rows(pick(grad_out, net.hi, 1), pick(grad_out, 1 - net.hi, 1))
+        if final:
+            final_sum.step(leaving[0])
         grad_heads = jnp.concatenate(net.trade(leaving, lo_bits), axis=0)
+        share_sum = SumLo(net, [x.reshape(-1, width) for x in shares])
+        share_sum.step()
+        grad_heads = after(grad_heads, *share_sum.moving)
+        out_sum = share_sum.parts()
         grad_query, grad_keys, grad_values, grad_gains, grad_pair = attend_backward(
             mixed, grad_heads, tables, gains, bias, kept
         )
-        grads = [grad_query, grad_keys, grad_values]
-        grad_normed = net.scatter(mixed_backward(grads, m_qkv, rows), lo_bits)
-        own_qkv = net.scatter_rows(*mixed_weights(net, normed, grads))
-        qkv_parts[layer] = restore_columns(net, own_qkv, lo_bits, local_width)
-        unused, first_pull = jax.vjp(rms_scale, layer_in, norm_gains[layer, 0])
-        grad_layer_in, gain_first = first_pull(grad_normed)
-        gradient = gradient + grad_layer_in
+        grads = [grad_query, after(grad_keys, *final_sum.moving) if final else grad_keys, grad_values]
+        if not final:
+            other_sums = attention_sums[layer + 1]
+            other_came = net.swap_hi(after(other_sums[1], leaving[0]))
+            grads[2] = after(grad_values, other_came)
+            total = other_sums[0].astype(F32) + other_came.astype(F32)
+            qkv_parts[layer + 1], out_parts[layer + 1] = split_pieces(
+                total, 3 * local_width, rows_out
+            )
+        last = layer == 0
+        mine, other = mixed_weights(net, normed, grads, out_sum, rows_out, F32 if last else BF)
+        if last:
+            sums = (mine, net.swap_hi(other))
+        else:
+            sent = [x.reshape(-1, x.shape[2]) for x in (mine, other)]
+            attention_sums[layer] = [
+                lax.psum_scatter(x, "dp", scatter_dimension=0, tiled=True) for x in sent
+            ]
+        grads[0] = after(grads[0], other)
+        normed_sum = SumLo(net, mixed_backward(grads, m_qkv, rows))
+        normed_sum.step()
+        gradient, low, gain_first = norm_backward(
+            gradient, normed_sum.parts(), layer_in, norm_gains[layer, 0]
+        )
         norm_parts[layer] = jnp.stack([gain_first, gain_second])
         qk_parts[layer] = grad_gains.reshape(-1, 2, 2, head_size).sum(axis=(0, 2))
         bias_parts[layer] = lax.dynamic_update_slice(
             jnp.zeros((2, heads), F32), grad_pair[:, 0, :2].T, (jnp.int32(0), head_start)
         )
-    input_grad = to_devices(gradient.astype(BF)).astype(F32)
+    both = SumBoth(net, *sums)
+    both.step()
+    final_sum.step(low)
+    qkv_parts[0], out_parts[0] = split_pieces(both.total(), 3 * local_width, rows_out)
+    for layer in range(layers):
+        in_parts[layer], down_parts[layer] = split_hidden(
+            hidden_sums[layer], width // net.dp_n, width
+        )
+    qkv_parts = return_rows(qkv_parts, "lo", lo_n)
+    in_parts = return_rows(in_parts, ("hi", "lo"), net.seq_n)
+    parts = final_sum.parts()
+    low_state = (saved[-1][7] + sum(x.astype(F32) for x in parts)).astype(BF)
+    layer_out = keep_own(low_state, net.swap_hi(low_state[tok_dev:]))
+    input_grad = keep_own(low, net.swap_hi(low[tok_dev:])).astype(F32)
     tops = best_scores.size
     small = jnp.concatenate(
         [best_scores.reshape(-1)]
         + [jnp.stack(part).reshape(-1) for part in (norm_parts, qk_parts, bias_parts)]
     )
+    small = after(small, both.own, hidden_sums[0])
     is_top = jnp.arange(small.size) < tops
     small = net.all_small(small, lambda a, b: jnp.where(is_top, jnp.maximum(a, b), a + b))
     best_scores = small[:tops].reshape(best_scores.shape)
@@ -1059,9 +1280,9 @@
     return (
         layer_out,
         input_grad,
-        jnp.stack(qkv_parts),
+        merge_columns(qkv_parts, layers, local_width),
         jnp.stack(out_parts),
-        jnp.stack(in_parts),
+        merge_columns(in_parts, layers, unit),
         jnp.stack(down_parts),
         norm_sum,
         qk_sum,

time: 770 us -> 670 us (0.87)
  other arithmetic: 70.5 us -> 25.4 us
  starting transfers between devices: 133 us -> 107 us
  Pallas kernels: 180 us -> 155 us
  waiting for transfers between devices: 260 us -> 240 us
  local copies, waits for them, and re-layouts: 98.2 us -> 114 us
    ppermute x18 -> x6, waiting for transfers between devices: 98.6 us -> 19.5 us  [shift_dp(): lax.ppermute(x, 'dp', [(i, (i + k + 1) % n) for i in range(n)])]
    unnamed x449 -> x495, local copies, waits for them, and re-layouts: 48.7 us -> 89.4 us
    ppermute x38 -> x27, waiting for transfers between devices: 69.5 us -> 100 us  [swap(): return lax.ppermute(x, 'hi', [(i, i ^ bit) for i in range(self.hi_n)])]
    all_gather x2 -> x3, waiting for transfers between devices: 0.01 us -> 20 us  [the longest x1 20 us: shards(): packs = [lax.all_gather(after(own_packs[0], *ring.by_dp), 'dp', axis=0)]]
    ppermute x38 -> x27, starting transfers between devices: 48.3 us -> 29 us  [swap(): return lax.ppermute(x, 'hi', [(i, i ^ bit) for i in range(self.hi_n)])]
    pallas_call x10 -> x0, Pallas kernels: 18.2 us -> none  [the longest x4 7.7 us: merge_columns(): pl.pallas_call(kernel, in_specs=[pl.BlockSpec(memory_space=pltpu.SMEM)] +...]
    ppermute x18 -> x6, starting transfers between devices: 25.9 us -> 8.55 us  [shift_dp(): lax.ppermute(x, 'dp', [(i, (i + k + 1) % n) for i in range(n)])]
    all_to_all x0 -> x4, waiting for transfers between devices: none -> 15.5 us  [the longest x1 9.87 us: shards(): in_came = lax.all_to_all(in_blocks, ('hi', 'lo'), 0, 0, tiled=True)]
  transfers between devices with their start and end apart: 183 -> 135, of which waited for: 61 -> 55; matrix products, arithmetic and copies ran while one was open for 16% -> 8% of each run, Pallas kernels for 23% -> 22%
where the time goes in v3:
time: 670 us; the launch traced here: 659 us
  waiting for transfers between devices  240 us (36%)
  Pallas kernels  155 us (23%)
  local copies, waits for them, and re-layouts  114 us (17%)
  starting transfers between devices  107 us (16%)
  other arithmetic  25.4 us (4%)
  between operations  17.4 us (3%)
    ppermute x27, waiting for transfers between devices, swap(): return lax.ppermute(x, 'hi', [(i, i ^ bit) for i in range(self.hi_n)])  100 us
    unnamed x495, local copies, waits for them, and re-layouts  89.4 us
    ppermute x89, waiting for transfers between devices, swap(): return lax.ppermute(x, 'lo', [(i, i ^ bit) for i in range(self.lo_n)])  80.3 us
    pallas_call x43, Pallas kernels, on_chip(): pl.pallas_call(kernel, in_specs=[SMEM] * len(first) + [VMEM] * len(arrays...  78.5 us
    ppermute x89, starting transfers between devices, swap(): return lax.ppermute(x, 'lo', [(i, i ^ bit) for i in range(self.lo_n)])  47 us
    pallas_call x2, Pallas kernels, attend_backward(): pl.pallas_call(functools.partial(attend_backward_kernel, min(256, length)...  33.1 us
    ppermute x27, starting transfers between devices, swap(): return lax.ppermute(x, 'hi', [(i, i ^ bit) for i in range(self.hi_n)])  29 us
    pallas_call x4, Pallas kernels, weight_call(): pl.pallas_call(body, in_specs=[SMEM] + [pl.BlockSpec(memory_space=pl.ANY)...  27.8 us
  transfers between devices with their start and end apart: 135, of which 55 were waited for; matrix products, arithmetic and copies ran while one was open for 8% of the time, Pallas kernels for 22%

profile of v3, /device:TPU:0, one launch (start us, length us, event | category | flops | bytes accessed | tf_op | source)
XLA Modules:
  0.0 658.7 jit_solution(7121070166169177772)
XLA Ops:
  33.6 9.9 %all-to-all-done.1 = bf16[8,64,1024]{2,1,0:T(8,128)(2,1)} async-done(((bf16[8,64,1024]{2,1,0:T(8,128)(2,1)}), bf16[8,64,1024]{2,1,0:T(8,128)(2,1)}, u32[]{:S(2)}, u32[]{:S(2)}) %all-to-all-start.1) | async-done | bytes 1048608 | tf_op jit(solution)/shard_map/all_to_all | solution.py:1097
  46.5 8.8 %collective-permute-done.3.refs_1_ = bf16[128,1024]{1,0:T(8,128)(2,1)S(1)} collective-permute-done((bf16[128,1024]{1,0:T(8,128)(2,1)S(1)}, bf16[128,1024]{1,0:T(8,128)(2,1)S(1)}, u32[]{:S(2)}, u32[]{:S(2)}) %collective-permute-start.3) | collective-permute-done | bytes 262176 | tf_op jit(solution)/shard_map/ppermute | solution.py:56
  63.7 6.9 %collective-permute-done.1.own_came = bf16[128,1024]{1,0:T(8,128)(2,1)S(1)} collective-permute-done((bf16[128,1024]{1,0:T(8,128)(2,1)S(1)}, bf16[128,1024]{1,0:T(8,128)(2,1)S(1)}, u32[]{:S(2)}, u32[]{:S(2)}) %collective-permute-start.1) | collective-permute-done | bytes 262176 | tf_op jit(solution)/shard_map/ppermute | solution.py:45
  77.0 12.5 %collective-permute-done.5.rest_came = bf16[384,1024]{1,0:T(8,128)(2,1)S(1)} collective-permute-done((bf16[384,1024]{1,0:T(8,128)(2,1)S(1)}, bf16[384,1024]{1,0:T(8,128)(2,1)S(1)}, u32[]{:S(2)}, u32[]{:S(2)}) %collective-permute-start.5) | collective-permute-done | bytes 786464 | tf_op jit(solution)/shard_map/ppermute | solution.py:45
  99.6 20.0 %all-gather.8.cloned.1.call-done = bf16[1536,1024]{1,0:T(8,128)(2,1)} async-done(((bf16[384,1024]{1,0:T(8,128)(2,1)}), bf16[1536,1024]{1,0:T(8,128)(2,1)}) %all-gather.8.cloned.1.call-update) | async-done | bytes 3145744 | tf_op jit(solution)/shard_map/all_gather | solution.py:1106
  121.4 7.6 %attend.2 = (bf16[1024,256]{1,0:T(8,128)(2,1)S(1)}, f32[4,1024,128]{2,1,0:T(8,128)S(1)}, f32[4,8,128]{2,1,0:T(8,128)S(1)}) custom-call(bf16[1024,768]{1,0:T(8,128)(2,1)S(1)} %copy-done.196, bf16[1024,768]{1,0:T(8,128)(2,1)S(1)} %copy-done.196, bf16[1024,768]{1,0:T(8,128)(2,1)S(1)} %copy-done.196, f32[1024,128]{1,0:T(8,128)S(1)} %pad_maximum_fusion.4.cosine, ...), custom_call_target="tpu_custom_call" | custom-call | flops 4294967296 | bytes 4194304 | tf_op jit(solution)/shard_map/attend/pallas_call | solution.py:927
  132.6 5.8 collective-permute-done.18
  148.3 7.9 %collective-permute-done.24.refs_3_.refs_4_ = bf16[256,1024]{1,0:T(8,128)(2,1)S(1)} collective-permute-done((bf16[256,1024]{1,0:T(8,128)(2,1)S(1)}, bf16[256,1024]{1,0:T(8,128)(2,1)S(1)}, u32[]{:S(2)}, u32[]{:S(2)}) %collective-permute-start.24) | collective-permute-done | bytes 524320 | tf_op jit(solution)/shard_map/ppermute | solution.py:45
  181.7 6.3 collective-permute-done.33.refs_5_
  191.6 10.8 %collective-permute-done.35.refs_3_ = bf16[256,1024]{1,0:T(8,128)(2,1)S(1)} collective-permute-done((bf16[256,1024]{1,0:T(8,128)(2,1)S(1)}, bf16[256,1024]{1,0:T(8,128)(2,1)S(1)}, u32[]{:S(2)}, u32[]{:S(2)}) %collective-permute-start.35) | collective-permute-done | bytes 524320 | tf_op jit(solution)/shard_map/ppermute | solution.py:45
  204.9 10.5 %collective-permute-done.40.refs_2_ = bf16[256,1024]{1,0:T(8,128)(2,1)S(1)} collective-permute-done((bf16[256,1024]{1,0:T(8,128)(2,1)S(1)}, bf16[256,1024]{1,0:T(8,128)(2,1)S(1)}, u32[]{:S(2)}, u32[]{:S(2)}) %collective-permute-start.40) | collective-permute-done | bytes 524320 | tf_op jit(solution)/shard_map/ppermute | solution.py:43
  221.4 4.4 collective-permute-done.42
  229.2 7.8 %attend.3 = (bf16[1024,256]{1,0:T(8,128)(2,1)S(1)}, f32[4,1024,128]{2,1,0:T(8,128)S(1)}, f32[4,8,128]{2,1,0:T(8,128)S(1)}) custom-call(bf16[1024,768]{1,0:T(8,128)(2,1)S(1)} %project.3.query_in.key_in.value_in, bf16[1024,768]{1,0:T(8,128)(2,1)S(1)} %project.3.query_in.key_in.value_in, bf16[1024,768]{1,0:T(8,128)(2,1)S(1)} %project.3.query_in.key_in.value_in, ...), custom_call_target="tpu_custom_call" | custom-call | flops 4294967296 | bytes 4194304 | tf_op jit(solution)/shard_map/attend/pallas_call | solution.py:927
  242.6 4.7 collective-permute-done.45
  282.6 5.0 feed_forward.10
  290.1 4.9 feed_backward.7
  308.3 6.6 collective-permute-done.70.refs_2_
  316.3 8.7 %hidden_weights.2 = bf16[1536,1024]{1,0:T(8,128)(2,1)S(1)} custom-call(s32[1]{0:T(128)} %bitcast.37.index.at, bf16[256,1024]{1,0:T(8,128)(2,1)} %get-tuple-element.225.refs_1_.refs_0_, bf16[256,1024]{1,0:T(8,128)(2,1)S(1)} %copy-done.164, bf16[256,1024]{1,0:T(8,128)(2,1)} %collective-permute-done.53.refs_1_.refs_2_, ...), custom_call_target="tpu_custom_call" | custom-call | flops 6442450944 | bytes 17825792 | tf_op jit(solution)/shard_map/hidden_weights/pallas_call | solution.py:561
  339.8 10.2 %collective-permute-done.73.refs_3_ = bf16[256,1024]{1,0:T(8,128)(2,1)S(1)} collective-permute-done((bf16[256,1024]{1,0:T(8,128)(2,1)S(1)}, bf16[256,1024]{1,0:T(8,128)(2,1)S(1)}, u32[]{:S(2)}, u32[]{:S(2)}) %collective-permute-start.73) | collective-permute-done | bytes 524320 | tf_op jit(solution)/shard_map/ppermute | solution.py:45
  358.3 5.6 collective-permute-done.77
  367.6 16.5 %attend_backward.2 = (bf16[1024,256]{1,0:T(8,128)(2,1)S(1)}, bf16[1024,256]{1,0:T(8,128)(2,1)S(1)}, bf16[1024,256]{1,0:T(8,128)(2,1)S(1)}, f32[2,2,128]{2,1,0:T(2,128)S(1)}, f32[4,8,128]{2,1,0:T(8,128)S(1)}) custom-call(bf16[1024,768]{1,0:T(8,128)(2,1)S(1)} %copy-done.199, bf16[1024,768]{1,0:T(8,128)(2,1)S(1)} %copy-done.199, ...), custom_call_target="tpu_custom_call" | custom-call | flops 10737418240 | bytes 6291456 | tf_op jit(solution)/shard_map/attend_backward/pallas_call | solution.py:965
  386.7 4.9 mixed_weights.2
  402.3 12.9 %collective-permute-done.84.refs_2_ = bf16[256,1024]{1,0:T(8,128)(2,1)S(1)} collective-permute-done((bf16[256,1024]{1,0:T(8,128)(2,1)S(1)}, bf16[256,1024]{1,0:T(8,128)(2,1)S(1)}, u32[]{:S(2)}, u32[]{:S(2)}) %collective-permute-start.84) | collective-permute-done | bytes 524320 | tf_op jit(solution)/shard_map/ppermute | solution.py:43
  428.2 5.3 collective-permute-done.89.refs_3_.refs_18_
  442.4 6.0 feed_backward.10
  469.0 6.2 collective-permute-done.95.refs_2_
  481.0 8.9 %hidden_weights.3 = bf16[1536,1024]{1,0:T(8,128)(2,1)S(1)} custom-call(s32[1]{0:T(128)} %bitcast.37.index.at, bf16[256,1024]{1,0:T(8,128)(2,1)S(1)} %copy-done.142, bf16[256,1024]{1,0:T(8,128)(2,1)S(1)} %copy-done.144, bf16[256,1024]{1,0:T(8,128)(2,1)S(1)} %copy-done.109, bf16[256,1024]{1,0:T(8,128)(2,1)S(1)} %copy-done.146, ...), custom_call_target="tpu_custom_call" | custom-call | flops 6442450944 | bytes 17825792 | tf_op jit(solution)/shard_map/hidden_weights/pallas_call | solution.py:561
  517.6 16.6 %attend_backward.3 = (bf16[1024,256]{1,0:T(8,128)(2,1)S(1)}, bf16[1024,256]{1,0:T(8,128)(2,1)S(1)}, bf16[1024,256]{1,0:T(8,128)(2,1)S(1)}, f32[2,2,128]{2,1,0:T(2,128)S(1)}, f32[4,8,128]{2,1,0:T(8,128)S(1)}) custom-call(bf16[1024,768]{1,0:T(8,128)(2,1)S(1)} %copy-done.197, bf16[1024,768]{1,0:T(8,128)(2,1)S(1)} %copy-done.197, ...), custom_call_target="tpu_custom_call" | custom-call | flops 10737418240 | bytes 6291456 | tf_op jit(solution)/shard_map/attend_backward/pallas_call | solution.py:965
  535.0 5.3 mixed_weights.3
  566.7 14.2 %collective-permute-done.115.y = bf16[4,128,1024]{2,1,0:T(8,128)(2,1)} collective-permute-done((bf16[4,128,1024]{2,1,0:T(8,128)(2,1)}, bf16[4,128,1024]{2,1,0:T(8,128)(2,1)}, u32[]{:S(2)}, u32[]{:S(2)}) %collective-permute-start.115) | collective-permute-done | bytes 1048608 | tf_op jit(solution)/shard_map/ppermute | solution.py:45
  596.2 9.3 %collective-permute-done.117 = bf16[128,1024]{1,0:T(8,128)(2,1)} collective-permute-done((bf16[128,1024]{1,0:T(8,128)(2,1)}, bf16[128,1024]{1,0:T(8,128)(2,1)}, u32[]{:S(2)}, u32[]{:S(2)}) %collective-permute-start.117) | collective-permute-done | bytes 262176 | tf_op jit(solution)/shard_map/ppermute | solution.py:56
  634.5 5.3 collective-permute-start.122
  (941 shorter events, 365.0 us)
Async XLA Ops:
  8.0 48.3 %collective-permute-start.12 = (s32[128,2]{0,1:T(2,128)S(1)}, s32[128,2]{0,1:T(2,128)S(1)}, u32[]{:S(2)}, u32[]{:S(2)}) collective-permute-start(s32[128,2]{0,1:T(2,128)S(1)} %bitcast.172), channel_id=1, source_target_pairs={{0,4},{4,0},{1,5},{5,1},{2,6},{6,2},{3,7},{7,3},{8,12},{12,8},{9,1... | collective-permute-start | bytes 3080 | tf_op jit(solution)/shard_map/ppermute | solution.py:45
  17.4 42.6 %collective-permute-start = (bf16[128,1024]{1,0:T(8,128)(2,1)S(1)}, bf16[128,1024]{1,0:T(8,128)(2,1)S(1)}, u32[]{:S(2)}, u32[]{:S(2)}) collective-permute-start(bf16[128,1024]{1,0:T(8,128)(2,1)S(1)} %get-tuple-element.398), channel_id=1, source_target_pairs={{0,4},{4,0},{1,5},{5,1},{2,6},{6,2},{3,7},{7,3},{8,12},{12,8},{9,1... | collective-permute-start | bytes 786440 | tf_op jit(solution)/shard_map/ppermute | solution.py:45
  23.8 19.7 %all-to-all-start.1 = ((bf16[8,64,1024]{2,1,0:T(8,128)(2,1)}), bf16[8,64,1024]{2,1,0:T(8,128)(2,1)}, u32[]{:S(2)}, u32[]{:S(2)}) async-start(bf16[8,64,1024]{2,1,0:T(8,128)(2,1)} %split_columns.3), calls=%async_computation.1 | async-start | bytes 2097152 | tf_op jit(solution)/shard_map/all_to_all | solution.py:1097
  28.0 91.6 %all-gather.8.cloned.1.call-start = ((), (), s32[]{:S(2)}) async-start(), calls=%async_computation.13 | async-start | bytes 3932160 | tf_op jit(solution)/shard_map/all_gather | solution.py:1106
  28.9 17.6 %collective-permute-start.4 = (bf16[128,1024]{1,0:T(8,128)(2,1)S(1)}, bf16[128,1024]{1,0:T(8,128)(2,1)S(1)}, u32[]{:S(2)}, u32[]{:S(2)}) collective-permute-start(bf16[128,1024]{1,0:T(8,128)(2,1)S(1)} %maximum_maximum_fusion.own), channel_id=1, source_target_pairs={{0,24},{8,0},{16,8},{24,16},{1,25},{9,1},{17,9},{25,17},{2,26},{10... | collective-permute-start | bytes 786440 | tf_op jit(solution)/shard_map/ppermute | solution.py:56
  32.6 22.8 %collective-permute-start.3 = (bf16[128,1024]{1,0:T(8,128)(2,1)S(1)}, bf16[128,1024]{1,0:T(8,128)(2,1)S(1)}, u32[]{:S(2)}, u32[]{:S(2)}) collective-permute-start(bf16[128,1024]{1,0:T(8,128)(2,1)S(1)} %maximum_maximum_fusion.own), channel_id=1, source_target_pairs={{0,16},{8,24},{16,0},{24,8},{1,17},{9,25},{17,1},{25,9},{2,18},{10... | collective-permute-start | bytes 786440 | tf_op jit(solution)/shard_map/ppermute | solution.py:56
  32.6 22.8 %collective-permute-start.2 = (bf16[128,1024]{1,0:T(8,128)(2,1)S(1)}, bf16[128,1024]{1,0:T(8,128)(2,1)S(1)}, u32[]{:S(2)}, u32[]{:S(2)}) collective-permute-start(bf16[128,1024]{1,0:T(8,128)(2,1)S(1)} %maximum_maximum_fusion.own), channel_id=1, source_target_pairs={{0,8},{8,16},{16,24},{24,0},{1,9},{9,17},{17,25},{25,1},{2,10},{10... | collective-permute-start | bytes 786440 | tf_op jit(solution)/shard_map/ppermute | solution.py:56
  55.4 115.6 %all-gather.6.cloned.1.call-start = ((), (), s32[]{:S(2)}) async-start(), calls=%async_computation.8 | async-start | bytes 2621440 | tf_op jit(solution)/shard_map/all_gather | solution.py:1146
  70.6 19.0 %collective-permute-start.5 = (bf16[384,1024]{1,0:T(8,128)(2,1)S(1)}, bf16[384,1024]{1,0:T(8,128)(2,1)S(1)}, u32[]{:S(2)}, u32[]{:S(2)}) collective-permute-start(bf16[384,1024]{1,0:T(8,128)(2,1)S(1)} %pad_maximum_fusion.1), channel_id=1, source_target_pairs={{0,4},{4,0},{1,5},{5,1},{2,6},{6,2},{3,7},{7,3},{8,12},{12,8},{9,1... | collective-permute-start | bytes 2359304 | tf_op jit(solution)/shard_map/ppermute | solution.py:45
  72.1 17.6 %collective-permute-start.9 = (bf16[256,1024]{1,0:T(8,128)(2,1)S(1)}, bf16[256,1024]{1,0:T(8,128)(2,1)S(1)}, u32[]{:S(2)}, u32[]{:S(2)}) collective-permute-start(bf16[256,1024]{1,0:T(8,128)(2,1)S(1)} %multiply_convert_fusion.refs_0_), channel_id=1, source_target_pairs={{0,1},{1,0},{2,3},{3,2},{4,5},{5,4},{6,7},{7,6},{8,9},{9,8},{10,11... | collective-permute-start | bytes 1572872 | tf_op jit(solution)/shard_map/ppermute | solution.py:43
  94.3 37.6 %collective-permute-start.7 = (bf16[8,128,256]{2,1,0:T(8,128)(2,1)S(1)}, bf16[8,128,256]{2,1,0:T(8,128)(2,1)S(1)}, u32[]{:S(2)}, u32[]{:S(2)}) collective-permute-start(bf16[8,128,256]{2,1,0:T(8,128)(2,1)S(1)} %slice.283.refs_0_), channel_id=1, source_target_pairs={{0,2},{1,3},{2,0},{3,1},{4,6},{5,7},{6,4},{7,5},{8,10},{9,11},{10,... | collective-permute-start | bytes 1572872 | tf_op jit(solution)/shard_map/ppermute | solution.py:43
  119.7 135.9 %all-gather.10.cloned.1.call-start = ((), (), s32[]{:S(2)}) async-start(), calls=%async_computation.14 | async-start | bytes 3932160 | tf_op jit(solution)/shard_map/all_gather | solution.py:1147
  171.0 284.4 %reduce-scatter.5.cloned.1.call-start = ((), (), s32[]{:S(2)}) async-start(), calls=%async_computation.9 | async-start | bytes 3932160 | tf_op jit(solution)/shard_map/reduce_scatter | solution.py:1198
  262.3 18.0 %collective-permute-start.48 = (bf16[256,1024]{1,0:T(8,128)(2,1)}, bf16[256,1024]{1,0:T(8,128)(2,1)S(1)}, u32[]{:S(2)}, u32[]{:S(2)}) collective-permute-start(bf16[256,1024]{1,0:T(8,128)(2,1)} %get-tuple-element.229.refs_1_.refs_14_), channel_id=1, source_target_pairs={{0,2},{1,3},{2,0},{3,1},{4,6},{5,7},{6,4},{7,5},{8,10},{9,11},{10,... | collective-permute-start | bytes 1572872 | tf_op jit(solution)/shard_map/ppermute | solution.py:43
  326.7 185.9 %reduce-scatter.7.cloned.1.call-start = ((), (), s32[]{:S(2)}) async-start(), calls=%async_computation.10 | async-start | bytes 1310720 | tf_op jit(solution)/shard_map/reduce_scatter | solution.py:1234
  364.2 21.0 %collective-permute-start.74 = (bf16[128,1024]{1,0:T(8,128)(2,1)S(1)}, bf16[128,1024]{1,0:T(8,128)(2,1)S(1)}, u32[]{:S(2)}, u32[]{:S(2)}) collective-permute-start(bf16[128,1024]{1,0:T(8,128)(2,1)S(1)} %get-tuple-element.271), channel_id=1, source_target_pairs={{0,4},{4,0},{1,5},{5,1},{2,6},{6,2},{3,7},{7,3},{8,12},{12,8},{9,1... | collective-permute-start | bytes 786440 | tf_op jit(solution)/shard_map/ppermute | solution.py:45
  365.2 20.7 %collective-permute-start.75 = (bf16[128,1024]{1,0:T(8,128)(2,1)S(1)}, bf16[128,1024]{1,0:T(8,128)(2,1)S(1)}, u32[]{:S(2)}, u32[]{:S(2)}) collective-permute-start(bf16[128,1024]{1,0:T(8,128)(2,1)S(1)} %get-tuple-element.274), channel_id=1, source_target_pairs={{0,2},{1,3},{2,0},{3,1},{4,6},{5,7},{6,4},{7,5},{8,10},{9,11},{10,... | collective-permute-start | bytes 786440 | tf_op jit(solution)/shard_map/ppermute | solution.py:43
  366.5 20.2 %collective-permute-start.81 = (bf16[256,1024]{1,0:T(8,128)(2,1)S(1)}, bf16[256,1024]{1,0:T(8,128)(2,1)S(1)}, u32[]{:S(2)}, u32[]{:S(2)}) collective-permute-start(bf16[256,1024]{1,0:T(8,128)(2,1)S(1)} %add_low.18), channel_id=1, source_target_pairs={{0,2},{1,3},{2,0},{3,1},{4,6},{5,7},{6,4},{7,5},{8,10},{9,11},{10,... | collective-permute-start | bytes 1572872 | tf_op jit(solution)/shard_map/ppermute | solution.py:43
  396.7 165.4 %reduce-scatter.9.cloned.1.call-start = ((), (), s32[]{:S(2)}) async-start(), calls=%async_computation.11 | async-start | bytes 1310720 | tf_op jit(solution)/shard_map/reduce_scatter | solution.py:1234
  434.9 188.9 %reduce-scatter.11.cloned.1.call-start = ((), (), s32[]{:S(2)}) async-start(), calls=%async_computation.12 | async-start | bytes 3932160 | tf_op jit(solution)/shard_map/reduce_scatter | solution.py:1198
  469.0 22.5 %collective-permute-start.96 = (bf16[256,1024]{1,0:T(8,128)(2,1)}, bf16[256,1024]{1,0:T(8,128)(2,1)}, u32[]{:S(2)}, u32[]{:S(2)}) collective-permute-start(bf16[256,1024]{1,0:T(8,128)(2,1)} %get-tuple-element.317), channel_id=1, source_target_pairs={{0,1},{1,0},{2,3},{3,2},{4,5},{5,4},{6,7},{7,6},{8,9},{9,8},{10,11... | collective-permute-start | bytes 1572872 | tf_op jit(solution)/shard_map/ppermute | solution.py:43
  512.7 21.5 %collective-permute-start.106 = (bf16[128,1024]{1,0:T(8,128)(2,1)}, bf16[128,1024]{1,0:T(8,128)(2,1)S(1)}, u32[]{:S(2)}, u32[]{:S(2)}) collective-permute-start(bf16[128,1024]{1,0:T(8,128)(2,1)} %reduce-scatter.7.cloned.1.call-done), channel_id=1, source_target_pairs={{0,4},{4,0},{1,5},{5,1},{2,6},{6,2},{3,7},{7,3},{8,12},{12,8},{9,1... | collective-permute-start | bytes 786440 | tf_op jit(solution)/shard_map/ppermute | solution.py:45
  515.1 19.2 %collective-permute-start.107 = (bf16[256,1024]{1,0:T(8,128)(2,1)S(1)}, bf16[256,1024]{1,0:T(8,128)(2,1)S(1)}, u32[]{:S(2)}, u32[]{:S(2)}) collective-permute-start(bf16[256,1024]{1,0:T(8,128)(2,1)S(1)} %add_low.22), channel_id=1, source_target_pairs={{0,2},{1,3},{2,0},{3,1},{4,6},{5,7},{6,4},{7,5},{8,10},{9,11},{10,... | collective-permute-start | bytes 1572872 | tf_op jit(solution)/shard_map/ppermute | solution.py:43
  554.7 26.1 %collective-permute-start.115 = (bf16[4,128,1024]{2,1,0:T(8,128)(2,1)}, bf16[4,128,1024]{2,1,0:T(8,128)(2,1)}, u32[]{:S(2)}, u32[]{:S(2)}) collective-permute-start(bf16[4,128,1024]{2,1,0:T(8,128)(2,1)} %copy-done.134), channel_id=1, source_target_pairs={{0,4},{4,0},{1,5},{5,1},{2,6},{6,2},{3,7},{7,3},{8,12},{12,8},{9,1... | collective-permute-start | bytes 3145736 | tf_op jit(solution)/shard_map/ppermute | solution.py:45
  557.4 30.3 %collective-permute-start.108 = (bf16[256,1024]{1,0:T(8,128)(2,1)}, bf16[256,1024]{1,0:T(8,128)(2,1)}, u32[]{:S(2)}, u32[]{:S(2)}) collective-permute-start(bf16[256,1024]{1,0:T(8,128)(2,1)} %copy-done.173), channel_id=1, source_target_pairs={{0,1},{1,0},{2,3},{3,2},{4,5},{5,4},{6,7},{7,6},{8,9},{9,8},{10,11... | collective-permute-start | bytes 1572872 | tf_op jit(solution)/shard_map/ppermute | solution.py:43
  560.8 26.9 %collective-permute-start.110 = (bf16[256,1024]{1,0:T(8,128)(2,1)}, bf16[256,1024]{1,0:T(8,128)(2,1)}, u32[]{:S(2)}, u32[]{:S(2)}) collective-permute-start(bf16[256,1024]{1,0:T(8,128)(2,1)} %add_low.23), channel_id=1, source_target_pairs={{0,2},{1,3},{2,0},{3,1},{4,6},{5,7},{6,4},{7,5},{8,10},{9,11},{10,... | collective-permute-start | bytes 1572872 | tf_op jit(solution)/shard_map/ppermute | solution.py:43
  583.9 21.5 %collective-permute-start.117 = (bf16[128,1024]{1,0:T(8,128)(2,1)}, bf16[128,1024]{1,0:T(8,128)(2,1)}, u32[]{:S(2)}, u32[]{:S(2)}) collective-permute-start(bf16[128,1024]{1,0:T(8,128)(2,1)} %get-tuple-element.353), channel_id=1, source_target_pairs={{0,16},{8,24},{16,0},{24,8},{1,17},{9,25},{17,1},{25,9},{2,18},{10... | collective-permute-start | bytes 786440 | tf_op jit(solution)/shard_map/ppermute | solution.py:56
  585.6 19.9 %collective-permute-start.118 = (bf16[128,1024]{1,0:T(8,128)(2,1)S(1)}, bf16[128,1024]{1,0:T(8,128)(2,1)}, u32[]{:S(2)}, u32[]{:S(2)}) collective-permute-start(bf16[128,1024]{1,0:T(8,128)(2,1)S(1)} %get-tuple-element.354), channel_id=1, source_target_pairs={{0,24},{8,0},{16,8},{24,16},{1,25},{9,1},{17,9},{25,17},{2,26},{10... | collective-permute-start | bytes 786440 | tf_op jit(solution)/shard_map/ppermute | solution.py:56
  590.7 21.1 %collective-permute-start.111 = (bf16[256,1024]{1,0:T(8,128)(2,1)}, bf16[256,1024]{1,0:T(8,128)(2,1)}, u32[]{:S(2)}, u32[]{:S(2)}) collective-permute-start(bf16[256,1024]{1,0:T(8,128)(2,1)} %get-tuple-element.347), channel_id=1, source_target_pairs={{0,2},{1,3},{2,0},{3,1},{4,6},{5,7},{6,4},{7,5},{8,10},{9,11},{10,... | collective-permute-start | bytes 1572872 | tf_op jit(solution)/shard_map/ppermute | solution.py:43
  592.0 19.8 %collective-permute-start.112 = (bf16[256,1024]{1,0:T(8,128)(2,1)S(1)}, bf16[256,1024]{1,0:T(8,128)(2,1)}, u32[]{:S(2)}, u32[]{:S(2)}) collective-permute-start(bf16[256,1024]{1,0:T(8,128)(2,1)S(1)} %copy-done.161), channel_id=1, source_target_pairs={{0,4},{4,0},{1,5},{5,1},{2,6},{6,2},{3,7},{7,3},{8,12},{12,8},{9,1... | collective-permute-start | bytes 1572872 | tf_op jit(solution)/shard_map/ppermute | solution.py:45
  595.3 24.8 %collective-permute-start.114 = (bf16[128,1024]{1,0:T(8,128)(2,1)}, bf16[128,1024]{1,0:T(8,128)(2,1)}, u32[]{:S(2)}, u32[]{:S(2)}) collective-permute-start(bf16[128,1024]{1,0:T(8,128)(2,1)} %get-tuple-element.379), channel_id=1, source_target_pairs={{0,4},{4,0},{1,5},{5,1},{2,6},{6,2},{3,7},{7,3},{8,12},{12,8},{9,1... | collective-permute-start | bytes 786440 | tf_op jit(solution)/shard_map/ppermute | solution.py:45
  630.8 19.0 %all-to-all-start.3 = ((bf16[8,64,1024]{2,1,0:T(8,128)(2,1)}), bf16[8,64,1024]{2,1,0:T(8,128)(2,1)S(1)}, u32[]{:S(2)}, u32[]{:S(2)}) async-start(bf16[8,64,1024]{2,1,0:T(8,128)(2,1)} %bitcast.65), calls=%async_computation.7 | async-start | bytes 2097152 | tf_op jit(solution)/shard_map/all_to_all | solution.py:302
  (348 other events, 3071.8 us)
Sparse Core Ops, SparseCore 0:
  55.5 64.0 all-gather.7
  121.2 44.6 all-gather.5
  171.2 61.4 all-gather.9
  326.8 58.0 reduce-scatter.4
  396.8 25.1 reduce-scatter.6
  435.0 24.9 reduce-scatter.8
  491.7 58.1 reduce-scatter.10

commit v4 on v3

--- a/solution.py
+++ b/solution.py
@@ -126,6 +126,7 @@
 class SumAll:
     def __init__(self, net, blocks):
         self.net, self.blocks, self.moving, self.step_n = net, blocks, [], 0
+        self.low = []
 
     def step(self, *earlier):
         net, bits = self.net, self.net.seq_bits
@@ -148,14 +149,11 @@
                 net.swap(after(bottom, *earlier), second),
             ]
         else:
-            top, bottom = self.moving
-            to_first, to_second = add_low(
+            top, bottom = (after(x, *earlier) for x in self.moving)
+            self.low = add_low(
                 [self.pairs[first], self.pairs[second]], [(half, bottom), (0, top)]
             )
-            self.moving = [
-                net.swap(after(to_first, *earlier), first),
-                net.swap(after(to_second, *earlier), second),
-            ]
+            self.moving = [net.swap(x, bit) for x, bit in zip(self.low, (first, second))]
 
     def parts(self):
         while self.step_n < 3:
@@ -296,10 +294,10 @@
     return [blocks[:, n].reshape(-1, columns) for n in range(layers)]
 
 
-def return_rows(layers, axes, count):
+def return_rows(layers, axes, count, *earlier):
     own = jnp.stack([x.astype(BF).reshape(count, -1, x.shape[1]) for x in layers], axis=1)
     own = own.reshape(count, -1, own.shape[-1])
-    return lax.all_to_all(own, axes, 0, 0, tiled=True)
+    return lax.all_to_all(after(own, *earlier), axes, 0, 0, tiled=True)
 
 
 def join_pieces(own, other, axis):
@@ -321,6 +319,7 @@
 VMEM = pl.BlockSpec(memory_space=pltpu.VMEM)
 SMEM = pl.BlockSpec(memory_space=pltpu.SMEM)
 LIMIT = 16 * 2**20
+WEIGHT_LIMIT = 32 * 2**20
 
 
 def on_chip(kernel, outs, *arrays, at=None, scratch=(), flops=0, name=None):
@@ -565,7 +564,7 @@
         out_shape=outs,
         scratch_shapes=[pltpu.VMEM(shape, BF) for shape in shapes]
         + [pltpu.SemaphoreType.DMA((len(flat),))],
-        compiler_params=pltpu.CompilerParams(vmem_limit_bytes=2 * LIMIT),
+        compiler_params=pltpu.CompilerParams(vmem_limit_bytes=WEIGHT_LIMIT),
         cost_estimate=pl.CostEstimate(flops=flops, bytes_accessed=moved, transcendentals=0),
         name=name,
     )(at.astype(jnp.int32).reshape(1), *flat)
@@ -947,7 +946,7 @@
             jax.ShapeDtypeStruct((heads, length, LANES), F32),
             jax.ShapeDtypeStruct((heads, 8, LANES), F32),
         ],
-        compiler_params=pltpu.CompilerParams(vmem_limit_bytes=LIMIT * max(1, length // 1024)),
+        compiler_params=pltpu.CompilerParams(vmem_limit_bytes=16 * 2**10 * max(1024, length)),
         cost_estimate=pl.CostEstimate(
             flops=8 * heads * length * length * LANES,
             bytes_accessed=16 * length * pairs * LANES,
@@ -996,7 +995,7 @@
             pltpu.VMEM((length, LANES), F32),
             pltpu.VMEM((length, LANES), F32),
         ],
-        compiler_params=pltpu.CompilerParams(vmem_limit_bytes=LIMIT * max(1, length // 1024)),
+        compiler_params=pltpu.CompilerParams(vmem_limit_bytes=16 * 2**10 * max(1024, length)),
         cost_estimate=pl.CostEstimate(
             flops=20 * heads * length * length * LANES,
             bytes_accessed=24 * length * pairs * LANES,
@@ -1099,11 +1098,12 @@
     ring = GatherBoth(net, join_pieces(own_qkv[0], w_out[0], 1))
     normed = rms_scale(state, norm_gains[0, 0]).astype(BF)
     normed_held = net.swap(normed, lo_bits[-1])
-    ring.step(tokens_came, ring.own_came)
+    ring.step()
     first_full = ring.finish()
     own_in = own_columns(in_came, layers)
     own_packs = [join_pieces(own_in[n], w_down[n], 0) for n in range(layers)]
-    packs = [lax.all_gather(after(own_packs[0], *ring.by_dp), "dp", axis=0)]
+    early = (*ring.by_dp, ring.own_came, tokens_came, normed_held)
+    packs = [lax.all_gather(after(own_packs[0], *early), "dp", axis=0)]
 
     pair = to_groups(jnp.stack([variate_ids, time_ids], axis=-1))
     pair = jnp.concatenate(net.gather(pair, lo_bits), axis=0)
@@ -1143,10 +1143,11 @@
         arrived = net.trade(jnp.split(leaving, lo_n, axis=0), lo_bits)
         if not final:
             own_next = in_order([own_next, came_next], net.hi).reshape(-1, own_next.shape[1])
-            full_next = lax.all_gather(after(own_next, packs[-1]), "dp", axis=0, tiled=True)
-            packs.append(lax.all_gather(after(own_packs[layer + 1], full_next), "dp", axis=0))
+            full_next = lax.all_gather(own_next, "dp", axis=0, tiled=True)
             full_next = full_next.reshape((net.dp_n * 2, -1) + full_next.shape[1:])
         middle, second = out_project(layer_in, arrived, m_out, norm_gains[layer, 1], net.lo)
+        if not final:
+            packs.append(lax.all_gather(after(own_packs[layer + 1], second), "dp", axis=0))
 
         def forward(n, blocks, pack=pack):
             joined, parts = feed_forward(blocks, pack)
@@ -1193,7 +1194,8 @@
         second_sum.step()
         moved = second_sum.moving
         second_sum.step()
-        joined_first = after(grad_joined[0], *second_sum.moving)
+        second_sum.step()
+        joined_first = after(grad_joined[0], *second_sum.low)
         grad_hidden = hidden_weights(net, second, [joined_first] + grad_joined[1:], gated, down_in)
         hidden_sums[layer] = lax.psum_scatter(
             grad_hidden, "dp", scatter_dimension=0, tiled=True
@@ -1236,8 +1238,9 @@
         grads[0] = after(grads[0], other)
         normed_sum = SumLo(net, mixed_backward(grads, m_qkv, rows))
         normed_sum.step()
+        parts = normed_sum.parts()
         gradient, low, gain_first = norm_backward(
-            gradient, normed_sum.parts(), layer_in, norm_gains[layer, 0]
+            gradient, parts, layer_in, norm_gains[layer, 0]
         )
         norm_parts[layer] = jnp.stack([gain_first, gain_second])
         qk_parts[layer] = grad_gains.reshape(-1, 2, 2, head_size).sum(axis=(0, 2))
@@ -1252,8 +1255,8 @@
         in_parts[layer], down_parts[layer] = split_hidden(
             hidden_sums[layer], width // net.dp_n, width
         )
-    qkv_parts = return_rows(qkv_parts, "lo", lo_n)
     in_parts = return_rows(in_parts, ("hi", "lo"), net.seq_n)
+    qkv_parts = return_rows(qkv_parts, "lo", lo_n, in_parts)
     parts = final_sum.parts()
     low_state = (saved[-1][7] + sum(x.astype(F32) for x in parts)).astype(BF)
     layer_out = keep_own(low_state, net.swap_hi(low_state[tok_dev:]))
@@ -1263,7 +1266,7 @@
         [best_scores.reshape(-1)]
         + [jnp.stack(part).reshape(-1) for part in (norm_parts, qk_parts, bias_parts)]
     )
-    small = after(small, both.own, hidden_sums[0])
+    small = after(small, *both.moving)
     is_top = jnp.arange(small.size) < tops
     small = net.all_small(small, lambda a, b: jnp.where(is_top, jnp.maximum(a, b), a + b))
     best_scores = small[:tops].reshape(best_scores.shape)

time: 670 us -> 658 us (0.982)
  waiting for transfers between devices: 240 us -> 208 us
  Pallas kernels: 155 us -> 165 us
  local copies, waits for them, and re-layouts: 114 us -> 124 us
    ppermute x27, waiting for transfers between devices: 100 us -> 55.3 us  [swap(): return lax.ppermute(x, 'hi', [(i, i ^ bit) for i in range(self.hi_n)])]
    ppermute x89, waiting for transfers between devices: 80.3 us -> 110 us  [swap(): return lax.ppermute(x, 'lo', [(i, i ^ bit) for i in range(self.lo_n)])]
    all_gather x3, waiting for transfers between devices: 20 us -> 0.84 us  [the longest x1 0.83 us: shards(): packs = [lax.all_gather(after(own_packs[0], *early), 'dp', axis=0)]]
    all_to_all x2, waiting for transfers between devices: 3.04 us -> 12.9 us  [return_rows(): return lax.all_to_all(after(own, *earlier), axes, 0, 0, tiled=True)]
    pallas_call x43, Pallas kernels: 78.5 us -> 86.7 us  [on_chip(): pl.pallas_call(kernel, in_specs=[SMEM] * len(first) + [VMEM] * len(arrays...]
    unnamed x495 -> x451, local copies, waits for them, and re-layouts: 89.4 us -> 93.7 us
  transfers between devices with their start and end apart: 135 -> 135, of which waited for: 55 -> 53; matrix products, arithmetic and copies ran while one was open for 8% -> 9% of each run, Pallas kernels for 22% -> 23%
where the time goes in v4:
time: 658 us; the launch traced here: 649 us
  waiting for transfers between devices  208 us (32%)
  Pallas kernels  165 us (25%)
  local copies, waits for them, and re-layouts  124 us (19%)
  starting transfers between devices  110 us (17%)
  other arithmetic  24.5 us (4%)
  between operations  17 us (3%)
    ppermute x89, waiting for transfers between devices, swap(): return lax.ppermute(x, 'lo', [(i, i ^ bit) for i in range(self.lo_n)])  110 us
    unnamed x451, local copies, waits for them, and re-layouts  93.7 us
    pallas_call x43, Pallas kernels, on_chip(): pl.pallas_call(kernel, in_specs=[SMEM] * len(first) + [VMEM] * len(arrays...  86.7 us
    ppermute x27, waiting for transfers between devices, swap(): return lax.ppermute(x, 'hi', [(i, i ^ bit) for i in range(self.hi_n)])  55.3 us
    ppermute x89, starting transfers between devices, swap(): return lax.ppermute(x, 'lo', [(i, i ^ bit) for i in range(self.lo_n)])  43.4 us
    pallas_call x2, Pallas kernels, attend_backward(): pl.pallas_call(functools.partial(attend_backward_kernel, min(256, length)...  33.6 us
    ppermute x27, starting transfers between devices, swap(): return lax.ppermute(x, 'hi', [(i, i ^ bit) for i in range(self.hi_n)])  30.2 us
    pallas_call x4, Pallas kernels, weight_call(): pl.pallas_call(body, in_specs=[SMEM] + [pl.BlockSpec(memory_space=pl.ANY)...  28.8 us
  transfers between devices with their start and end apart: 135, of which 53 were waited for; matrix products, arithmetic and copies ran while one was open for 9% of the time, Pallas kernels for 23%

profile of v4, /device:TPU:0, one launch (start us, length us, event | category | flops | bytes accessed | tf_op | source)
XLA Modules:
  0.0 648.5 jit_solution(1386679311100282919)
XLA Ops:
  35.3 5.6 all-to-all-done.1
  44.4 10.7 %collective-permute-done.3.refs_1_ = bf16[128,1024]{1,0:T(8,128)(2,1)S(1)} collective-permute-done((bf16[128,1024]{1,0:T(8,128)(2,1)S(1)}, bf16[128,1024]{1,0:T(8,128)(2,1)S(1)}, u32[]{:S(2)}, u32[]{:S(2)}) %collective-permute-start.3) | collective-permute-done | bytes 262176 | tf_op jit(solution)/shard_map/ppermute | solution.py:56
  65.9 15.4 %collective-permute-done.5.rest_came = bf16[384,1024]{1,0:T(8,128)(2,1)S(1)} collective-permute-done((bf16[384,1024]{1,0:T(8,128)(2,1)S(1)}, bf16[384,1024]{1,0:T(8,128)(2,1)S(1)}, u32[]{:S(2)}, u32[]{:S(2)}) %collective-permute-start.5) | collective-permute-done | bytes 786464 | tf_op jit(solution)/shard_map/ppermute | solution.py:45
  86.6 4.4 collective-permute-done.16
  94.1 7.6 %attend.2 = (bf16[1024,256]{1,0:T(8,128)(2,1)S(1)}, f32[4,1024,128]{2,1,0:T(8,128)S(1)}, f32[4,8,128]{2,1,0:T(8,128)S(1)}) custom-call(bf16[1024,768]{1,0:T(8,128)(2,1)S(1)} %copy-done.173, bf16[1024,768]{1,0:T(8,128)(2,1)S(1)} %copy-done.173, bf16[1024,768]{1,0:T(8,128)(2,1)S(1)} %copy-done.173, f32[1024,128]{1,0:T(8,128)S(1)} %pad_maximum_fusion.4.cosine, ...), custom_call_target="tpu_custom_call" | custom-call | flops 4294967296 | bytes 4194304 | tf_op jit(solution)/shard_map/attend/pallas_call | solution.py:926
  104.2 5.8 collective-permute-done.18
  133.5 5.4 feed_forward.7
  157.7 5.3 collective-permute-done.33.refs_5_
  166.8 10.9 %collective-permute-done.34.refs_2_ = bf16[256,1024]{1,0:T(8,128)(2,1)S(1)} collective-permute-done((bf16[256,1024]{1,0:T(8,128)(2,1)S(1)}, bf16[256,1024]{1,0:T(8,128)(2,1)S(1)}, u32[]{:S(2)}, u32[]{:S(2)}) %collective-permute-start.34) | collective-permute-done | bytes 524320 | tf_op jit(solution)/shard_map/ppermute | solution.py:43
  181.8 10.7 %collective-permute-done.40.refs_2_ = bf16[256,1024]{1,0:T(8,128)(2,1)S(1)} collective-permute-done((bf16[256,1024]{1,0:T(8,128)(2,1)}, bf16[256,1024]{1,0:T(8,128)(2,1)S(1)}, u32[]{:S(2)}, u32[]{:S(2)}) %collective-permute-start.40) | collective-permute-done | bytes 524320 | tf_op jit(solution)/shard_map/ppermute | solution.py:43
  210.9 8.1 %attend.3 = (bf16[1024,256]{1,0:T(8,128)(2,1)S(1)}, f32[4,1024,128]{2,1,0:T(8,128)S(1)}, f32[4,8,128]{2,1,0:T(8,128)S(1)}) custom-call(bf16[1024,768]{1,0:T(8,128)(2,1)S(1)} %project.3.query_in.key_in.value_in, bf16[1024,768]{1,0:T(8,128)(2,1)S(1)} %project.3.query_in.key_in.value_in, bf16[1024,768]{1,0:T(8,128)(2,1)S(1)} %project.3.query_in.key_in.value_in, ...), custom_call_target="tpu_custom_call" | custom-call | flops 4294967296 | bytes 4194304 | tf_op jit(solution)/shard_map/attend/pallas_call | solution.py:926
  223.7 4.5 collective-permute-done.45
  243.1 5.3 collective-permute-done.55.refs_3_.refs_4_
  263.5 5.0 feed_forward.10
  271.5 4.7 feed_backward.7
  288.9 6.9 %collective-permute-done.70.refs_5_ = bf16[128,1024]{1,0:T(8,128)(2,1)S(1)} collective-permute-done((bf16[128,1024]{1,0:T(8,128)(2,1)S(1)}, bf16[128,1024]{1,0:T(8,128)(2,1)S(1)}, u32[]{:S(2)}, u32[]{:S(2)}) %collective-permute-start.70) | collective-permute-done | bytes 262176 | tf_op jit(solution)/shard_map/ppermute | solution.py:43
  298.2 8.8 %hidden_weights.2 = bf16[1536,1024]{1,0:T(8,128)(2,1)S(1)} custom-call(s32[1]{0:T(128)} %bitcast.37.index.at, bf16[256,1024]{1,0:T(8,128)(2,1)} %get-tuple-element.222.refs_1_.refs_0_, bf16[256,1024]{1,0:T(8,128)(2,1)} %collective-permute-done.47.refs_2_.refs_1_, bf16[256,1024]{1,0:T(8,128)(2,1)} %collective-permute-done.53.refs_1_.refs_2_, ...), custom_call_target="tpu_custom_call" | custom-call | flops 6442450944 | bytes 17825792 | tf_op jit(solution)/shard_map/hidden_weights/pallas_call | solution.py:560
  316.2 10.0 %collective-permute-done.72.refs_2_ = bf16[256,1024]{1,0:T(8,128)(2,1)S(1)} collective-permute-done((bf16[256,1024]{1,0:T(8,128)(2,1)}, bf16[256,1024]{1,0:T(8,128)(2,1)S(1)}, u32[]{:S(2)}, u32[]{:S(2)}) %collective-permute-start.72) | collective-permute-done | bytes 524320 | tf_op jit(solution)/shard_map/ppermute | solution.py:43
  339.3 5.6 collective-permute-done.76
  348.3 16.8 %attend_backward.2 = (bf16[1024,256]{1,0:T(8,128)(2,1)S(1)}, bf16[1024,256]{1,0:T(8,128)(2,1)S(1)}, bf16[1024,256]{1,0:T(8,128)(2,1)S(1)}, f32[2,2,128]{2,1,0:T(2,128)S(1)}, f32[4,8,128]{2,1,0:T(8,128)S(1)}) custom-call(bf16[1024,768]{1,0:T(8,128)(2,1)S(1)} %copy-done.176, bf16[1024,768]{1,0:T(8,128)(2,1)S(1)} %copy-done.176, ...), custom_call_target="tpu_custom_call" | custom-call | flops 10737418240 | bytes 6291456 | tf_op jit(solution)/shard_map/attend_backward/pallas_call | solution.py:964
  367.7 5.7 mixed_weights.2
  379.1 12.3 %collective-permute-done.84.refs_2_ = bf16[256,1024]{1,0:T(8,128)(2,1)S(1)} collective-permute-done((bf16[256,1024]{1,0:T(8,128)(2,1)S(1)}, bf16[256,1024]{1,0:T(8,128)(2,1)S(1)}, u32[]{:S(2)}, u32[]{:S(2)}) %collective-permute-start.84) | collective-permute-done | bytes 524320 | tf_op jit(solution)/shard_map/ppermute | solution.py:43
  414.5 6.9 %feed_backward.10 = (bf16[1024,1024]{1,0:T(8,128)(2,1)S(1)}, bf16[1024,512]{1,0:T(8,128)(2,1)S(1)}, bf16[256,1024]{1,0:T(8,128)(2,1)S(1)}, bf16[256,1024]{1,0:T(...) custom-call(bf16[4,384,1024]{2,1,0:T(8,128)(2,1)S(1)} %bitcast.135, ...), custom_call_target="tpu_custom_call" | custom-call | flops 3221225472 | bytes 12582912 | tf_op jit(solution)/shard_map/feed_backward/pallas_call | solution.py:329
  445.3 6.7 %collective-permute-done.97.refs_5_ = bf16[128,1024]{1,0:T(8,128)(2,1)S(1)} collective-permute-done((bf16[128,1024]{1,0:T(8,128)(2,1)S(1)}, bf16[128,1024]{1,0:T(8,128)(2,1)S(1)}, u32[]{:S(2)}, u32[]{:S(2)}) %collective-permute-start.97) | collective-permute-done | bytes 262176 | tf_op jit(solution)/shard_map/ppermute | solution.py:43
  465.6 9.1 %hidden_weights.3 = bf16[1536,1024]{1,0:T(8,128)(2,1)S(1)} custom-call(s32[1]{0:T(128)} %bitcast.37.index.at, bf16[256,1024]{1,0:T(8,128)(2,1)} %get-tuple-element.195.refs_1_.refs_0_, bf16[256,1024]{1,0:T(8,128)(2,1)S(1)} %copy-done.128, bf16[256,1024]{1,0:T(8,128)(2,1)} %collective-permute-done.22.refs_1_.refs_2_, bf16[256,1024]{1,0:T(8,128)(2,1)S(1)} %copy-done.130, ...), custom_call_target="tpu_custom_call" | custom-call | flops 6442450944 | bytes 17825792 | tf_op jit(solution)/shard_map/hidden_weights/pallas_call | solution.py:560
  480.8 4.4 out_backward.3
  503.5 16.8 %attend_backward.3 = (bf16[1024,256]{1,0:T(8,128)(2,1)S(1)}, bf16[1024,256]{1,0:T(8,128)(2,1)S(1)}, bf16[1024,256]{1,0:T(8,128)(2,1)S(1)}, f32[2,2,128]{2,1,0:T(2,128)S(1)}, f32[4,8,128]{2,1,0:T(8,128)S(1)}) custom-call(bf16[1024,768]{1,0:T(8,128)(2,1)S(1)} %copy-done.174, bf16[1024,768]{1,0:T(8,128)(2,1)S(1)} %copy-done.174, ...), custom_call_target="tpu_custom_call" | custom-call | flops 10737418240 | bytes 6291456 | tf_op jit(solution)/shard_map/attend_backward/pallas_call | solution.py:964
  521.1 5.2 mixed_weights.3
  543.8 15.7 %collective-permute-done.115.y = bf16[4,128,1024]{2,1,0:T(8,128)(2,1)} collective-permute-done((bf16[4,128,1024]{2,1,0:T(8,128)(2,1)}, bf16[4,128,1024]{2,1,0:T(8,128)(2,1)}, u32[]{:S(2)}, u32[]{:S(2)}) %collective-permute-start.115) | collective-permute-done | bytes 1048608 | tf_op jit(solution)/shard_map/ppermute | solution.py:45
  575.6 8.3 %collective-permute-done.117 = bf16[128,1024]{1,0:T(8,128)(2,1)S(1)} collective-permute-done((bf16[128,1024]{1,0:T(8,128)(2,1)}, bf16[128,1024]{1,0:T(8,128)(2,1)S(1)}, u32[]{:S(2)}, u32[]{:S(2)}) %collective-permute-start.117) | collective-permute-done | bytes 262176 | tf_op jit(solution)/shard_map/ppermute | solution.py:56
  593.6 5.1 collective-permute-start.122
  620.6 9.1 %all-to-all-done.2.ref = bf16[8,64,1024]{2,1,0:T(8,128)(2,1)S(1)} async-done(((bf16[8,64,1024]{2,1,0:T(8,128)(2,1)}), bf16[8,64,1024]{2,1,0:T(8,128)(2,1)S(1)}, u32[]{:S(2)}, u32[]{:S(2)}) %all-to-all-start.2) | async-done | bytes 1048608 | tf_op jit(solution)/shard_map/all_to_all | solution.py:300
  (896 shorter events, 368.9 us)
Async XLA Ops:
  20.6 20.2 %all-to-all-start.1 = ((bf16[8,64,1024]{2,1,0:T(8,128)(2,1)}), bf16[8,64,1024]{2,1,0:T(8,128)(2,1)}, u32[]{:S(2)}, u32[]{:S(2)}) async-start(bf16[8,64,1024]{2,1,0:T(8,128)(2,1)} %split_columns.3), calls=%async_computation.1 | async-start | bytes 2097152 | tf_op jit(solution)/shard_map/all_to_all | solution.py:1096
  24.9 93.4 %all-gather.8.cloned.1.call-start = ((), (), s32[]{:S(2)}) async-start(), calls=%async_computation.13 | async-start | bytes 3932160 | tf_op jit(solution)/shard_map/all_gather | solution.py:1106
  25.4 29.7 %collective-permute-start.10 = (bf16[256,1024]{1,0:T(8,128)(2,1)S(1)}, bf16[256,1024]{1,0:T(8,128)(2,1)S(1)}, u32[]{:S(2)}, u32[]{:S(2)}) collective-permute-start(bf16[256,1024]{1,0:T(8,128)(2,1)S(1)} %multiply_convert_fusion.refs_0_), channel_id=1, source_target_pairs={{0,2},{1,3},{2,0},{3,1},{4,6},{5,7},{6,4},{7,5},{8,10},{9,11},{10,... | collective-permute-start | bytes 1572872 | tf_op jit(solution)/shard_map/ppermute | solution.py:43
  32.8 22.3 %collective-permute-start.3 = (bf16[128,1024]{1,0:T(8,128)(2,1)S(1)}, bf16[128,1024]{1,0:T(8,128)(2,1)S(1)}, u32[]{:S(2)}, u32[]{:S(2)}) collective-permute-start(bf16[128,1024]{1,0:T(8,128)(2,1)S(1)} %maximum_maximum_fusion.own), channel_id=1, source_target_pairs={{0,16},{8,24},{16,0},{24,8},{1,17},{9,25},{17,1},{25,9},{2,18},{10... | collective-permute-start | bytes 786440 | tf_op jit(solution)/shard_map/ppermute | solution.py:56
  32.8 22.3 %collective-permute-start.2 = (bf16[128,1024]{1,0:T(8,128)(2,1)S(1)}, bf16[128,1024]{1,0:T(8,128)(2,1)S(1)}, u32[]{:S(2)}, u32[]{:S(2)}) collective-permute-start(bf16[128,1024]{1,0:T(8,128)(2,1)S(1)} %maximum_maximum_fusion.own), channel_id=1, source_target_pairs={{0,8},{8,16},{16,24},{24,0},{1,9},{9,17},{17,25},{25,1},{2,10},{10... | collective-permute-start | bytes 786440 | tf_op jit(solution)/shard_map/ppermute | solution.py:56
  33.8 21.3 %collective-permute-start.1 = (bf16[128,1024]{1,0:T(8,128)(2,1)S(1)}, bf16[128,1024]{1,0:T(8,128)(2,1)S(1)}, u32[]{:S(2)}, u32[]{:S(2)}) collective-permute-start(bf16[128,1024]{1,0:T(8,128)(2,1)S(1)} %maximum_maximum_fusion.own), channel_id=1, source_target_pairs={{0,4},{4,0},{1,5},{5,1},{2,6},{6,2},{3,7},{7,3},{8,12},{12,8},{9,1... | collective-permute-start | bytes 786440 | tf_op jit(solution)/shard_map/ppermute | solution.py:45
  55.1 142.3 %all-gather.6.cloned.1.call-start = ((), (), s32[]{:S(2)}) async-start(), calls=%async_computation.8 | async-start | bytes 2621440 | tf_op jit(solution)/shard_map/all_gather | solution.py:1146
  61.6 19.7 %collective-permute-start.5 = (bf16[384,1024]{1,0:T(8,128)(2,1)S(1)}, bf16[384,1024]{1,0:T(8,128)(2,1)S(1)}, u32[]{:S(2)}, u32[]{:S(2)}) collective-permute-start(bf16[384,1024]{1,0:T(8,128)(2,1)S(1)} %pad_maximum_fusion.1), channel_id=1, source_target_pairs={{0,4},{4,0},{1,5},{5,1},{2,6},{6,2},{3,7},{7,3},{8,12},{12,8},{9,1... | collective-permute-start | bytes 2359304 | tf_op jit(solution)/shard_map/ppermute | solution.py:45
  63.1 18.3 %collective-permute-start.9 = (bf16[256,1024]{1,0:T(8,128)(2,1)S(1)}, bf16[256,1024]{1,0:T(8,128)(2,1)S(1)}, u32[]{:S(2)}, u32[]{:S(2)}) collective-permute-start(bf16[256,1024]{1,0:T(8,128)(2,1)S(1)} %multiply_convert_fusion.refs_0_), channel_id=1, source_target_pairs={{0,1},{1,0},{2,3},{3,2},{4,5},{5,4},{6,7},{7,6},{8,9},{9,8},{10,11... | collective-permute-start | bytes 1572872 | tf_op jit(solution)/shard_map/ppermute | solution.py:43
  63.2 18.2 %collective-permute-start.11 = (bf16[256,1024]{1,0:T(8,128)(2,1)S(1)}, bf16[256,1024]{1,0:T(8,128)(2,1)S(1)}, u32[]{:S(2)}, u32[]{:S(2)}) collective-permute-start(bf16[256,1024]{1,0:T(8,128)(2,1)S(1)} %collective-permute-done.10.refs_2_), channel_id=1, source_target_pairs={{0,1},{1,0},{2,3},{3,2},{4,5},{5,4},{6,7},{7,6},{8,9},{9,8},{10,11... | collective-permute-start | bytes 1572872 | tf_op jit(solution)/shard_map/ppermute | solution.py:43
  92.1 144.0 %all-gather.10.cloned.1.call-start = ((), (), s32[]{:S(2)}) async-start(), calls=%async_computation.14 | async-start | bytes 3932160 | tf_op jit(solution)/shard_map/all_gather | solution.py:1150
  145.9 280.8 %reduce-scatter.5.cloned.1.call-start = ((), (), s32[]{:S(2)}) async-start(), calls=%async_computation.9 | async-start | bytes 3932160 | tf_op jit(solution)/shard_map/reduce_scatter | solution.py:1200
  242.0 19.0 %collective-permute-start.48 = (bf16[256,1024]{1,0:T(8,128)(2,1)}, bf16[256,1024]{1,0:T(8,128)(2,1)S(1)}, u32[]{:S(2)}, u32[]{:S(2)}) collective-permute-start(bf16[256,1024]{1,0:T(8,128)(2,1)} %get-tuple-element.226.refs_1_.refs_14_), channel_id=1, source_target_pairs={{0,2},{1,3},{2,0},{3,1},{4,6},{5,7},{6,4},{7,5},{8,10},{9,11},{10,... | collective-permute-start | bytes 1572872 | tf_op jit(solution)/shard_map/ppermute | solution.py:43
  308.8 188.2 %reduce-scatter.7.cloned.1.call-start = ((), (), s32[]{:S(2)}) async-start(), calls=%async_computation.10 | async-start | bytes 1310720 | tf_op jit(solution)/shard_map/reduce_scatter | solution.py:1236
  345.1 21.2 %collective-permute-start.74 = (bf16[128,1024]{1,0:T(8,128)(2,1)S(1)}, bf16[128,1024]{1,0:T(8,128)(2,1)S(1)}, u32[]{:S(2)}, u32[]{:S(2)}) collective-permute-start(bf16[128,1024]{1,0:T(8,128)(2,1)S(1)} %get-tuple-element.268), channel_id=1, source_target_pairs={{0,4},{4,0},{1,5},{5,1},{2,6},{6,2},{3,7},{7,3},{8,12},{12,8},{9,1... | collective-permute-start | bytes 786440 | tf_op jit(solution)/shard_map/ppermute | solution.py:45
  345.9 21.1 %collective-permute-start.80 = (bf16[128,1024]{1,0:T(8,128)(2,1)S(1)}, bf16[128,1024]{1,0:T(8,128)(2,1)S(1)}, u32[]{:S(2)}, u32[]{:S(2)}) collective-permute-start(bf16[128,1024]{1,0:T(8,128)(2,1)S(1)} %get-tuple-element.280), channel_id=1, source_target_pairs={{0,2},{1,3},{2,0},{3,1},{4,6},{5,7},{6,4},{7,5},{8,10},{9,11},{10,... | collective-permute-start | bytes 786440 | tf_op jit(solution)/shard_map/ppermute | solution.py:43
  347.7 20.0 %collective-permute-start.81 = (bf16[256,1024]{1,0:T(8,128)(2,1)S(1)}, bf16[256,1024]{1,0:T(8,128)(2,1)S(1)}, u32[]{:S(2)}, u32[]{:S(2)}) collective-permute-start(bf16[256,1024]{1,0:T(8,128)(2,1)S(1)} %add_low.17), channel_id=1, source_target_pairs={{0,2},{1,3},{2,0},{3,1},{4,6},{5,7},{6,4},{7,5},{8,10},{9,11},{10,... | collective-permute-start | bytes 1572872 | tf_op jit(solution)/shard_map/ppermute | solution.py:43
  396.6 143.7 %reduce-scatter.9.cloned.1.call-start = ((), (), s32[]{:S(2)}) async-start(), calls=%async_computation.11 | async-start | bytes 1310720 | tf_op jit(solution)/shard_map/reduce_scatter | solution.py:1236
  439.7 168.9 %reduce-scatter.11.cloned.1.call-start = ((), (), s32[]{:S(2)}) async-start(), calls=%async_computation.12 | async-start | bytes 3932160 | tf_op jit(solution)/shard_map/reduce_scatter | solution.py:1200
  445.3 31.1 %collective-permute-start.98 = (bf16[256,1024]{1,0:T(8,128)(2,1)}, bf16[256,1024]{1,0:T(8,128)(2,1)}, u32[]{:S(2)}, u32[]{:S(2)}) collective-permute-start(bf16[256,1024]{1,0:T(8,128)(2,1)} %copy-done.143), channel_id=1, source_target_pairs={{0,1},{1,0},{2,3},{3,2},{4,5},{5,4},{6,7},{7,6},{8,9},{9,8},{10,11... | collective-permute-start | bytes 1572872 | tf_op jit(solution)/shard_map/ppermute | solution.py:43
  456.8 19.7 %collective-permute-start.99 = (bf16[256,1024]{1,0:T(8,128)(2,1)}, bf16[256,1024]{1,0:T(8,128)(2,1)}, u32[]{:S(2)}, u32[]{:S(2)}) collective-permute-start(bf16[256,1024]{1,0:T(8,128)(2,1)} %get-tuple-element.310), channel_id=1, source_target_pairs={{0,2},{1,3},{2,0},{3,1},{4,6},{5,7},{6,4},{7,5},{8,10},{9,11},{10,... | collective-permute-start | bytes 1572872 | tf_op jit(solution)/shard_map/ppermute | solution.py:43
  496.9 23.4 %collective-permute-start.106 = (bf16[128,1024]{1,0:T(8,128)(2,1)}, bf16[128,1024]{1,0:T(8,128)(2,1)S(1)}, u32[]{:S(2)}, u32[]{:S(2)}) collective-permute-start(bf16[128,1024]{1,0:T(8,128)(2,1)} %reduce-scatter.7.cloned.1.call-done), channel_id=1, source_target_pairs={{0,4},{4,0},{1,5},{5,1},{2,6},{6,2},{3,7},{7,3},{8,12},{12,8},{9,1... | collective-permute-start | bytes 786440 | tf_op jit(solution)/shard_map/ppermute | solution.py:45
  499.3 21.1 %collective-permute-start.107 = (bf16[256,1024]{1,0:T(8,128)(2,1)S(1)}, bf16[256,1024]{1,0:T(8,128)(2,1)S(1)}, u32[]{:S(2)}, u32[]{:S(2)}) collective-permute-start(bf16[256,1024]{1,0:T(8,128)(2,1)S(1)} %add_low.21), channel_id=1, source_target_pairs={{0,2},{1,3},{2,0},{3,1},{4,6},{5,7},{6,4},{7,5},{8,10},{9,11},{10,... | collective-permute-start | bytes 1572872 | tf_op jit(solution)/shard_map/ppermute | solution.py:43
  533.3 26.1 %collective-permute-start.115 = (bf16[4,128,1024]{2,1,0:T(8,128)(2,1)}, bf16[4,128,1024]{2,1,0:T(8,128)(2,1)}, u32[]{:S(2)}, u32[]{:S(2)}) collective-permute-start(bf16[4,128,1024]{2,1,0:T(8,128)(2,1)} %copy-done.119), channel_id=1, source_target_pairs={{0,4},{4,0},{1,5},{5,1},{2,6},{6,2},{3,7},{7,3},{8,12},{12,8},{9,1... | collective-permute-start | bytes 3145736 | tf_op jit(solution)/shard_map/ppermute | solution.py:45
  535.7 32.8 %collective-permute-start.108 = (bf16[256,1024]{1,0:T(8,128)(2,1)}, bf16[256,1024]{1,0:T(8,128)(2,1)}, u32[]{:S(2)}, u32[]{:S(2)}) collective-permute-start(bf16[256,1024]{1,0:T(8,128)(2,1)} %copy-done.153), channel_id=1, source_target_pairs={{0,1},{1,0},{2,3},{3,2},{4,5},{5,4},{6,7},{7,6},{8,9},{9,8},{10,11... | collective-permute-start | bytes 1572872 | tf_op jit(solution)/shard_map/ppermute | solution.py:43
  539.1 29.4 %collective-permute-start.110 = (bf16[256,1024]{1,0:T(8,128)(2,1)}, bf16[256,1024]{1,0:T(8,128)(2,1)}, u32[]{:S(2)}, u32[]{:S(2)}) collective-permute-start(bf16[256,1024]{1,0:T(8,128)(2,1)} %add_low.22), channel_id=1, source_target_pairs={{0,2},{1,3},{2,0},{3,1},{4,6},{5,7},{6,4},{7,5},{8,10},{9,11},{10,... | collective-permute-start | bytes 1572872 | tf_op jit(solution)/shard_map/ppermute | solution.py:43
  563.0 20.8 %collective-permute-start.117 = (bf16[128,1024]{1,0:T(8,128)(2,1)}, bf16[128,1024]{1,0:T(8,128)(2,1)S(1)}, u32[]{:S(2)}, u32[]{:S(2)}) collective-permute-start(bf16[128,1024]{1,0:T(8,128)(2,1)} %get-tuple-element.350), channel_id=1, source_target_pairs={{0,16},{8,24},{16,0},{24,8},{1,17},{9,25},{17,1},{25,9},{2,18},{10... | collective-permute-start | bytes 786440 | tf_op jit(solution)/shard_map/ppermute | solution.py:56
  565.5 18.3 %collective-permute-start.118 = (bf16[128,1024]{1,0:T(8,128)(2,1)S(1)}, bf16[128,1024]{1,0:T(8,128)(2,1)}, u32[]{:S(2)}, u32[]{:S(2)}) collective-permute-start(bf16[128,1024]{1,0:T(8,128)(2,1)S(1)} %get-tuple-element.351), channel_id=1, source_target_pairs={{0,24},{8,0},{16,8},{24,16},{1,25},{9,1},{17,9},{25,17},{2,26},{10... | collective-permute-start | bytes 786440 | tf_op jit(solution)/shard_map/ppermute | solution.py:56
  572.4 44.9 %collective-permute-start.114 = (bf16[128,1024]{1,0:T(8,128)(2,1)}, bf16[128,1024]{1,0:T(8,128)(2,1)}, u32[]{:S(2)}, u32[]{:S(2)}) collective-permute-start(bf16[128,1024]{1,0:T(8,128)(2,1)} %get-tuple-element.377), channel_id=1, source_target_pairs={{0,4},{4,0},{1,5},{5,1},{2,6},{6,2},{3,7},{7,3},{8,12},{12,8},{9,1... | collective-permute-start | bytes 786440 | tf_op jit(solution)/shard_map/ppermute | solution.py:45
  573.6 32.3 %collective-permute-start.111 = (bf16[256,1024]{1,0:T(8,128)(2,1)S(1)}, bf16[256,1024]{1,0:T(8,128)(2,1)}, u32[]{:S(2)}, u32[]{:S(2)}) collective-permute-start(bf16[256,1024]{1,0:T(8,128)(2,1)S(1)} %get-tuple-element.345), channel_id=1, source_target_pairs={{0,2},{1,3},{2,0},{3,1},{4,6},{5,7},{6,4},{7,5},{8,10},{9,11},{10,... | collective-permute-start | bytes 1572872 | tf_op jit(solution)/shard_map/ppermute | solution.py:43
  574.3 31.6 %collective-permute-start.112 = (bf16[256,1024]{1,0:T(8,128)(2,1)S(1)}, bf16[256,1024]{1,0:T(8,128)(2,1)}, u32[]{:S(2)}, u32[]{:S(2)}) collective-permute-start(bf16[256,1024]{1,0:T(8,128)(2,1)S(1)} %get-tuple-element.346), channel_id=1, source_target_pairs={{0,4},{4,0},{1,5},{5,1},{2,6},{6,2},{3,7},{7,3},{8,12},{12,8},{9,1... | collective-permute-start | bytes 1572872 | tf_op jit(solution)/shard_map/ppermute | solution.py:45
  610.8 18.9 %all-to-all-start.2 = ((bf16[8,64,1024]{2,1,0:T(8,128)(2,1)}), bf16[8,64,1024]{2,1,0:T(8,128)(2,1)S(1)}, u32[]{:S(2)}, u32[]{:S(2)}) async-start(bf16[8,64,1024]{2,1,0:T(8,128)(2,1)} %bitcast.63), calls=%async_computation.6 | async-start | bytes 2097152 | tf_op jit(solution)/shard_map/all_to_all | solution.py:300
  (325 other events, 2436.6 us)
Sparse Core Ops, SparseCore 0:
  55.3 63.0 all-gather.7
  119.9 44.5 all-gather.5
  166.7 62.2 all-gather.9
  308.9 59.7 reduce-scatter.4
  396.7 26.4 reduce-scatter.6
  439.8 26.4 reduce-scatter.8
  497.0 59.8 reduce-scatter.10

commit v5 on v4

--- a/solution.py
+++ b/solution.py
@@ -169,14 +169,15 @@
         net = self.net
         if len(net.lo_bits) != 2:
             self.left = [net.scatter(self.blocks, net.lo_bits)]
-            self.moving = []
+            self.moving, self.low = [], []
             return
         self.moving = [net.swap(after(self.blocks[r | 1], *earlier), 1) for r in (2, 0)]
         self.left = [self.blocks[0], self.moving[1]]
 
     def parts(self, *earlier):
         if self.moving:
-            (far,) = add_low([[self.blocks[2], self.moving[0]]])
+            self.low = add_low([[self.blocks[2], self.moving[0]]])
+            far = self.low[0]
             self.moving = [self.net.swap(after(far, *earlier), 2)]
         return self.left + self.moving
 
@@ -1102,11 +1103,12 @@
     first_full = ring.finish()
     own_in = own_columns(in_came, layers)
     own_packs = [join_pieces(own_in[n], w_down[n], 0) for n in range(layers)]
-    early = (*ring.by_dp, ring.own_came, tokens_came, normed_held)
+    pair = to_groups(jnp.stack([variate_ids, time_ids], axis=-1))
+    pairs = net.gather(pair, lo_bits)
+    early = (*ring.by_dp, ring.own_came, tokens_came, normed_held, pairs[-1])
     packs = [lax.all_gather(after(own_packs[0], *early), "dp", axis=0)]
 
-    pair = to_groups(jnp.stack([variate_ids, time_ids], axis=-1))
-    pair = jnp.concatenate(net.gather(pair, lo_bits), axis=0)
+    pair = jnp.concatenate(pairs, axis=0)
     tables = head_tables(pair[:, 0], pair[:, 1], head_size)
 
     def matrices(full):
@@ -1123,13 +1125,17 @@
         ring = None
         layer_in = state
         blocks = net.gather(normed, lo_bits, None if layer else normed_held)
-        mixed = project(blocks, m_qkv, 3 * local_width)
+        taken = blocks
+        if final:
+            seed_grad = jnp.concatenate([pick(cotangent, net.hi), seed_came], axis=0)
+            seed_held = [net.swap(after(seed_grad, blocks[0]), seq_bits[-1])]
+            taken = [after(blocks[0], *seed_held)] + blocks[1:]
+        mixed = project(taken, m_qkv, 3 * local_width)
         if not final:
             own_next = join_pieces(own_qkv[layer + 1], w_out[layer + 1], 1)
             came_next = net.swap_hi(after(own_next, mixed))
-        if final:
-            seed_grad = to_groups(after(cotangent, blocks[-1]))
-            seed_held = [net.swap(after(seed_grad, mixed), seq_bits[-1])]
+        if layer == 0:
+            seed_came = net.swap_hi(pick(after(cotangent, came_next), 1 - net.hi))
         bias_pair = lax.dynamic_slice_in_dim(head_bias[layer], head_start, local_heads, 1)
         gains = jnp.concatenate([qk_gains[layer]] * 2, axis=1)
         bias = bias_marks(bias_pair, head_size)
@@ -1138,9 +1144,10 @@
         best_scores = lax.dynamic_update_slice(
             best_scores, head_tops[None, :], (jnp.int32(layer), head_start)
         )
-        leaving = attended
-        leaving = after(attended, *(seed_held if final else [came_next]))
+        leaving = attended if final else after(attended, came_next)
         arrived = net.trade(jnp.split(leaving, lo_n, axis=0), lo_bits)
+        if layer == 0:
+            arrived[0] = after(arrived[0], seed_came)
         if not final:
             own_next = in_order([own_next, came_next], net.hi).reshape(-1, own_next.shape[1])
             full_next = lax.all_gather(own_next, "dp", axis=0, tiled=True)
@@ -1195,15 +1202,19 @@
         moved = second_sum.moving
         second_sum.step()
         second_sum.step()
-        joined_first = after(grad_joined[0], *second_sum.low)
-        grad_hidden = hidden_weights(net, second, [joined_first] + grad_joined[1:], gated, down_in)
-        hidden_sums[layer] = lax.psum_scatter(
-            grad_hidden, "dp", scatter_dimension=0, tiled=True
-        )
+        parts = second_sum.parts()
+
+        def weights_of(*earlier):
+            first = after(grad_joined[0], *earlier)
+            total = hidden_weights(net, second, [first] + grad_joined[1:], gated, down_in)
+            hidden_sums[layer] = lax.psum_scatter(total, "dp", scatter_dimension=0, tiled=True)
+            return total
+
         if final:
             final_sum.step(*moved)
-        parts = second_sum.parts()
-        parts[0] = after(parts[0], grad_hidden, *(final_sum.moving if final else []))
+            parts[0] = after(parts[0], *final_sum.moving)
+        else:
+            parts[0] = after(parts[0], weights_of(*second_sum.low))
         gradient, gain_second, leaving, shares = out_backward(
             net, gradient, parts, middle, norm_gains[layer, 1], m_out, arrived, rows_out
         )
@@ -1212,11 +1223,13 @@
         grad_heads = jnp.concatenate(net.trade(leaving, lo_bits), axis=0)
         share_sum = SumLo(net, [x.reshape(-1, width) for x in shares])
         share_sum.step()
-        grad_heads = after(grad_heads, *share_sum.moving)
+        late = [weights_of(leaving[0])] if final else []
+        grad_heads = after(grad_heads, *share_sum.moving, *late)
         out_sum = share_sum.parts()
         grad_query, grad_keys, grad_values, grad_gains, grad_pair = attend_backward(
             mixed, grad_heads, tables, gains, bias, kept
         )
+        grad_query = after(grad_query, *share_sum.moving)
         grads = [grad_query, after(grad_keys, *final_sum.moving) if final else grad_keys, grad_values]
         if not final:
             other_sums = attention_sums[layer + 1]
@@ -1227,6 +1240,11 @@
                 total, 3 * local_width, rows_out
             )
         last = layer == 0
+        if not last:
+            normed_sum = SumLo(net, mixed_backward(grads, m_qkv, rows))
+            normed_sum.step()
+            parts = normed_sum.parts()
+            grads = [grads[0], after(grads[1], *normed_sum.low), grads[2]]
         mine, other = mixed_weights(net, normed, grads, out_sum, rows_out, F32 if last else BF)
         if last:
             sums = (mine, net.swap_hi(other))
@@ -1235,10 +1253,13 @@
             attention_sums[layer] = [
                 lax.psum_scatter(x, "dp", scatter_dimension=0, tiled=True) for x in sent
             ]
-        grads[0] = after(grads[0], other)
-        normed_sum = SumLo(net, mixed_backward(grads, m_qkv, rows))
-        normed_sum.step()
-        parts = normed_sum.parts()
+        if last:
+            grads[0] = after(grads[0], other)
+            normed_sum = SumLo(net, mixed_backward(grads, m_qkv, rows))
+            normed_sum.step()
+            parts = normed_sum.parts()
+        else:
+            parts[0] = after(parts[0], other)
         gradient, low, gain_first = norm_backward(
             gradient, parts, layer_in, norm_gains[layer, 0]
         )
@@ -1255,8 +1276,8 @@
         in_parts[layer], down_parts[layer] = split_hidden(
             hidden_sums[layer], width // net.dp_n, width
         )
-    in_parts = return_rows(in_parts, ("hi", "lo"), net.seq_n)
-    qkv_parts = return_rows(qkv_parts, "lo", lo_n, in_parts)
+    qkv_parts = return_rows(qkv_parts, "lo", lo_n)
+    in_parts = return_rows(in_parts, ("hi", "lo"), net.seq_n, qkv_parts)
     parts = final_sum.parts()
     low_state = (saved[-1][7] + sum(x.astype(F32) for x in parts)).astype(BF)
     layer_out = keep_own(low_state, net.swap_hi(low_state[tok_dev:]))

time: 658 us -> 635 us (0.965)
  waiting for transfers between devices: 208 us -> 179 us
  other arithmetic: 24.5 us -> 31.9 us
    ppermute x89, waiting for transfers between devices: 110 us -> 94.8 us  [swap(): return lax.ppermute(x, 'lo', [(i, i ^ bit) for i in range(self.lo_n)])]
    all_to_all x2, waiting for transfers between devices: 12.9 us -> 6.1 us  [return_rows(): return lax.all_to_all(after(own, *earlier), axes, 0, 0, tiled=True)]
    unnamed x451 -> x481, local copies, waits for them, and re-layouts: 93.7 us -> 93.3 us
  transfers between devices with their start and end apart: 135 -> 135, of which waited for: 53 -> 42; matrix products, arithmetic and copies ran while one was open for 9% -> 10% of each run, Pallas kernels for 23% -> 24%
where the time goes in v5:
time: 635 us; the launch traced here: 627 us
  waiting for transfers between devices  179 us (28%)
  Pallas kernels  163 us (26%)
  local copies, waits for them, and re-layouts  124 us (20%)
  starting transfers between devices  112 us (18%)
  other arithmetic  31.9 us (5%)
  between operations  17 us (3%)
    ppermute x89, waiting for transfers between devices, swap(): return lax.ppermute(x, 'lo', [(i, i ^ bit) for i in range(self.lo_n)])  94.8 us
    unnamed x481, local copies, waits for them, and re-layouts  93.3 us
    pallas_call x43, Pallas kernels, on_chip(): pl.pallas_call(kernel, in_specs=[SMEM] * len(first) + [VMEM] * len(arrays...  84.5 us
    ppermute x27, waiting for transfers between devices, swap(): return lax.ppermute(x, 'hi', [(i, i ^ bit) for i in range(self.hi_n)])  50.8 us
    ppermute x89, starting transfers between devices, swap(): return lax.ppermute(x, 'lo', [(i, i ^ bit) for i in range(self.lo_n)])  44.4 us
    ppermute x27, starting transfers between devices, swap(): return lax.ppermute(x, 'hi', [(i, i ^ bit) for i in range(self.hi_n)])  33.9 us
    pallas_call x2, Pallas kernels, attend_backward(): pl.pallas_call(functools.partial(attend_backward_kernel, min(256, length)...  33.3 us
    pallas_call x4, Pallas kernels, weight_call(): pl.pallas_call(body, in_specs=[SMEM] + [pl.BlockSpec(memory_space=pl.ANY)...  29.4 us
  transfers between devices with their start and end apart: 135, of which 42 were waited for; matrix products, arithmetic and copies ran while one was open for 10% of the time, Pallas kernels for 24%

profile of v5, /device:TPU:0, one launch (start us, length us, event | category | flops | bytes accessed | tf_op | source)
XLA Modules:
  0.0 626.6 jit_solution(10032912661077941361)
XLA Ops:
  39.0 4.6 all-to-all-done.1
  46.4 12.6 %collective-permute-done.3.refs_1_ = bf16[128,1024]{1,0:T(8,128)(2,1)S(1)} collective-permute-done((bf16[128,1024]{1,0:T(8,128)(2,1)S(1)}, bf16[128,1024]{1,0:T(8,128)(2,1)S(1)}, u32[]{:S(2)}, u32[]{:S(2)}) %collective-permute-start.3) | collective-permute-done | bytes 262176 | tf_op jit(solution)/shard_map/ppermute | solution.py:56
  68.2 13.8 %collective-permute-done.5.rest_came = bf16[384,1024]{1,0:T(8,128)(2,1)S(1)} collective-permute-done((bf16[384,1024]{1,0:T(8,128)(2,1)S(1)}, bf16[384,1024]{1,0:T(8,128)(2,1)S(1)}, u32[]{:S(2)}, u32[]{:S(2)}) %collective-permute-start.5) | collective-permute-done | bytes 786464 | tf_op jit(solution)/shard_map/ppermute | solution.py:45
  100.8 7.6 %attend.2 = (bf16[1024,256]{1,0:T(8,128)(2,1)S(1)}, f32[4,1024,128]{2,1,0:T(8,128)S(1)}, f32[4,8,128]{2,1,0:T(8,128)S(1)}) custom-call(bf16[1024,768]{1,0:T(8,128)(2,1)S(1)} %copy-done.173, bf16[1024,768]{1,0:T(8,128)(2,1)S(1)} %copy-done.173, bf16[1024,768]{1,0:T(8,128)(2,1)S(1)} %copy-done.173, f32[1024,128]{1,0:T(8,128)S(1)} %copy-done.67, ...), custom_call_target="tpu_custom_call" | custom-call | flops 4294967296 | bytes 4194304 | tf_op jit(solution)/shard_map/attend/pallas_call | solution.py:927
  112.6 5.9 collective-permute-done.19
  143.7 5.0 feed_forward.7
  165.9 6.1 collective-permute-done.34.refs_5_
  175.6 10.1 %collective-permute-done.35.refs_2_ = bf16[256,1024]{1,0:T(8,128)(2,1)S(1)} collective-permute-done((bf16[256,1024]{1,0:T(8,128)(2,1)S(1)}, bf16[256,1024]{1,0:T(8,128)(2,1)S(1)}, u32[]{:S(2)}, u32[]{:S(2)}) %collective-permute-start.35) | collective-permute-done | bytes 524320 | tf_op jit(solution)/shard_map/ppermute | solution.py:43
  192.6 8.4 %collective-permute-done.42.refs_2_ = bf16[256,1024]{1,0:T(8,128)(2,1)} collective-permute-done((bf16[256,1024]{1,0:T(8,128)(2,1)}, bf16[256,1024]{1,0:T(8,128)(2,1)}, u32[]{:S(2)}, u32[]{:S(2)}) %collective-permute-start.42) | collective-permute-done | bytes 524320 | tf_op jit(solution)/shard_map/ppermute | solution.py:43
  209.4 7.8 %attend.3 = (bf16[1024,256]{1,0:T(8,128)(2,1)S(1)}, f32[4,1024,128]{2,1,0:T(8,128)S(1)}, f32[4,8,128]{2,1,0:T(8,128)S(1)}) custom-call(bf16[1024,768]{1,0:T(8,128)(2,1)S(1)} %project.3.query_in.key_in.value_in, bf16[1024,768]{1,0:T(8,128)(2,1)S(1)} %project.3.query_in.key_in.value_in, bf16[1024,768]{1,0:T(8,128)(2,1)S(1)} %project.3.query_in.key_in.value_in, ...), custom_call_target="tpu_custom_call" | custom-call | flops 4294967296 | bytes 4194304 | tf_op jit(solution)/shard_map/attend/pallas_call | solution.py:927
  220.7 6.4 %collective-permute-done.45 = bf16[512,256]{1,0:T(8,128)(2,1)S(1)} collective-permute-done((bf16[512,256]{1,0:T(8,128)(2,1)S(1)}, bf16[512,256]{1,0:T(8,128)(2,1)S(1)}, u32[]{:S(2)}, u32[]{:S(2)}) %collective-permute-start.45) | collective-permute-done | bytes 262176 | tf_op jit(solution)/shard_map/ppermute | solution.py:43
  242.1 5.1 collective-permute-done.55.refs_3_.refs_4_
  262.3 5.0 feed_forward.10
  270.8 4.9 feed_backward.7
  289.1 5.8 collective-permute-done.71.refs_5_
  300.9 8.7 %collective-permute-done.72.refs_2_ = bf16[256,1024]{1,0:T(8,128)(2,1)S(1)} collective-permute-done((bf16[256,1024]{1,0:T(8,128)(2,1)S(1)}, bf16[256,1024]{1,0:T(8,128)(2,1)S(1)}, u32[]{:S(2)}, u32[]{:S(2)}) %collective-permute-start.72) | collective-permute-done | bytes 524320 | tf_op jit(solution)/shard_map/ppermute | solution.py:43
  319.7 8.8 %hidden_weights.2 = bf16[1536,1024]{1,0:T(8,128)(2,1)S(1)} custom-call(s32[1]{0:T(128)} %bitcast.39.index.at, bf16[256,1024]{1,0:T(8,128)(2,1)} %get-tuple-element.227.refs_1_.refs_0_, bf16[256,1024]{1,0:T(8,128)(2,1)} %collective-permute-done.47.refs_2_.refs_1_, bf16[256,1024]{1,0:T(8,128)(2,1)} %collective-permute-done.53.refs_1_.refs_2_, ...), custom_call_target="tpu_custom_call" | custom-call | flops 6442450944 | bytes 17825792 | tf_op jit(solution)/shard_map/hidden_weights/pallas_call | solution.py:561
  333.3 5.1 collective-permute-done.76
  346.1 16.7 %attend_backward.2 = (bf16[1024,256]{1,0:T(8,128)(2,1)S(1)}, bf16[1024,256]{1,0:T(8,128)(2,1)S(1)}, bf16[1024,256]{1,0:T(8,128)(2,1)S(1)}, f32[2,2,128]{2,1,0:T(2,128)S(1)}, f32[4,8,128]{2,1,0:T(8,128)S(1)}) custom-call(bf16[1024,768]{1,0:T(8,128)(2,1)S(1)} %copy-done.176, bf16[1024,768]{1,0:T(8,128)(2,1)S(1)} %copy-done.176, ...), custom_call_target="tpu_custom_call" | custom-call | flops 10737418240 | bytes 6291456 | tf_op jit(solution)/shard_map/attend_backward/pallas_call | solution.py:965
  370.9 6.0 mixed_weights.2
  376.9 6.5 %collective-permute-done.84.refs_2_ = bf16[256,1024]{1,0:T(8,128)(2,1)S(1)} collective-permute-done((bf16[256,1024]{1,0:T(8,128)(2,1)S(1)}, bf16[256,1024]{1,0:T(8,128)(2,1)S(1)}, u32[]{:S(2)}, u32[]{:S(2)}) %collective-permute-start.84) | collective-permute-done | bytes 524320 | tf_op jit(solution)/shard_map/ppermute | solution.py:43
  405.3 6.9 %feed_backward.10 = (bf16[1024,1024]{1,0:T(8,128)(2,1)S(1)}, bf16[1024,512]{1,0:T(8,128)(2,1)S(1)}, bf16[256,1024]{1,0:T(8,128)(2,1)S(1)}, bf16[256,1024]{1,0:T(...) custom-call(bf16[4,384,1024]{2,1,0:T(8,128)(2,1)S(1)} %bitcast.135, ...), custom_call_target="tpu_custom_call" | custom-call | flops 3221225472 | bytes 12582912 | tf_op jit(solution)/shard_map/feed_backward/pallas_call | solution.py:330
  421.3 4.2 feed_backward.11
  434.5 7.1 %collective-permute-done.97.refs_5_ = bf16[128,1024]{1,0:T(8,128)(2,1)S(1)} collective-permute-done((bf16[128,1024]{1,0:T(8,128)(2,1)S(1)}, bf16[128,1024]{1,0:T(8,128)(2,1)S(1)}, u32[]{:S(2)}, u32[]{:S(2)}) %collective-permute-start.97) | collective-permute-done | bytes 262176 | tf_op jit(solution)/shard_map/ppermute | solution.py:43
  457.1 8.9 %hidden_weights.3 = bf16[1536,1024]{1,0:T(8,128)(2,1)S(1)} custom-call(s32[1]{0:T(128)} %bitcast.39.index.at, bf16[256,1024]{1,0:T(8,128)(2,1)} %get-tuple-element.201.refs_1_.refs_0_, bf16[256,1024]{1,0:T(8,128)(2,1)S(1)} %copy-done.135, bf16[256,1024]{1,0:T(8,128)(2,1)} %collective-permute-done.23.refs_1_.refs_2_, bf16[256,1024]{1,0:T(8,128)(2,1)S(1)} %copy-done.137, ...), custom_call_target="tpu_custom_call" | custom-call | flops 6442450944 | bytes 17825792 | tf_op jit(solution)/shard_map/hidden_weights/pallas_call | solution.py:561
  472.1 4.4 out_backward.3
  492.8 16.5 %attend_backward.3 = (bf16[1024,256]{1,0:T(8,128)(2,1)S(1)}, bf16[1024,256]{1,0:T(8,128)(2,1)S(1)}, bf16[1024,256]{1,0:T(8,128)(2,1)S(1)}, f32[2,2,128]{2,1,0:T(2,128)S(1)}, f32[4,8,128]{2,1,0:T(8,128)S(1)}) custom-call(bf16[1024,768]{1,0:T(8,128)(2,1)S(1)} %copy-done.174, bf16[1024,768]{1,0:T(8,128)(2,1)S(1)} %copy-done.174, ...), custom_call_target="tpu_custom_call" | custom-call | flops 10737418240 | bytes 6291456 | tf_op jit(solution)/shard_map/attend_backward/pallas_call | solution.py:965
  509.4 5.7 mixed_weights.3
  529.5 16.3 %collective-permute-done.115.y = bf16[4,128,1024]{2,1,0:T(8,128)(2,1)S(1)} collective-permute-done((bf16[4,128,1024]{2,1,0:T(8,128)(2,1)}, bf16[4,128,1024]{2,1,0:T(8,128)(2,1)S(1)}, u32[]{:S(2)}, u32[]{:S(2)}) %collective-permute-start.115) | collective-permute-done | bytes 1048608 | tf_op jit(solution)/shard_map/ppermute | solution.py:45
  563.4 6.5 %collective-permute-done.117 = bf16[128,1024]{1,0:T(8,128)(2,1)} collective-permute-done((bf16[128,1024]{1,0:T(8,128)(2,1)}, bf16[128,1024]{1,0:T(8,128)(2,1)}, u32[]{:S(2)}, u32[]{:S(2)}) %collective-permute-start.117) | collective-permute-done | bytes 262176 | tf_op jit(solution)/shard_map/ppermute | solution.py:56
  581.0 5.5 collective-permute-start.122
  611.9 6.1 all-to-all-done.3.ref
  (927 shorter events, 360.7 us)
Async XLA Ops:
  24.1 19.4 %all-to-all-start.1 = ((bf16[8,64,1024]{2,1,0:T(8,128)(2,1)}), bf16[8,64,1024]{2,1,0:T(8,128)(2,1)S(1)}, u32[]{:S(2)}, u32[]{:S(2)}) async-start(bf16[8,64,1024]{2,1,0:T(8,128)(2,1)} %split_columns.3), calls=%async_computation.1 | async-start | bytes 2097152 | tf_op jit(solution)/shard_map/all_to_all | solution.py:1097
  27.7 99.0 %all-gather.8.cloned.1.call-start = ((), (), s32[]{:S(2)}) async-start(), calls=%async_computation.13 | async-start | bytes 3932160 | tf_op jit(solution)/shard_map/all_gather | solution.py:1109
  29.9 29.1 %collective-permute-start.10 = (bf16[256,1024]{1,0:T(8,128)(2,1)}, bf16[256,1024]{1,0:T(8,128)(2,1)}, u32[]{:S(2)}, u32[]{:S(2)}) collective-permute-start(bf16[256,1024]{1,0:T(8,128)(2,1)} %multiply_convert_fusion.refs_0_), channel_id=1, source_target_pairs={{0,2},{1,3},{2,0},{3,1},{4,6},{5,7},{6,4},{7,5},{8,10},{9,11},{10,... | collective-permute-start | bytes 1572872 | tf_op jit(solution)/shard_map/ppermute | solution.py:43
  36.5 22.5 %collective-permute-start.3 = (bf16[128,1024]{1,0:T(8,128)(2,1)S(1)}, bf16[128,1024]{1,0:T(8,128)(2,1)S(1)}, u32[]{:S(2)}, u32[]{:S(2)}) collective-permute-start(bf16[128,1024]{1,0:T(8,128)(2,1)S(1)} %maximum_maximum_fusion.own), channel_id=1, source_target_pairs={{0,16},{8,24},{16,0},{24,8},{1,17},{9,25},{17,1},{25,9},{2,18},{10... | collective-permute-start | bytes 786440 | tf_op jit(solution)/shard_map/ppermute | solution.py:56
  36.5 22.5 %collective-permute-start.2 = (bf16[128,1024]{1,0:T(8,128)(2,1)S(1)}, bf16[128,1024]{1,0:T(8,128)(2,1)S(1)}, u32[]{:S(2)}, u32[]{:S(2)}) collective-permute-start(bf16[128,1024]{1,0:T(8,128)(2,1)S(1)} %maximum_maximum_fusion.own), channel_id=1, source_target_pairs={{0,8},{8,16},{16,24},{24,0},{1,9},{9,17},{17,25},{25,1},{2,10},{10... | collective-permute-start | bytes 786440 | tf_op jit(solution)/shard_map/ppermute | solution.py:56
  37.5 21.5 %collective-permute-start.1 = (bf16[128,1024]{1,0:T(8,128)(2,1)S(1)}, bf16[128,1024]{1,0:T(8,128)(2,1)S(1)}, u32[]{:S(2)}, u32[]{:S(2)}) collective-permute-start(bf16[128,1024]{1,0:T(8,128)(2,1)S(1)} %maximum_maximum_fusion.own), channel_id=1, source_target_pairs={{0,4},{4,0},{1,5},{5,1},{2,6},{6,2},{3,7},{7,3},{8,12},{12,8},{9,1... | collective-permute-start | bytes 786440 | tf_op jit(solution)/shard_map/ppermute | solution.py:45
  59.1 142.6 %all-gather.6.cloned.1.call-start = ((), (), s32[]{:S(2)}) async-start(), calls=%async_computation.8 | async-start | bytes 2621440 | tf_op jit(solution)/shard_map/all_gather | solution.py:1153
  62.3 19.7 %collective-permute-start.5 = (bf16[384,1024]{1,0:T(8,128)(2,1)S(1)}, bf16[384,1024]{1,0:T(8,128)(2,1)S(1)}, u32[]{:S(2)}, u32[]{:S(2)}) collective-permute-start(bf16[384,1024]{1,0:T(8,128)(2,1)S(1)} %pad_maximum_fusion.1), channel_id=1, source_target_pairs={{0,4},{4,0},{1,5},{5,1},{2,6},{6,2},{3,7},{7,3},{8,12},{12,8},{9,1... | collective-permute-start | bytes 2359304 | tf_op jit(solution)/shard_map/ppermute | solution.py:45
  64.5 19.5 %collective-permute-start.9 = (bf16[256,1024]{1,0:T(8,128)(2,1)}, bf16[256,1024]{1,0:T(8,128)(2,1)S(1)}, u32[]{:S(2)}, u32[]{:S(2)}) collective-permute-start(bf16[256,1024]{1,0:T(8,128)(2,1)} %multiply_convert_fusion.refs_0_), channel_id=1, source_target_pairs={{0,1},{1,0},{2,3},{3,2},{4,5},{5,4},{6,7},{7,6},{8,9},{9,8},{10,11... | collective-permute-start | bytes 1572872 | tf_op jit(solution)/shard_map/ppermute | solution.py:43
  64.5 19.5 %collective-permute-start.11 = (bf16[256,1024]{1,0:T(8,128)(2,1)}, bf16[256,1024]{1,0:T(8,128)(2,1)S(1)}, u32[]{:S(2)}, u32[]{:S(2)}) collective-permute-start(bf16[256,1024]{1,0:T(8,128)(2,1)} %collective-permute-done.10.refs_2_), channel_id=1, source_target_pairs={{0,1},{1,0},{2,3},{3,2},{4,5},{5,4},{6,7},{7,6},{8,9},{9,8},{10,11... | collective-permute-start | bytes 1572872 | tf_op jit(solution)/shard_map/ppermute | solution.py:43
  91.2 20.8 %collective-permute-start.7 = (bf16[8,128,256]{2,1,0:T(8,128)(2,1)S(1)}, bf16[8,128,256]{2,1,0:T(8,128)(2,1)S(1)}, u32[]{:S(2)}, u32[]{:S(2)}) collective-permute-start(bf16[8,128,256]{2,1,0:T(8,128)(2,1)S(1)} %slice.283.refs_0_), channel_id=1, source_target_pairs={{0,2},{1,3},{2,0},{3,1},{4,6},{5,7},{6,4},{7,5},{8,10},{9,11},{10,... | collective-permute-start | bytes 1572872 | tf_op jit(solution)/shard_map/ppermute | solution.py:43
  96.8 138.6 %all-gather.10.cloned.1.call-start = ((), (), s32[]{:S(2)}) async-start(), calls=%async_computation.14 | async-start | bytes 3932160 | tf_op jit(solution)/shard_map/all_gather | solution.py:1157
  99.2 19.6 %collective-permute-start.6 = (bf16[8,128,256]{2,1,0:T(8,128)(2,1)S(1)}, bf16[8,128,256]{2,1,0:T(8,128)(2,1)S(1)}, u32[]{:S(2)}, u32[]{:S(2)}) collective-permute-start(bf16[8,128,256]{2,1,0:T(8,128)(2,1)S(1)} %slice.283.refs_0_), channel_id=1, source_target_pairs={{0,1},{1,0},{2,3},{3,2},{4,5},{5,4},{6,7},{7,6},{8,9},{9,8},{10,11... | collective-permute-start | bytes 1572872 | tf_op jit(solution)/shard_map/ppermute | solution.py:43
  154.9 261.2 %reduce-scatter.5.cloned.1.call-start = ((), (), s32[]{:S(2)}) async-start(), calls=%async_computation.9 | async-start | bytes 3932160 | tf_op jit(solution)/shard_map/reduce_scatter | solution.py:1210
  330.2 157.4 %reduce-scatter.7.cloned.1.call-start = ((), (), s32[]{:S(2)}) async-start(), calls=%async_computation.10 | async-start | bytes 1310720 | tf_op jit(solution)/shard_map/reduce_scatter | solution.py:1254
  339.7 24.3 %collective-permute-start.74 = (bf16[128,1024]{1,0:T(8,128)(2,1)S(1)}, bf16[128,1024]{1,0:T(8,128)(2,1)S(1)}, u32[]{:S(2)}, u32[]{:S(2)}) collective-permute-start(bf16[128,1024]{1,0:T(8,128)(2,1)S(1)} %get-tuple-element.268), channel_id=1, source_target_pairs={{0,4},{4,0},{1,5},{5,1},{2,6},{6,2},{3,7},{7,3},{8,12},{12,8},{9,1... | collective-permute-start | bytes 786440 | tf_op jit(solution)/shard_map/ppermute | solution.py:45
  341.2 23.4 %collective-permute-start.81 = (bf16[128,1024]{1,0:T(8,128)(2,1)S(1)}, bf16[128,1024]{1,0:T(8,128)(2,1)S(1)}, u32[]{:S(2)}, u32[]{:S(2)}) collective-permute-start(bf16[128,1024]{1,0:T(8,128)(2,1)S(1)} %get-tuple-element.287), channel_id=1, source_target_pairs={{0,2},{1,3},{2,0},{3,1},{4,6},{5,7},{6,4},{7,5},{8,10},{9,11},{10,... | collective-permute-start | bytes 786440 | tf_op jit(solution)/shard_map/ppermute | solution.py:43
  343.7 21.7 %collective-permute-start.80 = (bf16[256,1024]{1,0:T(8,128)(2,1)S(1)}, bf16[256,1024]{1,0:T(8,128)(2,1)S(1)}, u32[]{:S(2)}, u32[]{:S(2)}) collective-permute-start(bf16[256,1024]{1,0:T(8,128)(2,1)S(1)} %add_low.17), channel_id=1, source_target_pairs={{0,2},{1,3},{2,0},{3,1},{4,6},{5,7},{6,4},{7,5},{8,10},{9,11},{10,... | collective-permute-start | bytes 1572872 | tf_op jit(solution)/shard_map/ppermute | solution.py:43
  387.2 137.6 %reduce-scatter.9.cloned.1.call-start = ((), (), s32[]{:S(2)}) async-start(), calls=%async_computation.11 | async-start | bytes 1310720 | tf_op jit(solution)/shard_map/reduce_scatter | solution.py:1254
  428.7 168.1 %reduce-scatter.11.cloned.1.call-start = ((), (), s32[]{:S(2)}) async-start(), calls=%async_computation.12 | async-start | bytes 3932160 | tf_op jit(solution)/shard_map/reduce_scatter | solution.py:1210
  434.5 33.2 %collective-permute-start.98 = (bf16[256,1024]{1,0:T(8,128)(2,1)}, bf16[256,1024]{1,0:T(8,128)(2,1)}, u32[]{:S(2)}, u32[]{:S(2)}) collective-permute-start(bf16[256,1024]{1,0:T(8,128)(2,1)} %copy-done.144), channel_id=1, source_target_pairs={{0,1},{1,0},{2,3},{3,2},{4,5},{5,4},{6,7},{7,6},{8,9},{9,8},{10,11... | collective-permute-start | bytes 1572872 | tf_op jit(solution)/shard_map/ppermute | solution.py:43
  446.6 21.1 %collective-permute-start.99 = (bf16[256,1024]{1,0:T(8,128)(2,1)}, bf16[256,1024]{1,0:T(8,128)(2,1)}, u32[]{:S(2)}, u32[]{:S(2)}) collective-permute-start(bf16[256,1024]{1,0:T(8,128)(2,1)} %get-tuple-element.317), channel_id=1, source_target_pairs={{0,2},{1,3},{2,0},{3,1},{4,6},{5,7},{6,4},{7,5},{8,10},{9,11},{10,... | collective-permute-start | bytes 1572872 | tf_op jit(solution)/shard_map/ppermute | solution.py:43
  448.0 19.7 %collective-permute-start.100 = (bf16[256,1024]{1,0:T(8,128)(2,1)}, bf16[256,1024]{1,0:T(8,128)(2,1)}, u32[]{:S(2)}, u32[]{:S(2)}) collective-permute-start(bf16[256,1024]{1,0:T(8,128)(2,1)} %get-tuple-element.318), channel_id=1, source_target_pairs={{0,4},{4,0},{1,5},{5,1},{2,6},{6,2},{3,7},{7,3},{8,12},{12,8},{9,1... | collective-permute-start | bytes 1572872 | tf_op jit(solution)/shard_map/ppermute | solution.py:45
  487.7 21.7 %collective-permute-start.107 = (bf16[128,1024]{1,0:T(8,128)(2,1)}, bf16[128,1024]{1,0:T(8,128)(2,1)S(1)}, u32[]{:S(2)}, u32[]{:S(2)}) collective-permute-start(bf16[128,1024]{1,0:T(8,128)(2,1)} %reduce-scatter.7.cloned.1.call-done), channel_id=1, source_target_pairs={{0,4},{4,0},{1,5},{5,1},{2,6},{6,2},{3,7},{7,3},{8,12},{12,8},{9,1... | collective-permute-start | bytes 786440 | tf_op jit(solution)/shard_map/ppermute | solution.py:45
  519.7 26.0 %collective-permute-start.115 = (bf16[4,128,1024]{2,1,0:T(8,128)(2,1)}, bf16[4,128,1024]{2,1,0:T(8,128)(2,1)S(1)}, u32[]{:S(2)}, u32[]{:S(2)}) collective-permute-start(bf16[4,128,1024]{2,1,0:T(8,128)(2,1)} %copy-done.128), channel_id=1, source_target_pairs={{0,4},{4,0},{1,5},{5,1},{2,6},{6,2},{3,7},{7,3},{8,12},{12,8},{9,1... | collective-permute-start | bytes 3145736 | tf_op jit(solution)/shard_map/ppermute | solution.py:45
  522.2 31.6 %collective-permute-start.108 = (bf16[256,1024]{1,0:T(8,128)(2,1)}, bf16[256,1024]{1,0:T(8,128)(2,1)}, u32[]{:S(2)}, u32[]{:S(2)}) collective-permute-start(bf16[256,1024]{1,0:T(8,128)(2,1)} %get-tuple-element.346), channel_id=1, source_target_pairs={{0,1},{1,0},{2,3},{3,2},{4,5},{5,4},{6,7},{7,6},{8,9},{9,8},{10,11... | collective-permute-start | bytes 1572872 | tf_op jit(solution)/shard_map/ppermute | solution.py:43
  523.6 30.2 %collective-permute-start.110 = (bf16[256,1024]{1,0:T(8,128)(2,1)}, bf16[256,1024]{1,0:T(8,128)(2,1)}, u32[]{:S(2)}, u32[]{:S(2)}) collective-permute-start(bf16[256,1024]{1,0:T(8,128)(2,1)} %add_low.22), channel_id=1, source_target_pairs={{0,2},{1,3},{2,0},{3,1},{4,6},{5,7},{6,4},{7,5},{8,10},{9,11},{10,... | collective-permute-start | bytes 1572872 | tf_op jit(solution)/shard_map/ppermute | solution.py:43
  548.9 21.0 %collective-permute-start.117 = (bf16[128,1024]{1,0:T(8,128)(2,1)}, bf16[128,1024]{1,0:T(8,128)(2,1)}, u32[]{:S(2)}, u32[]{:S(2)}) collective-permute-start(bf16[128,1024]{1,0:T(8,128)(2,1)} %get-tuple-element.358), channel_id=1, source_target_pairs={{0,16},{8,24},{16,0},{24,8},{1,17},{9,25},{17,1},{25,9},{2,18},{10... | collective-permute-start | bytes 786440 | tf_op jit(solution)/shard_map/ppermute | solution.py:56
  558.9 47.6 %collective-permute-start.114 = (bf16[128,1024]{1,0:T(8,128)(2,1)}, bf16[128,1024]{1,0:T(8,128)(2,1)}, u32[]{:S(2)}, u32[]{:S(2)}) collective-permute-start(bf16[128,1024]{1,0:T(8,128)(2,1)} %get-tuple-element.385), channel_id=1, source_target_pairs={{0,4},{4,0},{1,5},{5,1},{2,6},{6,2},{3,7},{7,3},{8,12},{12,8},{9,1... | collective-permute-start | bytes 786440 | tf_op jit(solution)/shard_map/ppermute | solution.py:45
  560.7 32.8 %collective-permute-start.111 = (bf16[256,1024]{1,0:T(8,128)(2,1)}, bf16[256,1024]{1,0:T(8,128)(2,1)}, u32[]{:S(2)}, u32[]{:S(2)}) collective-permute-start(bf16[256,1024]{1,0:T(8,128)(2,1)} %get-tuple-element.353), channel_id=1, source_target_pairs={{0,2},{1,3},{2,0},{3,1},{4,6},{5,7},{6,4},{7,5},{8,10},{9,11},{10,... | collective-permute-start | bytes 1572872 | tf_op jit(solution)/shard_map/ppermute | solution.py:43
  562.0 31.5 %collective-permute-start.112 = (bf16[256,1024]{1,0:T(8,128)(2,1)S(1)}, bf16[256,1024]{1,0:T(8,128)(2,1)}, u32[]{:S(2)}, u32[]{:S(2)}) collective-permute-start(bf16[256,1024]{1,0:T(8,128)(2,1)S(1)} %get-tuple-element.354), channel_id=1, source_target_pairs={{0,4},{4,0},{1,5},{5,1},{2,6},{6,2},{3,7},{7,3},{8,12},{12,8},{9,1... | collective-permute-start | bytes 1572872 | tf_op jit(solution)/shard_map/ppermute | solution.py:45
  577.5 21.4 %all-to-all-start.2 = ((bf16[4,64,768]{2,1,0:T(8,128)(2,1)}), bf16[4,64,768]{2,1,0:T(8,128)(2,1)S(1)}, u32[]{:S(2)}, u32[]{:S(2)}) async-start(bf16[4,64,768]{2,1,0:T(8,128)(2,1)} %bitcast.58), calls=%async_computation.5 | async-start | bytes 786432 | tf_op jit(solution)/shard_map/all_to_all | solution.py:301
  (340 other events, 2617.0 us)
Sparse Core Ops, SparseCore 0:
  59.2 62.9 all-gather.7
  123.8 44.5 all-gather.5
  170.5 62.2 all-gather.9
  330.3 60.4 reduce-scatter.4
  393.0 27.1 reduce-scatter.6
  428.8 25.7 reduce-scatter.8
  487.7 59.8 reduce-scatter.10

commit v6 on v5

--- a/solution.py
+++ b/solution.py
@@ -1133,7 +1133,7 @@
         mixed = project(taken, m_qkv, 3 * local_width)
         if not final:
             own_next = join_pieces(own_qkv[layer + 1], w_out[layer + 1], 1)
-            came_next = net.swap_hi(after(own_next, mixed))
+            came_next = net.swap_hi(after(own_next, first_full))
         if layer == 0:
             seed_came = net.swap_hi(pick(after(cotangent, came_next), 1 - net.hi))
         bias_pair = lax.dynamic_slice_in_dim(head_bias[layer], head_start, local_heads, 1)

time: 635 us -> 631 us (level)
    unnamed x481 -> x467, local copies, waits for them, and re-layouts: 93.3 us -> 90.3 us
  transfers between devices with their start and end apart: 135 -> 135, of which waited for: 42 -> 44; matrix products, arithmetic and copies ran while one was open for 10% -> 10% of each run, Pallas kernels for 24% -> 24%
where the time goes in v6:
time: 631 us; the launch traced here: 623 us
  waiting for transfers between devices  177 us (28%)
  Pallas kernels  165 us (26%)
  local copies, waits for them, and re-layouts  120 us (19%)
  starting transfers between devices  112 us (18%)
  other arithmetic  30.7 us (5%)
  between operations  16.9 us (3%)
    ppermute x89, waiting for transfers between devices, swap(): return lax.ppermute(x, 'lo', [(i, i ^ bit) for i in range(self.lo_n)])  93.6 us
    unnamed x467, local copies, waits for them, and re-layouts  90.3 us
    pallas_call x43, Pallas kernels, on_chip(): pl.pallas_call(kernel, in_specs=[SMEM] * len(first) + [VMEM] * len(arrays...  85.3 us
    ppermute x27, waiting for transfers between devices, swap(): return lax.ppermute(x, 'hi', [(i, i ^ bit) for i in range(self.hi_n)])  48 us
    ppermute x89, starting transfers between devices, swap(): return lax.ppermute(x, 'lo', [(i, i ^ bit) for i in range(self.lo_n)])  45.1 us
    ppermute x27, starting transfers between devices, swap(): return lax.ppermute(x, 'hi', [(i, i ^ bit) for i in range(self.hi_n)])  33.7 us
    pallas_call x2, Pallas kernels, attend_backward(): pl.pallas_call(functools.partial(attend_backward_kernel, min(256, length)...  33.7 us
    pallas_call x4, Pallas kernels, weight_call(): pl.pallas_call(body, in_specs=[SMEM] + [pl.BlockSpec(memory_space=pl.ANY)...  29.6 us
  transfers between devices with their start and end apart: 135, of which 44 were waited for; matrix products, arithmetic and copies ran while one was open for 10% of the time, Pallas kernels for 24%

profile of v6, /device:TPU:0, one launch (start us, length us, event | category | flops | bytes accessed | tf_op | source)
XLA Modules:
  0.0 622.6 jit_solution(16728074468978851489)
XLA Ops:
  32.4 4.1 collective-permute-start.4
  39.0 4.6 all-to-all-done.1
  46.4 12.6 %collective-permute-done.3.refs_1_ = bf16[128,1024]{1,0:T(8,128)(2,1)S(1)} collective-permute-done((bf16[128,1024]{1,0:T(8,128)(2,1)S(1)}, bf16[128,1024]{1,0:T(8,128)(2,1)S(1)}, u32[]{:S(2)}, u32[]{:S(2)}) %collective-permute-start.3) | collective-permute-done | bytes 262176 | tf_op jit(solution)/shard_map/ppermute | solution.py:56
  68.0 14.6 %collective-permute-done.5.rest_came = bf16[384,1024]{1,0:T(8,128)(2,1)S(1)} collective-permute-done((bf16[384,1024]{1,0:T(8,128)(2,1)S(1)}, bf16[384,1024]{1,0:T(8,128)(2,1)S(1)}, u32[]{:S(2)}, u32[]{:S(2)}) %collective-permute-start.5) | collective-permute-done | bytes 786464 | tf_op jit(solution)/shard_map/ppermute | solution.py:45
  97.0 8.1 %attend.2 = (bf16[1024,256]{1,0:T(8,128)(2,1)S(1)}, f32[4,1024,128]{2,1,0:T(8,128)S(1)}, f32[4,8,128]{2,1,0:T(8,128)S(1)}) custom-call(bf16[1024,768]{1,0:T(8,128)(2,1)S(1)} %project.2.query_in.key_in.value_in, bf16[1024,768]{1,0:T(8,128)(2,1)S(1)} %project.2.query_in.key_in.value_in, bf16[1024,768]{1,0:T(8,128)(2,1)S(1)} %project.2.query_in.key_in.value_in, ...), custom_call_target="tpu_custom_call" | custom-call | flops 4294967296 | bytes 4194304 | tf_op jit(solution)/shard_map/attend/pallas_call | solution.py:927
  109.3 4.1 collective-permute-done.19
  138.7 5.0 feed_forward.7
  160.9 6.1 collective-permute-done.34.refs_5_
  170.6 10.2 %collective-permute-done.35.refs_2_ = bf16[256,1024]{1,0:T(8,128)(2,1)S(1)} collective-permute-done((bf16[256,1024]{1,0:T(8,128)(2,1)S(1)}, bf16[256,1024]{1,0:T(8,128)(2,1)S(1)}, u32[]{:S(2)}, u32[]{:S(2)}) %collective-permute-start.35) | collective-permute-done | bytes 524320 | tf_op jit(solution)/shard_map/ppermute | solution.py:43
  187.6 8.5 %collective-permute-done.42.refs_2_ = bf16[256,1024]{1,0:T(8,128)(2,1)} collective-permute-done((bf16[256,1024]{1,0:T(8,128)(2,1)}, bf16[256,1024]{1,0:T(8,128)(2,1)}, u32[]{:S(2)}, u32[]{:S(2)}) %collective-permute-start.42) | collective-permute-done | bytes 524320 | tf_op jit(solution)/shard_map/ppermute | solution.py:43
  204.5 8.1 %attend.3 = (bf16[1024,256]{1,0:T(8,128)(2,1)S(1)}, f32[4,1024,128]{2,1,0:T(8,128)S(1)}, f32[4,8,128]{2,1,0:T(8,128)S(1)}) custom-call(bf16[1024,768]{1,0:T(8,128)(2,1)S(1)} %project.3.query_in.key_in.value_in, bf16[1024,768]{1,0:T(8,128)(2,1)S(1)} %project.3.query_in.key_in.value_in, bf16[1024,768]{1,0:T(8,128)(2,1)S(1)} %project.3.query_in.key_in.value_in, ...), custom_call_target="tpu_custom_call" | custom-call | flops 4294967296 | bytes 4194304 | tf_op jit(solution)/shard_map/attend/pallas_call | solution.py:927
  216.0 6.5 %collective-permute-done.45 = bf16[512,256]{1,0:T(8,128)(2,1)S(1)} collective-permute-done((bf16[512,256]{1,0:T(8,128)(2,1)S(1)}, bf16[512,256]{1,0:T(8,128)(2,1)S(1)}, u32[]{:S(2)}, u32[]{:S(2)}) %collective-permute-start.45) | collective-permute-done | bytes 262176 | tf_op jit(solution)/shard_map/ppermute | solution.py:43
  257.7 5.0 feed_forward.10
  266.1 4.7 feed_backward.7
  284.3 5.8 collective-permute-done.71.refs_5_
  296.2 8.7 %collective-permute-done.72.refs_2_ = bf16[256,1024]{1,0:T(8,128)(2,1)S(1)} collective-permute-done((bf16[256,1024]{1,0:T(8,128)(2,1)S(1)}, bf16[256,1024]{1,0:T(8,128)(2,1)S(1)}, u32[]{:S(2)}, u32[]{:S(2)}) %collective-permute-start.72) | collective-permute-done | bytes 524320 | tf_op jit(solution)/shard_map/ppermute | solution.py:43
  315.0 8.8 %hidden_weights.2 = bf16[1536,1024]{1,0:T(8,128)(2,1)S(1)} custom-call(s32[1]{0:T(128)} %bitcast.39.index.at, bf16[256,1024]{1,0:T(8,128)(2,1)} %get-tuple-element.227.refs_1_.refs_0_, bf16[256,1024]{1,0:T(8,128)(2,1)} %collective-permute-done.47.refs_2_.refs_1_, bf16[256,1024]{1,0:T(8,128)(2,1)} %collective-permute-done.53.refs_1_.refs_2_, ...), custom_call_target="tpu_custom_call" | custom-call | flops 6442450944 | bytes 17825792 | tf_op jit(solution)/shard_map/hidden_weights/pallas_call | solution.py:561
  328.5 5.0 collective-permute-done.76
  341.3 17.0 %attend_backward.2 = (bf16[1024,256]{1,0:T(8,128)(2,1)S(1)}, bf16[1024,256]{1,0:T(8,128)(2,1)S(1)}, bf16[1024,256]{1,0:T(8,128)(2,1)S(1)}, f32[2,2,128]{2,1,0:T(2,128)S(1)}, f32[4,8,128]{2,1,0:T(8,128)S(1)}) custom-call(bf16[1024,768]{1,0:T(8,128)(2,1)S(1)} %copy-done.169, bf16[1024,768]{1,0:T(8,128)(2,1)S(1)} %copy-done.169, ...), custom_call_target="tpu_custom_call" | custom-call | flops 10737418240 | bytes 6291456 | tf_op jit(solution)/shard_map/attend_backward/pallas_call | solution.py:965
  366.4 6.0 mixed_weights.2
  372.4 6.5 %collective-permute-done.84.refs_2_ = bf16[256,1024]{1,0:T(8,128)(2,1)S(1)} collective-permute-done((bf16[256,1024]{1,0:T(8,128)(2,1)S(1)}, bf16[256,1024]{1,0:T(8,128)(2,1)S(1)}, u32[]{:S(2)}, u32[]{:S(2)}) %collective-permute-start.84) | collective-permute-done | bytes 524320 | tf_op jit(solution)/shard_map/ppermute | solution.py:43
  400.8 6.9 %feed_backward.10 = (bf16[1024,1024]{1,0:T(8,128)(2,1)S(1)}, bf16[1024,512]{1,0:T(8,128)(2,1)S(1)}, bf16[256,1024]{1,0:T(8,128)(2,1)S(1)}, bf16[256,1024]{1,0:T(...) custom-call(bf16[4,384,1024]{2,1,0:T(8,128)(2,1)S(1)} %bitcast.135, ...), custom_call_target="tpu_custom_call" | custom-call | flops 3221225472 | bytes 12582912 | tf_op jit(solution)/shard_map/feed_backward/pallas_call | solution.py:330
  416.8 4.2 feed_backward.11
  429.9 7.2 %collective-permute-done.97.refs_5_ = bf16[128,1024]{1,0:T(8,128)(2,1)S(1)} collective-permute-done((bf16[128,1024]{1,0:T(8,128)(2,1)S(1)}, bf16[128,1024]{1,0:T(8,128)(2,1)S(1)}, u32[]{:S(2)}, u32[]{:S(2)}) %collective-permute-start.97) | collective-permute-done | bytes 262176 | tf_op jit(solution)/shard_map/ppermute | solution.py:43
  452.5 8.9 %hidden_weights.3 = bf16[1536,1024]{1,0:T(8,128)(2,1)S(1)} custom-call(s32[1]{0:T(128)} %bitcast.39.index.at, bf16[256,1024]{1,0:T(8,128)(2,1)} %get-tuple-element.201.refs_1_.refs_0_, bf16[256,1024]{1,0:T(8,128)(2,1)S(1)} %copy-done.129, bf16[256,1024]{1,0:T(8,128)(2,1)} %collective-permute-done.23.refs_1_.refs_2_, bf16[256,1024]{1,0:T(8,128)(2,1)S(1)} %copy-done.131, ...), custom_call_target="tpu_custom_call" | custom-call | flops 6442450944 | bytes 17825792 | tf_op jit(solution)/shard_map/hidden_weights/pallas_call | solution.py:561
  467.5 4.4 out_backward.3
  488.2 16.8 %attend_backward.3 = (bf16[1024,256]{1,0:T(8,128)(2,1)S(1)}, bf16[1024,256]{1,0:T(8,128)(2,1)S(1)}, bf16[1024,256]{1,0:T(8,128)(2,1)S(1)}, f32[2,2,128]{2,1,0:T(2,128)S(1)}, f32[4,8,128]{2,1,0:T(8,128)S(1)}) custom-call(bf16[1024,768]{1,0:T(8,128)(2,1)S(1)} %copy-done.167, bf16[1024,768]{1,0:T(8,128)(2,1)S(1)} %copy-done.167, ...), custom_call_target="tpu_custom_call" | custom-call | flops 10737418240 | bytes 6291456 | tf_op jit(solution)/shard_map/attend_backward/pallas_call | solution.py:965
  505.1 6.0 mixed_weights.3
  525.4 16.3 %collective-permute-done.115.y = bf16[4,128,1024]{2,1,0:T(8,128)(2,1)S(1)} collective-permute-done((bf16[4,128,1024]{2,1,0:T(8,128)(2,1)}, bf16[4,128,1024]{2,1,0:T(8,128)(2,1)S(1)}, u32[]{:S(2)}, u32[]{:S(2)}) %collective-permute-start.115) | collective-permute-done | bytes 1048608 | tf_op jit(solution)/shard_map/ppermute | solution.py:45
  559.6 6.3 %collective-permute-done.117 = bf16[128,1024]{1,0:T(8,128)(2,1)} collective-permute-done((bf16[128,1024]{1,0:T(8,128)(2,1)}, bf16[128,1024]{1,0:T(8,128)(2,1)}, u32[]{:S(2)}, u32[]{:S(2)}) %collective-permute-start.117) | collective-permute-done | bytes 262176 | tf_op jit(solution)/shard_map/ppermute | solution.py:56
  577.0 5.6 collective-permute-start.122
  607.9 6.1 all-to-all-done.3.ref
  (913 shorter events, 357.3 us)
Async XLA Ops:
  24.1 19.4 %all-to-all-start.1 = ((bf16[8,64,1024]{2,1,0:T(8,128)(2,1)}), bf16[8,64,1024]{2,1,0:T(8,128)(2,1)S(1)}, u32[]{:S(2)}, u32[]{:S(2)}) async-start(bf16[8,64,1024]{2,1,0:T(8,128)(2,1)} %split_columns.3), calls=%async_computation.1 | async-start | bytes 2097152 | tf_op jit(solution)/shard_map/all_to_all | solution.py:1097
  27.7 94.5 %all-gather.8.cloned.1.call-start = ((), (), s32[]{:S(2)}) async-start(), calls=%async_computation.13 | async-start | bytes 3932160 | tf_op jit(solution)/shard_map/all_gather | solution.py:1109
  30.0 29.1 %collective-permute-start.10 = (bf16[256,1024]{1,0:T(8,128)(2,1)}, bf16[256,1024]{1,0:T(8,128)(2,1)}, u32[]{:S(2)}, u32[]{:S(2)}) collective-permute-start(bf16[256,1024]{1,0:T(8,128)(2,1)} %multiply_convert_fusion.refs_0_), channel_id=1, source_target_pairs={{0,2},{1,3},{2,0},{3,1},{4,6},{5,7},{6,4},{7,5},{8,10},{9,11},{10,... | collective-permute-start | bytes 1572872 | tf_op jit(solution)/shard_map/ppermute | solution.py:43
  36.5 22.5 %collective-permute-start.3 = (bf16[128,1024]{1,0:T(8,128)(2,1)S(1)}, bf16[128,1024]{1,0:T(8,128)(2,1)S(1)}, u32[]{:S(2)}, u32[]{:S(2)}) collective-permute-start(bf16[128,1024]{1,0:T(8,128)(2,1)S(1)} %maximum_maximum_fusion.own), channel_id=1, source_target_pairs={{0,16},{8,24},{16,0},{24,8},{1,17},{9,25},{17,1},{25,9},{2,18},{10... | collective-permute-start | bytes 786440 | tf_op jit(solution)/shard_map/ppermute | solution.py:56
  36.5 22.5 %collective-permute-start.2 = (bf16[128,1024]{1,0:T(8,128)(2,1)S(1)}, bf16[128,1024]{1,0:T(8,128)(2,1)S(1)}, u32[]{:S(2)}, u32[]{:S(2)}) collective-permute-start(bf16[128,1024]{1,0:T(8,128)(2,1)S(1)} %maximum_maximum_fusion.own), channel_id=1, source_target_pairs={{0,8},{8,16},{16,24},{24,0},{1,9},{9,17},{17,25},{25,1},{2,10},{10... | collective-permute-start | bytes 786440 | tf_op jit(solution)/shard_map/ppermute | solution.py:56
  37.5 21.5 %collective-permute-start.1 = (bf16[128,1024]{1,0:T(8,128)(2,1)S(1)}, bf16[128,1024]{1,0:T(8,128)(2,1)S(1)}, u32[]{:S(2)}, u32[]{:S(2)}) collective-permute-start(bf16[128,1024]{1,0:T(8,128)(2,1)S(1)} %maximum_maximum_fusion.own), channel_id=1, source_target_pairs={{0,4},{4,0},{1,5},{5,1},{2,6},{6,2},{3,7},{7,3},{8,12},{12,8},{9,1... | collective-permute-start | bytes 786440 | tf_op jit(solution)/shard_map/ppermute | solution.py:45
  59.1 137.7 %all-gather.6.cloned.1.call-start = ((), (), s32[]{:S(2)}) async-start(), calls=%async_computation.8 | async-start | bytes 2621440 | tf_op jit(solution)/shard_map/all_gather | solution.py:1153
  62.9 19.7 %collective-permute-start.5 = (bf16[384,1024]{1,0:T(8,128)(2,1)S(1)}, bf16[384,1024]{1,0:T(8,128)(2,1)S(1)}, u32[]{:S(2)}, u32[]{:S(2)}) collective-permute-start(bf16[384,1024]{1,0:T(8,128)(2,1)S(1)} %pad_maximum_fusion.1), channel_id=1, source_target_pairs={{0,4},{4,0},{1,5},{5,1},{2,6},{6,2},{3,7},{7,3},{8,12},{12,8},{9,1... | collective-permute-start | bytes 2359304 | tf_op jit(solution)/shard_map/ppermute | solution.py:45
  67.3 26.2 %collective-permute-start.9 = (bf16[256,1024]{1,0:T(8,128)(2,1)}, bf16[256,1024]{1,0:T(8,128)(2,1)}, u32[]{:S(2)}, u32[]{:S(2)}) collective-permute-start(bf16[256,1024]{1,0:T(8,128)(2,1)} %multiply_convert_fusion.refs_0_), channel_id=1, source_target_pairs={{0,1},{1,0},{2,3},{3,2},{4,5},{5,4},{6,7},{7,6},{8,9},{9,8},{10,11... | collective-permute-start | bytes 1572872 | tf_op jit(solution)/shard_map/ppermute | solution.py:43
  67.4 26.1 %collective-permute-start.11 = (bf16[256,1024]{1,0:T(8,128)(2,1)}, bf16[256,1024]{1,0:T(8,128)(2,1)}, u32[]{:S(2)}, u32[]{:S(2)}) collective-permute-start(bf16[256,1024]{1,0:T(8,128)(2,1)} %collective-permute-done.10.refs_2_), channel_id=1, source_target_pairs={{0,1},{1,0},{2,3},{3,2},{4,5},{5,4},{6,7},{7,6},{8,9},{9,8},{10,11... | collective-permute-start | bytes 1572872 | tf_op jit(solution)/shard_map/ppermute | solution.py:43
  88.9 19.9 %collective-permute-start.7 = (bf16[8,128,256]{2,1,0:T(8,128)(2,1)S(1)}, bf16[8,128,256]{2,1,0:T(8,128)(2,1)}, u32[]{:S(2)}, u32[]{:S(2)}) collective-permute-start(bf16[8,128,256]{2,1,0:T(8,128)(2,1)S(1)} %slice.283.refs_0_), channel_id=1, source_target_pairs={{0,2},{1,3},{2,0},{3,1},{4,6},{5,7},{6,4},{7,5},{8,10},{9,11},{10,... | collective-permute-start | bytes 1572872 | tf_op jit(solution)/shard_map/ppermute | solution.py:43
  89.5 24.2 %collective-permute-start.6 = (bf16[8,128,256]{2,1,0:T(8,128)(2,1)S(1)}, bf16[8,128,256]{2,1,0:T(8,128)(2,1)}, u32[]{:S(2)}, u32[]{:S(2)}) collective-permute-start(bf16[8,128,256]{2,1,0:T(8,128)(2,1)S(1)} %slice.283.refs_0_), channel_id=1, source_target_pairs={{0,1},{1,0},{2,3},{3,2},{4,5},{5,4},{6,7},{7,6},{8,9},{9,8},{10,11... | collective-permute-start | bytes 1572872 | tf_op jit(solution)/shard_map/ppermute | solution.py:43
  93.4 139.4 %all-gather.10.cloned.1.call-start = ((), (), s32[]{:S(2)}) async-start(), calls=%async_computation.14 | async-start | bytes 3932160 | tf_op jit(solution)/shard_map/all_gather | solution.py:1157
  149.9 261.8 %reduce-scatter.5.cloned.1.call-start = ((), (), s32[]{:S(2)}) async-start(), calls=%async_computation.9 | async-start | bytes 3932160 | tf_op jit(solution)/shard_map/reduce_scatter | solution.py:1210
  325.5 157.5 %reduce-scatter.7.cloned.1.call-start = ((), (), s32[]{:S(2)}) async-start(), calls=%async_computation.10 | async-start | bytes 1310720 | tf_op jit(solution)/shard_map/reduce_scatter | solution.py:1254
  334.9 24.6 %collective-permute-start.74 = (bf16[128,1024]{1,0:T(8,128)(2,1)S(1)}, bf16[128,1024]{1,0:T(8,128)(2,1)S(1)}, u32[]{:S(2)}, u32[]{:S(2)}) collective-permute-start(bf16[128,1024]{1,0:T(8,128)(2,1)S(1)} %get-tuple-element.268), channel_id=1, source_target_pairs={{0,4},{4,0},{1,5},{5,1},{2,6},{6,2},{3,7},{7,3},{8,12},{12,8},{9,1... | collective-permute-start | bytes 786440 | tf_op jit(solution)/shard_map/ppermute | solution.py:45
  336.5 23.7 %collective-permute-start.81 = (bf16[128,1024]{1,0:T(8,128)(2,1)S(1)}, bf16[128,1024]{1,0:T(8,128)(2,1)S(1)}, u32[]{:S(2)}, u32[]{:S(2)}) collective-permute-start(bf16[128,1024]{1,0:T(8,128)(2,1)S(1)} %get-tuple-element.287), channel_id=1, source_target_pairs={{0,2},{1,3},{2,0},{3,1},{4,6},{5,7},{6,4},{7,5},{8,10},{9,11},{10,... | collective-permute-start | bytes 786440 | tf_op jit(solution)/shard_map/ppermute | solution.py:43
  339.0 21.9 %collective-permute-start.80 = (bf16[256,1024]{1,0:T(8,128)(2,1)S(1)}, bf16[256,1024]{1,0:T(8,128)(2,1)S(1)}, u32[]{:S(2)}, u32[]{:S(2)}) collective-permute-start(bf16[256,1024]{1,0:T(8,128)(2,1)S(1)} %add_low.17), channel_id=1, source_target_pairs={{0,2},{1,3},{2,0},{3,1},{4,6},{5,7},{6,4},{7,5},{8,10},{9,11},{10,... | collective-permute-start | bytes 1572872 | tf_op jit(solution)/shard_map/ppermute | solution.py:43
  382.6 138.1 %reduce-scatter.9.cloned.1.call-start = ((), (), s32[]{:S(2)}) async-start(), calls=%async_computation.11 | async-start | bytes 1310720 | tf_op jit(solution)/shard_map/reduce_scatter | solution.py:1254
  424.2 168.5 %reduce-scatter.11.cloned.1.call-start = ((), (), s32[]{:S(2)}) async-start(), calls=%async_computation.12 | async-start | bytes 3932160 | tf_op jit(solution)/shard_map/reduce_scatter | solution.py:1210
  429.9 33.2 %collective-permute-start.98 = (bf16[256,1024]{1,0:T(8,128)(2,1)}, bf16[256,1024]{1,0:T(8,128)(2,1)}, u32[]{:S(2)}, u32[]{:S(2)}) collective-permute-start(bf16[256,1024]{1,0:T(8,128)(2,1)} %copy-done.138), channel_id=1, source_target_pairs={{0,1},{1,0},{2,3},{3,2},{4,5},{5,4},{6,7},{7,6},{8,9},{9,8},{10,11... | collective-permute-start | bytes 1572872 | tf_op jit(solution)/shard_map/ppermute | solution.py:43
  442.1 21.0 %collective-permute-start.99 = (bf16[256,1024]{1,0:T(8,128)(2,1)}, bf16[256,1024]{1,0:T(8,128)(2,1)}, u32[]{:S(2)}, u32[]{:S(2)}) collective-permute-start(bf16[256,1024]{1,0:T(8,128)(2,1)} %get-tuple-element.317), channel_id=1, source_target_pairs={{0,2},{1,3},{2,0},{3,1},{4,6},{5,7},{6,4},{7,5},{8,10},{9,11},{10,... | collective-permute-start | bytes 1572872 | tf_op jit(solution)/shard_map/ppermute | solution.py:43
  443.5 19.6 %collective-permute-start.100 = (bf16[256,1024]{1,0:T(8,128)(2,1)}, bf16[256,1024]{1,0:T(8,128)(2,1)}, u32[]{:S(2)}, u32[]{:S(2)}) collective-permute-start(bf16[256,1024]{1,0:T(8,128)(2,1)} %get-tuple-element.318), channel_id=1, source_target_pairs={{0,4},{4,0},{1,5},{5,1},{2,6},{6,2},{3,7},{7,3},{8,12},{12,8},{9,1... | collective-permute-start | bytes 1572872 | tf_op jit(solution)/shard_map/ppermute | solution.py:45
  483.0 22.0 %collective-permute-start.107 = (bf16[128,1024]{1,0:T(8,128)(2,1)}, bf16[128,1024]{1,0:T(8,128)(2,1)S(1)}, u32[]{:S(2)}, u32[]{:S(2)}) collective-permute-start(bf16[128,1024]{1,0:T(8,128)(2,1)} %reduce-scatter.7.cloned.1.call-done), channel_id=1, source_target_pairs={{0,4},{4,0},{1,5},{5,1},{2,6},{6,2},{3,7},{7,3},{8,12},{12,8},{9,1... | collective-permute-start | bytes 786440 | tf_op jit(solution)/shard_map/ppermute | solution.py:45
  515.6 26.0 %collective-permute-start.115 = (bf16[4,128,1024]{2,1,0:T(8,128)(2,1)}, bf16[4,128,1024]{2,1,0:T(8,128)(2,1)S(1)}, u32[]{:S(2)}, u32[]{:S(2)}) collective-permute-start(bf16[4,128,1024]{2,1,0:T(8,128)(2,1)} %copy-done.126), channel_id=1, source_target_pairs={{0,4},{4,0},{1,5},{5,1},{2,6},{6,2},{3,7},{7,3},{8,12},{12,8},{9,1... | collective-permute-start | bytes 3145736 | tf_op jit(solution)/shard_map/ppermute | solution.py:45
  518.1 31.8 %collective-permute-start.108 = (bf16[256,1024]{1,0:T(8,128)(2,1)}, bf16[256,1024]{1,0:T(8,128)(2,1)}, u32[]{:S(2)}, u32[]{:S(2)}) collective-permute-start(bf16[256,1024]{1,0:T(8,128)(2,1)} %get-tuple-element.346), channel_id=1, source_target_pairs={{0,1},{1,0},{2,3},{3,2},{4,5},{5,4},{6,7},{7,6},{8,9},{9,8},{10,11... | collective-permute-start | bytes 1572872 | tf_op jit(solution)/shard_map/ppermute | solution.py:43
  519.5 30.5 %collective-permute-start.110 = (bf16[256,1024]{1,0:T(8,128)(2,1)}, bf16[256,1024]{1,0:T(8,128)(2,1)}, u32[]{:S(2)}, u32[]{:S(2)}) collective-permute-start(bf16[256,1024]{1,0:T(8,128)(2,1)} %add_low.22), channel_id=1, source_target_pairs={{0,2},{1,3},{2,0},{3,1},{4,6},{5,7},{6,4},{7,5},{8,10},{9,11},{10,... | collective-permute-start | bytes 1572872 | tf_op jit(solution)/shard_map/ppermute | solution.py:43
  544.9 21.0 %collective-permute-start.117 = (bf16[128,1024]{1,0:T(8,128)(2,1)}, bf16[128,1024]{1,0:T(8,128)(2,1)}, u32[]{:S(2)}, u32[]{:S(2)}) collective-permute-start(bf16[128,1024]{1,0:T(8,128)(2,1)} %get-tuple-element.358), channel_id=1, source_target_pairs={{0,16},{8,24},{16,0},{24,8},{1,17},{9,25},{17,1},{25,9},{2,18},{10... | collective-permute-start | bytes 786440 | tf_op jit(solution)/shard_map/ppermute | solution.py:56
  555.1 47.5 %collective-permute-start.114 = (bf16[128,1024]{1,0:T(8,128)(2,1)}, bf16[128,1024]{1,0:T(8,128)(2,1)}, u32[]{:S(2)}, u32[]{:S(2)}) collective-permute-start(bf16[128,1024]{1,0:T(8,128)(2,1)} %get-tuple-element.385), channel_id=1, source_target_pairs={{0,4},{4,0},{1,5},{5,1},{2,6},{6,2},{3,7},{7,3},{8,12},{12,8},{9,1... | collective-permute-start | bytes 786440 | tf_op jit(solution)/shard_map/ppermute | solution.py:45
  556.8 32.7 %collective-permute-start.111 = (bf16[256,1024]{1,0:T(8,128)(2,1)}, bf16[256,1024]{1,0:T(8,128)(2,1)}, u32[]{:S(2)}, u32[]{:S(2)}) collective-permute-start(bf16[256,1024]{1,0:T(8,128)(2,1)} %get-tuple-element.353), channel_id=1, source_target_pairs={{0,2},{1,3},{2,0},{3,1},{4,6},{5,7},{6,4},{7,5},{8,10},{9,11},{10,... | collective-permute-start | bytes 1572872 | tf_op jit(solution)/shard_map/ppermute | solution.py:43
  558.2 31.3 %collective-permute-start.112 = (bf16[256,1024]{1,0:T(8,128)(2,1)S(1)}, bf16[256,1024]{1,0:T(8,128)(2,1)}, u32[]{:S(2)}, u32[]{:S(2)}) collective-permute-start(bf16[256,1024]{1,0:T(8,128)(2,1)S(1)} %get-tuple-element.354), channel_id=1, source_target_pairs={{0,4},{4,0},{1,5},{5,1},{2,6},{6,2},{3,7},{7,3},{8,12},{12,8},{9,1... | collective-permute-start | bytes 1572872 | tf_op jit(solution)/shard_map/ppermute | solution.py:45
  573.5 21.5 %all-to-all-start.2 = ((bf16[4,64,768]{2,1,0:T(8,128)(2,1)}), bf16[4,64,768]{2,1,0:T(8,128)(2,1)S(1)}, u32[]{:S(2)}, u32[]{:S(2)}) async-start(bf16[4,64,768]{2,1,0:T(8,128)(2,1)} %bitcast.58), calls=%async_computation.5 | async-start | bytes 786432 | tf_op jit(solution)/shard_map/all_to_all | solution.py:301
  (333 other events, 2534.1 us)
Sparse Core Ops, SparseCore 0:
  59.2 62.9 all-gather.7
  123.8 44.5 all-gather.5
  170.5 62.2 all-gather.9
  325.6 60.4 reduce-scatter.4
  388.3 27.1 reduce-scatter.6
  424.3 25.7 reduce-scatter.8
  483.1 60.0 reduce-scatter.10
